TPU v7x, 512 devices: a whole 4x4x16 slice. The times are simulated.
512 devices in a mesh: dp: 64 (over z, x), tensor: 8 (over y, core).
Axes of the slice: x: 4, y: 4, z: 16, core: 2. Of those that a mesh axis runs over, the one named last changes fastest.
Arguments:
- x_quant: bfloat16 [12288, 8192], P('dp', 'tensor'), may hold values from -6 to 6
- x_scale: float32 [12288, 64], P('dp', 'tensor'), may hold values from 0.1 to 30
- key_quant: bfloat16 [8192, 1024], P('tensor', 'dp'), may hold values from -0.0625 to 0.0625
- key_scale: float32 [64, 1024], P('tensor', 'dp'), may hold values from 0.1 to 20
- value_quant: bfloat16 [8192, 1024], P('tensor', 'dp'), may hold values from -0.0625 to 0.0625
- value_scale: float32 [64, 1024], P('tensor', 'dp'), may hold values from 0.1 to 20
- grad_key: bfloat16 [12288, 1024], P('dp', 'tensor'), may hold values from -1000 to 1000
- grad_value: bfloat16 [12288, 1024], P('dp', 'tensor'), may hold values from -1000 to 1000
Outputs:
- grad_input: bfloat16 [12288, 8192], P('dp', 'tensor')
- grad_key_weight: bfloat16 [8192, 1024], P('tensor', 'dp')
- grad_value_weight: bfloat16 [8192, 1024], P('tensor', 'dp')
- peaks: float32 [2], replicated
- cotangent_peak: float32 [1], replicated
All inputs are finite; a program needn't handle non-finite values. Where the computation divides by a largest or mean magnitude, that divisor is 1e-20 or more.
Results may differ from a plain program's by a relative error of at most 0.0059.
Values may be sent and summed in bfloat16 or wider, within the bound.
No kernel may reach another device: no remote copies, remote signals or barrier semaphores. Data moves between devices by JAX's collectives and lax.ppermute only.
A program may use at most 64 MiB of HBM per device.

v0:
```python
import jax
import jax.numpy as jnp
from jax import lax
from jax.sharding import PartitionSpec as P

BLOCK = 128


def dequant_rows(quantized, scales):
    row_count, col_count = quantized.shape
    scaled = (
        quantized.astype(jnp.float32).reshape(row_count // BLOCK, BLOCK, col_count)
        * scales[:, None, :]
    )
    return scaled.reshape(row_count, col_count).astype(jnp.bfloat16)


def dequant_cols(quantized, scales):
    row_count, col_count = quantized.shape
    scaled = (
        quantized.astype(jnp.float32).reshape(row_count, col_count // BLOCK, BLOCK)
        * scales[:, :, None]
    )
    return scaled.reshape(row_count, col_count).astype(jnp.bfloat16)


def contract_rows(former, latter):
    return lax.dot_general(
        former, latter, (((0,), (0,)), ((), ())), preferred_element_type=jnp.float32
    )


def contract_cols(former, latter):
    return lax.dot_general(
        former, latter, (((1,), (1,)), ((), ())), preferred_element_type=jnp.float32
    )


def block_quant(partial_value, pieces):
    row_count, col_count = partial_value.shape
    blocks = partial_value.reshape(row_count // BLOCK, BLOCK, pieces, col_count // pieces)
    block_peak = jnp.max(jnp.abs(blocks), axis=(1, 3)) + 1e-06
    quantized = (blocks / block_peak[:, None, :, None]).astype(jnp.bfloat16)
    return (quantized.reshape(row_count, col_count), block_peak)


def restore_sum(arrived, arrived_scales, pieces):
    total_rows, col_count = arrived.shape
    row_count = total_rows // pieces
    blocks = arrived.reshape(pieces, row_count // BLOCK, BLOCK, col_count).astype(jnp.float32)
    blocks = blocks * arrived_scales.reshape(pieces, row_count // BLOCK)[:, :, None, None]
    return jnp.sum(blocks, axis=0).reshape(row_count, col_count)


def input_part(key_grads, value_grads, key_weight, value_weight):
    key_all, value_all = (
        lax.all_gather(key_weight, "dp", axis=1, tiled=True),
        lax.all_gather(value_weight, "dp", axis=1, tiled=True),
    )
    input_sum = contract_cols(key_grads, key_all) + contract_cols(value_grads, value_all)
    local_peak = jnp.max(jnp.abs(input_sum))
    local_peak = lax.pmax(local_peak, ("dp", "tensor"))
    return (input_sum, local_peak)


def weight_part(inputs, key_grads, value_grads):
    pieces = lax.axis_size("dp")
    key_quantized, key_blockpeak = block_quant(contract_rows(inputs, key_grads), pieces)
    value_quantized, value_blockpeak = block_quant(contract_rows(inputs, value_grads), pieces)
    arrived_key, arrived_value = (
        lax.all_to_all(key_quantized, "dp", split_axis=1, concat_axis=0, tiled=True),
        lax.all_to_all(value_quantized, "dp", split_axis=1, concat_axis=0, tiled=True),
    )
    scales_key, scales_value = (
        lax.all_to_all(key_blockpeak, "dp", split_axis=1, concat_axis=0, tiled=True),
        lax.all_to_all(value_blockpeak, "dp", split_axis=1, concat_axis=0, tiled=True),
    )
    return (
        restore_sum(arrived_key, scales_key, pieces),
        restore_sum(arrived_value, scales_value, pieces),
    )


def per_device(
    x_quant, x_scale, key_quant, key_scale, value_quant, value_scale, grad_key, grad_value
):
    inputs = dequant_cols(x_quant, x_scale)
    key_weight = dequant_rows(key_quant, key_scale)
    value_weight = dequant_rows(value_quant, value_scale)
    key_grads, value_grads = (
        lax.all_gather(grad_key, "tensor", axis=1, tiled=True),
        lax.all_gather(grad_value, "tensor", axis=1, tiled=True),
    )
    input_sum, input_peak = input_part(key_grads, value_grads, key_weight, value_weight)
    key_sum, value_sum = weight_part(inputs, key_grads, value_grads)
    key_local = jnp.max(jnp.abs(key_sum))
    value_local = jnp.max(jnp.abs(value_sum))
    key_peak, value_peak = lax.pmax((key_local, value_local), ("dp", "tensor"))
    input_peak = input_peak + 1e-06
    key_peak = key_peak + 1e-06
    value_peak = value_peak + 1e-06
    grad_input = (input_sum / input_peak).astype(jnp.bfloat16)
    grad_key_weight = (key_sum / key_peak).astype(jnp.bfloat16)
    grad_value_weight = (value_sum / value_peak).astype(jnp.bfloat16)
    peaks = jnp.stack([key_peak, value_peak])
    cotangent_peak = jnp.reshape(input_peak, (1,))
    return (grad_input, grad_key_weight, grad_value_weight, peaks, cotangent_peak)


def solution(mesh):
    in_specs = (
        P("dp", "tensor"),
        P("dp", "tensor"),
        P("tensor", "dp"),
        P("tensor", "dp"),
        P("tensor", "dp"),
        P("tensor", "dp"),
        P("dp", "tensor"),
        P("dp", "tensor"),
    )
    out_specs = (P("dp", "tensor"), P("tensor", "dp"), P("tensor", "dp"), P(), P())
    return jax.shard_map(
        per_device, mesh=mesh, in_specs=in_specs, out_specs=out_specs, check_vma=False
    )
```

profile of v0, /device:TPU:1, one launch (start us, length us, event | category | flops | bytes accessed | tf_op | source)
XLA Modules:
  0.0 561.2 jit_solution(17272238604402254088)
XLA Ops:
  7.2 0.8 copy.49
  8.0 0.3 mul.69
  8.3 1.2 fusion.9
  9.5 0.1 copy.67
  9.6 0.1 copy.48
  9.7 19.8 %all_gather.15 = bf16[192,1024]{0,1:T(8,128)(2,1)S(1)} all-gather(bf16[192,128]{0,1:T(8,128)(2,1)S(1)} %copy.48), channel_id=1, replica_groups=mesh['dp'=64,'tensor'=8] {'tensor'}, dimensions={1}, use_global_device_ids=true | all-gather | bytes 442368 | tf_op jit(solution)/shard_map/all_gather | solution.py:92
  29.5 2.7 abs_reduce_fusion
  32.2 0.7 copy.57
  33.0 13.4 %all-to-all-start.3 = ((f32[8,64,1]{0,2,1:T(1,128)}), f32[8,64,1]{0,2,1:T(1,128)S(1)}, u32[]{:S(2)}, u32[]{:S(2)}) async-start(f32[8,64,1]{0,2,1:T(1,128)} %copy.57), calls=%async_computation.3 | async-start | bytes 65536 | tf_op jit(solution)/shard_map/all_to_all | solution.py:76
  46.4 0.1 copy.46
  46.5 13.4 %all_gather.13 = bf16[192,1024]{0,1:T(8,128)(2,1)S(1)} all-gather(bf16[192,128]{0,1:T(8,128)(2,1)S(1)} %copy.46), channel_id=1, replica_groups=mesh['dp'=64,'tensor'=8] {'tensor'}, dimensions={1}, use_global_device_ids=true | all-gather | bytes 442368 | tf_op jit(solution)/shard_map/all_gather | solution.py:91
  59.9 2.7 abs_reduce_fusion.1
  62.6 0.7 copy.53
  63.3 14.8 %all-to-all-start.1 = ((f32[8,64,1]{0,2,1:T(1,128)}), f32[8,64,1]{0,2,1:T(1,128)S(1)}, u32[]{:S(2)}, u32[]{:S(2)}) async-start(f32[8,64,1]{0,2,1:T(1,128)} %copy.53), calls=%async_computation.1 | async-start | bytes 65536 | tf_op jit(solution)/shard_map/all_to_all | solution.py:75
  78.1 2.8 divide_convert_fusion
  81.0 1.4 copy.56
  82.3 2.4 all_to_all.44
  84.7 6.8 %all-to-all-done.1 = f32[8,64,1]{0,2,1:T(1,128)S(1)} async-done(((f32[8,64,1]{0,2,1:T(1,128)}), f32[8,64,1]{0,2,1:T(1,128)S(1)}, u32[]{:S(2)}, u32[]{:S(2)}) %all-to-all-start.1) | async-done | bytes 2080 | tf_op jit(solution)/shard_map/all_to_all | solution.py:75
  91.5 7.9 %all-to-all-start.2 = ((bf16[1024,64,16]{0,2,1:T(8,128)(2,1)}), bf16[1024,64,16]{0,2,1:T(8,128)(2,1)S(1)}, u32[]{:S(2)}, u32[]{:S(2)}) async-start(bf16[1024,64,16]{0,2,1:T(8,128)(2,1)} %all_to_all.44), calls=%async_computation.2 | async-start | bytes 4194304 | tf_op jit(solution)/shard_map/all_to_all | solution.py:72
  99.4 0.0 all-gather.3.cloned.1.call-start
  99.4 0.1 copy.45
  99.5 0.1 mul.63
  99.6 0.6 fusion.14
  100.2 2.8 divide_convert_fusion.1
  103.1 2.7 copy.52
  105.8 4.2 all_to_all.40
  109.9 86.9 %all-to-all-done.2 = bf16[1024,64,16]{0,2,1:T(8,128)(2,1)S(1)} async-done(((bf16[1024,64,16]{0,2,1:T(8,128)(2,1)}), bf16[1024,64,16]{0,2,1:T(8,128)(2,1)S(1)}, u32[]{:S(2)}, u32[]{:S(2)}) %all-to-all-start.2) | async-done | bytes 2097184 | tf_op jit(solution)/shard_map/all_to_all | solution.py:72
  196.8 11.1 %all-to-all-start = ((bf16[1024,64,16]{0,2,1:T(8,128)(2,1)}), bf16[1024,64,16]{0,2,1:T(8,128)(2,1)}, u32[]{:S(2)}, u32[]{:S(2)}) async-start(bf16[1024,64,16]{0,2,1:T(8,128)(2,1)} %all_to_all.40), calls=%async_computation | async-start | bytes 4194304 | tf_op jit(solution)/shard_map/all_to_all | solution.py:71
  207.8 0.0 all-gather.5.cloned.1.call-start
  207.9 0.1 copy.47
  208.0 0.1 mul.66
  208.1 0.6 fusion.13
  208.7 0.1 mul.78
  208.8 0.8 copy.97
  209.6 0.1 mul.73
  209.7 0.8 copy.98
  210.5 78.2 %all-gather.3.cloned.1.call-done = bf16[1024,1024]{0,1:T(8,128)(2,1)} async-done(((bf16[1024,16]{0,1:T(8,128)(2,1)}), bf16[1024,1024]{0,1:T(8,128)(2,1)}) %all-gather.3.cloned.1.call-update) | async-done | bytes 2097168 | tf_op jit(solution)/shard_map/all_gather | solution.py:57
  288.7 2.3 fusion.17
  291.0 140.9 %all-gather.5.cloned.1.call-done = bf16[1024,1024]{0,1:T(8,128)(2,1)} async-done(((bf16[1024,16]{0,1:T(8,128)(2,1)}), bf16[1024,1024]{0,1:T(8,128)(2,1)}) %all-gather.5.cloned.1.call-update) | async-done | bytes 2097168 | tf_op jit(solution)/shard_map/all_gather | solution.py:58
  431.9 3.7 abs_reduce_fusion.2
  435.7 0.6 fusion
  436.3 0.6 abs_reduce_fusion.3
  436.9 2.1 fusion.1
  439.0 0.6 abs_reduce_fusion.4
  439.6 109.6 %all-reduce = (f32[]{:T(128)}, f32[]{:T(128)}, f32[]{:T(128)}) all-reduce(f32[]{:T(128)} %get-tuple-element.12, f32[]{:T(128)} %abs_reduce_fusion.4, f32[]{:T(128)} %abs_reduce_fusion.3), channel_id=1, replica_groups=mesh['dp'=64,'tensor'=8] {'dp','tensor'}, use_global_device_ids=true, to_apply=%region_1.0 | all-reduce | flops 3 | bytes 24 | tf_op jit(solution)/shard_map/pmax | solution.py:62
  551.2 0.6 divide_convert_fusion.3
  551.8 0.6 pad_maximum_fusion
  552.4 0.8 fusion.10
  (26 shorter events, 0.1 us)
Async XLA Ops:
  7.2 2.4 copy-start.4
  29.5 16.9 %copy-start.5 = (bf16[192,128]{1,0:T(8,128)(2,1)S(1)}, bf16[192,128]{1,0:T(8,128)(2,1)}, u32[]{:S(2)}) copy-start(bf16[192,128]{1,0:T(8,128)(2,1)} %param.14) | copy-start | bytes 147460
  33.0 30.3 %all-to-all-start.3 = ((f32[8,64,1]{0,2,1:T(1,128)}), f32[8,64,1]{0,2,1:T(1,128)S(1)}, u32[]{:S(2)}, u32[]{:S(2)}) async-start(f32[8,64,1]{0,2,1:T(1,128)} %copy.57), calls=%async_computation.3 | async-start | bytes 65536 | tf_op jit(solution)/shard_map/all_to_all | solution.py:76
  59.9 2.7 copy-start.1
  63.3 28.2 %all-to-all-start.1 = ((f32[8,64,1]{0,2,1:T(1,128)}), f32[8,64,1]{0,2,1:T(1,128)S(1)}, u32[]{:S(2)}, u32[]{:S(2)}) async-start(f32[8,64,1]{0,2,1:T(1,128)} %copy.53), calls=%async_computation.1 | async-start | bytes 65536 | tf_op jit(solution)/shard_map/all_to_all | solution.py:75
  84.7 14.7 %copy-start.8 = (f32[8,16]{1,0:T(8,128)S(1)}, f32[8,16]{1,0:T(8,128)}, u32[]{:S(2)}) copy-start(f32[8,16]{1,0:T(8,128)} %param.11) | copy-start | bytes 1540
  84.7 14.9 %copy-start.6 = (bf16[1024,16]{0,1:T(8,128)(2,1)S(1)}, bf16[1024,16]{0,1:T(8,128)(2,1)}, u32[]{:S(2)}) copy-start(bf16[1024,16]{0,1:T(8,128)(2,1)} %param.10) | copy-start | bytes 98308
  91.5 105.3 %all-to-all-start.2 = ((bf16[1024,64,16]{0,2,1:T(8,128)(2,1)}), bf16[1024,64,16]{0,2,1:T(8,128)(2,1)S(1)}, u32[]{:S(2)}, u32[]{:S(2)}) async-start(bf16[1024,64,16]{0,2,1:T(8,128)(2,1)} %all_to_all.44), calls=%async_computation.2 | async-start | bytes 4194304 | tf_op jit(solution)/shard_map/all_to_all | solution.py:72
  99.4 189.3 %all-gather.3.cloned.1.call-start = ((), (), s32[]{:S(2)}) async-start(), calls=%async_computation.4 | async-start | bytes 2129920 | tf_op jit(solution)/shard_map/all_gather | solution.py:57
  109.9 98.0 %copy-start.9 = (f32[8,16]{1,0:T(8,128)S(1)}, f32[8,16]{1,0:T(8,128)}, u32[]{:S(2)}) copy-start(f32[8,16]{1,0:T(8,128)} %param.13) | copy-start | bytes 1540
  109.9 98.1 %copy-start.7 = (bf16[1024,16]{0,1:T(8,128)(2,1)S(1)}, bf16[1024,16]{0,1:T(8,128)(2,1)}, u32[]{:S(2)}) copy-start(bf16[1024,16]{0,1:T(8,128)(2,1)} %param.12) | copy-start | bytes 98308
  196.8 240.1 %all-to-all-start = ((bf16[1024,64,16]{0,2,1:T(8,128)(2,1)}), bf16[1024,64,16]{0,2,1:T(8,128)(2,1)}, u32[]{:S(2)}, u32[]{:S(2)}) async-start(bf16[1024,64,16]{0,2,1:T(8,128)(2,1)} %all_to_all.40), calls=%async_computation | async-start | bytes 4194304 | tf_op jit(solution)/shard_map/all_to_all | solution.py:71
  207.8 224.1 %all-gather.5.cloned.1.call-start = ((), (), s32[]{:S(2)}) async-start(), calls=%async_computation.5 | async-start | bytes 2129920 | tf_op jit(solution)/shard_map/all_gather | solution.py:58
  431.9 3.8 copy-start.3
  435.7 1.3 copy-start.2
  435.7 116.7 %copy-start = (f32[1024,192]{0,1:T(8,128)S(1)}, f32[1024,192]{0,1:T(8,128)}, u32[]{:S(2)}) copy-start(f32[1024,192]{0,1:T(8,128)} %get-tuple-element.13) | copy-start | bytes 2359300
Sparse Core Ops, SparseCore 0:
  103.7 184.9 all-gather.2
  292.2 139.6 all-gather.4
where the time goes:
time: 562 us; the launch traced here: 561 us
  waiting for transfers between devices  313 us (56%)
  blocking collectives  143 us (25%)
  starting transfers between devices  47.2 us (8%)
  between operations  17.3 us (3%)
  local copies, waits for them, and re-layouts  15.4 us (3%)
  other arithmetic  14.1 us (3%)
  matrix products  11.5 us (2%)
    all_gather x1, waiting for transfers between devices, input_part(): lax.all_gather(value_weight, 'dp', axis=1, tiled=True)  141 us
    pmax x1, blocking collectives, input_part(): local_peak = lax.pmax(local_peak, ('dp', 'tensor'))  110 us
    all_to_all x1, waiting for transfers between devices, weight_part(): lax.all_to_all(value_quantized, 'dp', split_axis=1, concat_axis=0, tiled=...  86.9 us
    all_gather x1, waiting for transfers between devices, input_part(): lax.all_gather(key_weight, 'dp', axis=1, tiled=True)  78.2 us
    all_gather x1, blocking collectives, per_device(): lax.all_gather(grad_value, 'tensor', axis=1, tiled=True)  19.8 us
    all_to_all x1, starting transfers between devices, weight_part(): lax.all_to_all(key_blockpeak, 'dp', split_axis=1, concat_axis=0, tiled=True)  14.8 us
    all_to_all x1, starting transfers between devices, weight_part(): lax.all_to_all(value_blockpeak, 'dp', split_axis=1, concat_axis=0, tiled=...  13.4 us
    all_gather x1, blocking collectives, per_device(): lax.all_gather(grad_key, 'tensor', axis=1, tiled=True)  13.4 us
  transfers between devices with their start and end apart: 6, of which 4 were waited for; matrix products, arithmetic and copies ran while one was open for 4% of the time, Pallas kernels for 0%

commit v1 on v0

v1 whole, which is shorter than its diff:
```python
import jax
import jax.numpy as jnp
from jax import lax
from jax.sharding import Mesh, PartitionSpec as P

BLOCK = 128
DP = ("zh", "zl", "x")
TENSOR = ("y", "c")
F32, BF16 = jnp.float32, jnp.bfloat16


def spread(block, axes):
    count = lax.axis_size(axes)
    copies = jnp.broadcast_to(block[None], (count, *block.shape))
    return lax.all_to_all(copies, axes, 0, 0, tiled=True)


def per_device(
    x_quant, x_scale, key_quant, key_scale, value_quant, value_scale, grad_key, grad_value
):
    tokens, features = x_quant.shape
    cols = key_quant.shape[1]
    nx = lax.axis_size("x")
    nzh, nzl = lax.axis_size("zh"), lax.axis_size("zl")

    grads = jnp.stack([grad_key.T, grad_value.T])
    grads = grads.reshape(2, 2, nx, cols, tokens).transpose(2, 1, 0, 3, 4)
    grads = grads.reshape(nx, 1, 4 * cols, tokens)
    grads = jnp.broadcast_to(grads, (nx, lax.axis_size(TENSOR), 4 * cols, tokens))
    grads = lax.all_to_all(
        grads.reshape(-1, 4 * cols, tokens), ("x", *TENSOR), 0, 0, tiled=True
    )
    grads = grads.reshape(nx, nzh, 2, 2, 2 * cols, tokens)
    grads = grads.transpose(0, 2, 3, 1, 4, 5).reshape(nx, nzl * nzh * 2 * cols, tokens)

    inputs = x_quant.astype(F32).reshape(tokens, features // BLOCK, BLOCK)
    inputs = (inputs * x_scale[:, :, None]).astype(BF16).reshape(tokens, features)
    inputs = spread(inputs, "x")

    weight = jnp.stack([key_quant.T, value_quant.T]).astype(F32)
    scale = jnp.stack([key_scale.T, value_scale.T])
    weight = weight.reshape(2, cols, features // BLOCK, BLOCK) * scale[..., None]
    weight = weight.astype(BF16).reshape(2 * cols, features)
    weight = spread(weight, "zh").reshape(nzh * 2 * cols, features)
    weight = spread(weight, "zl").reshape(nzl * nzh * 2 * cols, features)

    part = jnp.einsum("xct,xtd->cd", grads, inputs, preferred_element_type=F32)
    part = part.astype(BF16).reshape(nzl, nzh * 2 * cols, features)
    part = lax.all_to_all(part, "zl", 0, 0, tiled=True)
    part = jnp.sum(part.astype(F32), axis=0).astype(BF16)
    part = part.reshape(nzh, 2 * cols, features)
    part = lax.all_to_all(part, "zh", 0, 0, tiled=True)
    weight_sum = jnp.sum(part.astype(F32), axis=0).reshape(2, cols, features)
    weight_peak = jnp.max(jnp.abs(weight_sum), axis=(1, 2))

    part = jnp.einsum("xct,cd->xtd", grads, weight, preferred_element_type=F32)
    part = lax.all_to_all(part.astype(BF16), "x", 0, 0, tiled=True)
    input_sum = jnp.sum(part.astype(F32), axis=0)
    input_peak = jnp.max(jnp.abs(input_sum))

    peaks = jnp.concatenate([weight_peak, input_peak[None]])
    peaks = jnp.pad(peaks, (0, 125))
    peaks = jnp.max(spread(peaks, DP), axis=0)
    peaks = jnp.max(spread(peaks, TENSOR), axis=0) + 1e-06
    grad_weight = (weight_sum / peaks[:2, None, None]).astype(BF16)
    grad_input = (input_sum / peaks[2]).astype(BF16)
    return (grad_input, grad_weight[0].T, grad_weight[1].T, peaks[:2], peaks[2:3])


def solution(mesh):
    whole = Mesh(mesh.devices.reshape(4, 4, 4, 4, 2), (*DP, *TENSOR))
    in_specs = (
        P(DP, TENSOR),
        P(DP, TENSOR),
        P(TENSOR, DP),
        P(TENSOR, DP),
        P(TENSOR, DP),
        P(TENSOR, DP),
        P(DP, TENSOR),
        P(DP, TENSOR),
    )
    out_specs = (P(DP, TENSOR), P(TENSOR, DP), P(TENSOR, DP), P(), P())
    return jax.shard_map(
        per_device, mesh=whole, in_specs=in_specs, out_specs=out_specs, check_vma=False
    )
```

time: 562 us -> 227 us (0.40)
  waiting for transfers between devices: 313 us -> 103 us
  blocking collectives: 143 us -> 66.7 us
  between operations: 17.3 us -> 0.86 us
  other arithmetic: 14.1 us -> 4.81 us
  starting transfers between devices: 47.2 us -> 38.2 us
  matrix products: 11.5 us -> 4.22 us
  local copies, waits for them, and re-layouts: 15.4 us -> 9.06 us
    all_gather x2 -> x0, waiting for transfers between devices: 219 us -> none  [the longest x1 141 us: input_part(): lax.all_gather(value_weight, 'dp', axis=1, tiled=True)]
    pmax x1 -> x0, blocking collectives: 110 us -> none  [input_part(): local_peak = lax.pmax(local_peak, ('dp', 'tensor'))]
    all_to_all x0 -> x3, blocking collectives: none -> 66.7 us  [the longest x1 33.4 us: per_device(): part = lax.all_to_all(part, 'zl', 0, 0, tiled=True)]
    all_gather x2 -> x0, blocking collectives: 33.2 us -> none  [the longest x1 19.8 us: per_device(): lax.all_gather(grad_value, 'tensor', axis=1, tiled=True)]
    all_to_all x4 -> x6, starting transfers between devices: 47.1 us -> 38.2 us  [the longest x3 20.2 us: spread(): return lax.all_to_all(copies, axes, 0, 0, tiled=True)]
    all_to_all x4 -> x6, waiting for transfers between devices: 93.7 us -> 103 us  [the longest x3 54.7 us: spread(): return lax.all_to_all(copies, axes, 0, 0, tiled=True)]
    dot_general x4 -> x2, matrix products: 11.5 us -> 4.22 us  [the longest x1 2.16 us: per_device(): part = jnp.einsum('xct,cd->xtd', grads, weight, preferred_element_type=F32)]
    convert_element_type x6 -> x4, other arithmetic: 8.41 us -> 1.87 us  [the longest x1 1.46 us: per_device(): grad_input = (input_sum / peaks[2]).astype(BF16)]
  transfers between devices with their start and end apart: 6 -> 6, of which waited for: 4 -> 6; matrix products, arithmetic and copies ran while one was open for 4% -> 3% of each run, Pallas kernels for 0% -> 0%
where the time goes in v1:
time: 227 us; the launch traced here: 226 us
  waiting for transfers between devices  103 us (45%)
  blocking collectives  66.7 us (29%)
  starting transfers between devices  38.2 us (17%)
  local copies, waits for them, and re-layouts  9.06 us (4%)
  other arithmetic  4.81 us (2%)
  matrix products  4.22 us (2%)
    all_to_all x3, waiting for transfers between devices, spread(): return lax.all_to_all(copies, axes, 0, 0, tiled=True)  54.7 us
    all_to_all x1, blocking collectives, per_device(): part = lax.all_to_all(part, 'zl', 0, 0, tiled=True)  33.4 us
    all_to_all x2, blocking collectives, spread(): return lax.all_to_all(copies, axes, 0, 0, tiled=True)  33.4 us
    all_to_all x3, starting transfers between devices, spread(): return lax.all_to_all(copies, axes, 0, 0, tiled=True)  20.2 us
    all_to_all x1, waiting for transfers between devices, per_device(): part = lax.all_to_all(part.astype(BF16), 'x', 0, 0, tiled=True)  17.4 us
    all_to_all x1, waiting for transfers between devices, per_device(): lax.all_to_all(grads.reshape(-1, 4 * cols, tokens), ('x', *TENSOR), 0, 0,...  16.4 us
    all_to_all x1, waiting for transfers between devices, per_device(): part = lax.all_to_all(part, 'zh', 0, 0, tiled=True)  14.1 us
    all_to_all x1, starting transfers between devices, per_device(): lax.all_to_all(grads.reshape(-1, 4 * cols, tokens), ('x', *TENSOR), 0, 0,...  10.6 us
  transfers between devices with their start and end apart: 6, of which 6 were waited for; matrix products, arithmetic and copies ran while one was open for 3% of the time, Pallas kernels for 0%

profile of v1, /device:TPU:1, one launch (start us, length us, event | category | flops | bytes accessed | tf_op | source)
XLA Modules:
  0.0 226.3 jit_solution(4847479191202871831)
XLA Ops:
  0.6 0.9 copy.31
  1.5 0.9 copy.32
  2.5 0.0 copy-start.5
  2.5 1.1 broadcast_in_dim.19
  3.6 10.6 %all-to-all-start = ((bf16[32,64,192]{2,1,0:T(8,128)(2,1)}), bf16[32,64,192]{2,1,0:T(8,128)(2,1)S(1)}, u32[]{:S(2)}, u32[]{:S(2)}) async-start(bf16[32,64,192]{2,1,0:T(8,128)(2,1)} %bitcast.6), calls=%async_computation | async-start | bytes 2097152 | tf_op jit(solution)/shard_map/all_to_all | solution.py:30
  14.2 0.0 copy-done.5
  14.2 0.1 copy.37
  14.3 0.3 mul.27
  14.6 0.0 copy-done.2
  14.6 0.2 fusion
  14.9 16.4 %all-to-all-done = bf16[32,64,192]{2,1,0:T(8,128)(2,1)S(1)} async-done(((bf16[32,64,192]{2,1,0:T(8,128)(2,1)}), bf16[32,64,192]{2,1,0:T(8,128)(2,1)S(1)}, u32[]{:S(2)}, u32[]{:S(2)}) %all-to-all-start) | async-done | bytes 786464 | tf_op jit(solution)/shard_map/all_to_all | solution.py:30
  31.2 1.4 broadcast_in_dim.23
  32.6 3.7 %all-to-all-start.4 = ((bf16[4,192,1024]{2,1,0:T(8,128)(2,1)}), bf16[4,192,1024]{2,1,0:T(8,128)(2,1)S(1)}, u32[]{:S(2)}, u32[]{:S(2)}) async-start(bf16[4,192,1024]{2,1,0:T(8,128)(2,1)} %broadcast_in_dim.23), calls=%async_computation.4 | async-start | bytes 3145728 | tf_op jit(solution)/shard_map/all_to_all | solution.py:15
  36.3 0.0 copy-done.3
  36.3 0.0 copy-done.4
  36.3 0.0 copy-done.6
  36.4 0.0 copy-done.7
  36.4 0.1 copy.35
  36.4 0.1 multiply_convert_fusion
  36.6 20.4 %all-to-all-done.4 = bf16[4,192,1024]{2,1,0:T(8,128)(2,1)S(1)} async-done(((bf16[4,192,1024]{2,1,0:T(8,128)(2,1)}), bf16[4,192,1024]{2,1,0:T(8,128)(2,1)S(1)}, u32[]{:S(2)}, u32[]{:S(2)}) %all-to-all-start.4) | async-done | bytes 1572896 | tf_op jit(solution)/shard_map/all_to_all | solution.py:15
  57.0 0.7 broadcast_in_dim.20
  57.7 12.9 %all-to-all-start.1 = ((bf16[4,32,1024]{2,1,0:T(8,128)(2,1)}), bf16[4,32,1024]{2,1,0:T(8,128)(2,1)S(1)}, u32[]{:S(2)}, u32[]{:S(2)}) async-start(bf16[4,32,1024]{2,1,0:T(8,128)(2,1)} %broadcast_in_dim.20), calls=%async_computation.1 | async-start | bytes 524288 | tf_op jit(solution)/shard_map/all_to_all | solution.py:15
  70.5 0.1 copy.34
  70.7 1.0 copy-done
  71.6 2.1 bitcast_convert_fusion
  73.7 10.1 %all-to-all-done.1 = bf16[4,32,1024]{2,1,0:T(8,128)(2,1)S(1)} async-done(((bf16[4,32,1024]{2,1,0:T(8,128)(2,1)}), bf16[4,32,1024]{2,1,0:T(8,128)(2,1)S(1)}, u32[]{:S(2)}, u32[]{:S(2)}) %all-to-all-start.1) | async-done | bytes 262176 | tf_op jit(solution)/shard_map/all_to_all | solution.py:15
  83.8 33.4 %all_to_all.47 = bf16[4,128,1024]{2,1,0:T(8,128)(2,1)S(1)} all-to-all(bf16[4,128,1024]{2,1,0:T(8,128)(2,1)} %bitcast.71), channel_id=1, replica_groups=mesh['zh'=4,'zl'=4,'x'=4,'y'=4,'c'=2] {'zl'}, dimensions={0} | all-to-all | bytes 2097152 | tf_op jit(solution)/shard_map/all_to_all | solution.py:49
  117.1 1.2 broadcast_in_dim.22
  118.3 3.6 %all-to-all-start.2 = ((bf16[4,128,1024]{2,1,0:T(8,128)(2,1)}), bf16[4,128,1024]{2,1,0:T(8,128)(2,1)S(1)}, u32[]{:S(2)}, u32[]{:S(2)}) async-start(bf16[4,128,1024]{2,1,0:T(8,128)(2,1)} %broadcast_in_dim.22), calls=%async_computation.2 | async-start | bytes 2097152 | tf_op jit(solution)/shard_map/all_to_all | solution.py:15
  122.0 0.9 reduce_sum.31
  122.9 24.2 %all-to-all-done.2 = bf16[4,128,1024]{2,1,0:T(8,128)(2,1)S(1)} async-done(((bf16[4,128,1024]{2,1,0:T(8,128)(2,1)}), bf16[4,128,1024]{2,1,0:T(8,128)(2,1)S(1)}, u32[]{:S(2)}, u32[]{:S(2)}) %all-to-all-start.2) | async-done | bytes 1048608 | tf_op jit(solution)/shard_map/all_to_all | solution.py:15
  147.1 3.8 %all-to-all-start.6 = ((bf16[4,32,1024]{2,1,0:T(8,128)(2,1)}), bf16[4,32,1024]{2,1,0:T(8,128)(2,1)S(1)}, u32[]{:S(2)}, u32[]{:S(2)}) async-start(bf16[4,32,1024]{2,1,0:T(8,128)(2,1)} %bitcast.21), calls=%async_computation.6 | async-start | bytes 524288 | tf_op jit(solution)/shard_map/all_to_all | solution.py:52
  150.9 2.2 convolution_convert_fusion
  153.1 14.1 %all-to-all-done.6 = bf16[4,32,1024]{2,1,0:T(8,128)(2,1)S(1)} async-done(((bf16[4,32,1024]{2,1,0:T(8,128)(2,1)}), bf16[4,32,1024]{2,1,0:T(8,128)(2,1)S(1)}, u32[]{:S(2)}, u32[]{:S(2)}) %all-to-all-start.6) | async-done | bytes 262176 | tf_op jit(solution)/shard_map/all_to_all | solution.py:52
  167.2 3.6 %all-to-all-start.3 = ((bf16[4,192,1024]{2,1,0:T(8,128)(2,1)}), bf16[4,192,1024]{2,1,0:T(8,128)(2,1)S(1)}, u32[]{:S(2)}, u32[]{:S(2)}) async-start(bf16[4,192,1024]{2,1,0:T(8,128)(2,1)} %convolution_convert_fusion), calls=%async_computation.3 | async-start | bytes 3145728 | tf_op jit(solution)/shard_map/all_to_all | solution.py:57
  170.8 0.1 abs_reduce_fusion.1
  170.9 0.1 reduce_max.44
  171.0 0.1 reduce_max.45
  171.1 17.4 %all-to-all-done.3 = bf16[4,192,1024]{2,1,0:T(8,128)(2,1)S(1)} async-done(((bf16[4,192,1024]{2,1,0:T(8,128)(2,1)}), bf16[4,192,1024]{2,1,0:T(8,128)(2,1)S(1)}, u32[]{:S(2)}, u32[]{:S(2)}) %all-to-all-start.3) | async-done | bytes 1572896 | tf_op jit(solution)/shard_map/all_to_all | solution.py:57
  188.5 0.3 convert_reduce_fusion
  188.8 0.7 abs_reduce_fusion
  189.4 0.7 fusion.1
  190.2 22.2 %all_to_all.48 = f32[64,1,128]{2,1,0:T(1,128)S(1)} all-to-all(f32[64,1,128]{2,1,0:T(1,128)S(1)} %broadcast_in_dim.49), channel_id=1, replica_groups=mesh['zh'=4,'zl'=4,'x'=4,'y'=4,'c'=2] {'zh','zl','x'}, dimensions={0} | all-to-all | bytes 65536 | tf_op jit(solution)/shard_map/all_to_all | solution.py:15
  212.4 11.2 %all_to_all.49 = f32[8,1,128]{2,1,0:T(1,128)S(1)} all-to-all(f32[8,1,128]{2,1,0:T(1,128)S(1)} %broadcast_in_dim.50), channel_id=1, replica_groups=mesh['zh'=4,'zl'=4,'x'=4,'y'=4,'c'=2] {'y','c'}, dimensions={0} | all-to-all | bytes 8192 | tf_op jit(solution)/shard_map/all_to_all | solution.py:15
  223.6 0.6 slice.14
  224.2 0.1 divide_convert_fusion.1
  224.2 0.6 slice_bitcast_fusion
  224.9 1.5 divide_convert_fusion
  (22 shorter events, 0.2 us)
Async XLA Ops:
  2.5 11.7 %copy-start.5 = (f32[192,8]{0,1:T(8,128)S(1)}, f32[192,8]{0,1:T(8,128)}, u32[]{:S(2)}) copy-start(f32[192,8]{0,1:T(8,128)} %param.9) | copy-start | bytes 18436
  3.6 11.0 %copy-start.2 = (bf16[192,1024]{1,0:T(8,128)(2,1)S(1)}, bf16[192,1024]{1,0:T(8,128)(2,1)}, u32[]{:S(2)}) copy-start(bf16[192,1024]{1,0:T(8,128)(2,1)} %param.8) | copy-start | bytes 1179652
  3.6 27.6 %all-to-all-start = ((bf16[32,64,192]{2,1,0:T(8,128)(2,1)}), bf16[32,64,192]{2,1,0:T(8,128)(2,1)S(1)}, u32[]{:S(2)}, u32[]{:S(2)}) async-start(bf16[32,64,192]{2,1,0:T(8,128)(2,1)} %bitcast.6), calls=%async_computation | async-start | bytes 2097152 | tf_op jit(solution)/shard_map/all_to_all | solution.py:30
  32.6 3.7 %copy-start.3 = (bf16[1024,16]{0,1:T(8,128)(2,1)S(1)}, bf16[1024,16]{0,1:T(8,128)(2,1)}, u32[]{:S(2)}) copy-start(bf16[1024,16]{0,1:T(8,128)(2,1)} %param.10) | copy-start | bytes 98308
  32.6 3.7 %copy-start.4 = (bf16[1024,16]{0,1:T(8,128)(2,1)S(1)}, bf16[1024,16]{0,1:T(8,128)(2,1)}, u32[]{:S(2)}) copy-start(bf16[1024,16]{0,1:T(8,128)(2,1)} %param.12) | copy-start | bytes 98308
  32.6 3.8 %copy-start.6 = (f32[8,16]{1,0:T(8,128)S(1)}, f32[8,16]{1,0:T(8,128)}, u32[]{:S(2)}) copy-start(f32[8,16]{1,0:T(8,128)} %param.13) | copy-start | bytes 1540
  32.6 3.8 %copy-start.7 = (f32[8,16]{1,0:T(8,128)S(1)}, f32[8,16]{1,0:T(8,128)}, u32[]{:S(2)}) copy-start(f32[8,16]{1,0:T(8,128)} %param.11) | copy-start | bytes 1540
  32.6 24.4 %all-to-all-start.4 = ((bf16[4,192,1024]{2,1,0:T(8,128)(2,1)}), bf16[4,192,1024]{2,1,0:T(8,128)(2,1)S(1)}, u32[]{:S(2)}, u32[]{:S(2)}) async-start(bf16[4,192,1024]{2,1,0:T(8,128)(2,1)} %broadcast_in_dim.23), calls=%async_computation.4 | async-start | bytes 3145728 | tf_op jit(solution)/shard_map/all_to_all | solution.py:15
  57.7 26.1 %all-to-all-start.1 = ((bf16[4,32,1024]{2,1,0:T(8,128)(2,1)}), bf16[4,32,1024]{2,1,0:T(8,128)(2,1)S(1)}, u32[]{:S(2)}, u32[]{:S(2)}) async-start(bf16[4,32,1024]{2,1,0:T(8,128)(2,1)} %broadcast_in_dim.20), calls=%async_computation.1 | async-start | bytes 524288 | tf_op jit(solution)/shard_map/all_to_all | solution.py:15
  70.6 1.0 copy-start
  118.3 32.6 %copy-start.1 = (bf16[4,2,2,4,32,192]{5,4,3,2,1,0:T(8,128)(2,1)S(1)}, bf16[4,2,2,4,32,192]{5,4,3,2,1,0:T(8,128)(2,1)}, u32[]{:S(2)}) copy-start(bf16[4,2,2,4,32,192]{5,4,3,2,1,0:T(8,128)(2,1)} %copy-done) | copy-start | bytes 2359300
  118.3 28.8 %all-to-all-start.2 = ((bf16[4,128,1024]{2,1,0:T(8,128)(2,1)}), bf16[4,128,1024]{2,1,0:T(8,128)(2,1)S(1)}, u32[]{:S(2)}, u32[]{:S(2)}) async-start(bf16[4,128,1024]{2,1,0:T(8,128)(2,1)} %broadcast_in_dim.22), calls=%async_computation.2 | async-start | bytes 2097152 | tf_op jit(solution)/shard_map/all_to_all | solution.py:15
  147.1 20.1 %all-to-all-start.6 = ((bf16[4,32,1024]{2,1,0:T(8,128)(2,1)}), bf16[4,32,1024]{2,1,0:T(8,128)(2,1)S(1)}, u32[]{:S(2)}, u32[]{:S(2)}) async-start(bf16[4,32,1024]{2,1,0:T(8,128)(2,1)} %bitcast.21), calls=%async_computation.6 | async-start | bytes 524288 | tf_op jit(solution)/shard_map/all_to_all | solution.py:52
  167.2 21.3 %all-to-all-start.3 = ((bf16[4,192,1024]{2,1,0:T(8,128)(2,1)}), bf16[4,192,1024]{2,1,0:T(8,128)(2,1)S(1)}, u32[]{:S(2)}, u32[]{:S(2)}) async-start(bf16[4,192,1024]{2,1,0:T(8,128)(2,1)} %convolution_convert_fusion), calls=%async_computation.3 | async-start | bytes 3145728 | tf_op jit(solution)/shard_map/all_to_all | solution.py:57
  223.6 2.8 %copy-start.8 = (f32[128]{0:T(128)}, f32[128]{0:T(128)S(1)}, u32[]{:S(2)}) copy-start(f32[128]{0:T(128)S(1)} %broadcast_add_fusion) | copy-start | bytes 1540

commit v2 on v1

v2 whole, which is shorter than its diff:
```python
import jax
import jax.numpy as jnp
from jax import lax
from jax.experimental import pallas as pl
from jax.experimental.pallas import tpu as pltpu
from jax.sharding import Mesh, PartitionSpec as P

BLOCK = 128
DP = ("zh", "zl", "x")
TENSOR = ("y", "c")
RING = ("zh", "zl")
F32, BF16 = jnp.float32, jnp.bfloat16
VMEM = pl.BlockSpec(memory_space=pltpu.VMEM)
SMEM = pl.BlockSpec(memory_space=pltpu.SMEM)


def kernel_call(body, out_shape, in_specs, out_specs=None, scratch=(), flops=0):
    if out_specs is None:
        out_specs = jax.tree.map(lambda _: VMEM, out_shape)
    return pl.pallas_call(
        body,
        out_shape=out_shape,
        in_specs=in_specs,
        out_specs=out_specs,
        scratch_shapes=list(scratch),
        cost_estimate=pl.CostEstimate(flops=flops, bytes_accessed=0, transcendentals=0),
        compiler_params=pltpu.CompilerParams(vmem_limit_bytes=40 * 2**20),
    )


def shape(dims, dtype):
    return jax.ShapeDtypeStruct(dims, dtype)


def shift(value, axes, by):
    count = lax.axis_size(axes)
    return lax.ppermute(value, axes, [(i, (i + by) % count) for i in range(count)])


def spread(block, axes):
    count = lax.axis_size(axes)
    copies = jnp.broadcast_to(block[None], (count, *block.shape))
    return lax.all_to_all(copies, axes, 0, 0, tiled=True)


def grads_body(key_ref, value_ref, out_ref):
    key, value = key_ref[...].T, value_ref[...].T
    for x in range(4):
        rows = []
        for zz in range(2):
            start = zz * 64 + x * 16
            rows += [key[start : start + 16], value[start : start + 16]]
        block = jnp.concatenate(rows, axis=0)
        for copy in range(4):
            out_ref[x, copy] = block


def scale_body(x_ref, x_scale_ref, key_ref, key_scale_ref, value_ref, value_scale_ref, out_ref, weight_ref):
    for b in range(8):
        at = slice(b * BLOCK, (b + 1) * BLOCK)
        out_ref[:, at] = (x_ref[:, at].astype(F32) * x_scale_ref[:, b : b + 1]).astype(BF16)
        for part, ref, scale in ((0, key_ref, key_scale_ref), (1, value_ref, value_scale_ref)):
            weight_ref[part * 16 : (part + 1) * 16, at] = (
                ref[:, at].astype(F32) * scale[:, b : b + 1]
            ).astype(BF16)


def weight_body(place, own_ref, twin_ref, x0, x1, x2, x3, keep_ref, out1, out2a, out2b, out3, total):
    x, zl, core = place[0], place[1], place[2]
    for i, part in enumerate((own_ref, twin_ref)):
        value = None
        for ref, back in ((x0, 0), (x1, 1), (x2, 2), (x3, 3)):
            lhs = part[lax.rem(x + 4 - back, 4)]
            term = jnp.dot(lhs, ref[...], preferred_element_type=F32)
            value = term if value is None else value + term
        total[i] = value.reshape(4, 2, 32, 1024)
    for k, out in enumerate((keep_ref, out1, None, out3)):
        group = lax.rem(zl + k, 4)
        half, zz = lax.rem(group // 2 + core, 2), lax.rem(group, 2)
        for y in range(4):
            block = total[half, y, zz]
            if k == 2:
                target = (out2a, out2b)[y // 2]
                target[(y % 2) * 32 : (y % 2 + 1) * 32] = block.astype(BF16)
            else:
                out[y * 32 : (y + 1) * 32] = block.astype(out.dtype)


def input_body(place, own_ref, twin_ref, w0, w1, w2, w3, keep_ref, out1, out2, out3, weight):
    x, zl, core = place[0], place[1], place[2]
    for back, ref in enumerate((w0, w1, w2, w3)):
        group = lax.rem(zl + 4 - back, 4)
        half, zz = lax.rem(group // 2 + core, 2), lax.rem(group, 2)
        for y in range(4):
            weight[half, y, zz] = ref[y * 32 : (y + 1) * 32]
    for k, out in enumerate((keep_ref, out1, out2, out3)):
        member = lax.rem(x + k, 4)
        value = jnp.dot(
            own_ref[member].T, weight[0].reshape(256, 1024), preferred_element_type=F32
        ) + jnp.dot(
            twin_ref[member].T, weight[1].reshape(256, 1024), preferred_element_type=F32
        )
        out[...] = value.astype(out.dtype)


def near_body(keep_ref, r1, r2a, r2b, r3, out_ref):
    for i, r2 in enumerate((r2a, r2b)):
        at = slice(i * 64, (i + 1) * 64)
        total = keep_ref[at] + r1[at].astype(F32) + r2[...].astype(F32) + r3[at].astype(F32)
        out_ref[i * 2 : (i + 1) * 2] = total.astype(BF16).reshape(2, 32, 1024)


def peak_body(far_ref, keep_ref, r1, r2, r3, weight_ref, input_ref, peak_ref):
    weight = far_ref[0].astype(F32)
    for i in range(1, 4):
        weight = weight + far_ref[i].astype(F32)
    weight_ref[...] = weight
    total = keep_ref[...] + r1[...].astype(F32) + r2[...].astype(F32) + r3[...].astype(F32)
    input_ref[...] = total
    size = jnp.abs(weight)
    lane = lax.broadcasted_iota(jnp.int32, peak_ref.shape, 1)
    peak_ref[...] = jnp.where(
        lane == 0,
        jnp.max(size[:16]),
        jnp.where(lane == 1, jnp.max(size[16:]), jnp.max(jnp.abs(total))),
    )


def final_body(peaks_ref, weight_ref, input_ref, out_ref, key_ref, value_ref, pair_ref, one_ref):
    peaks = jnp.max(peaks_ref[...], axis=0, keepdims=True) + 1e-06
    key_peak, value_peak, input_peak = peaks[0, 0], peaks[0, 1], peaks[0, 2]
    key_ref[...] = (weight_ref[:16] / key_peak).astype(BF16)
    value_ref[...] = (weight_ref[16:] / value_peak).astype(BF16)
    out_ref[...] = (input_ref[...] / input_peak).astype(BF16)
    pair_ref[0] = key_peak
    pair_ref[1] = value_peak
    one_ref[0] = input_peak


def per_device(
    x_quant, x_scale, key_quant, key_scale, value_quant, value_scale, grad_key, grad_value
):
    place = jnp.stack([lax.axis_index(axis) for axis in ("x", "zl", "c")]).astype(jnp.int32)

    own = kernel_call(grads_body, shape((4, 4, 64, 192), BF16), [VMEM] * 2)(grad_key, grad_value)
    own = lax.all_to_all(own.reshape(16, 64, 192), ("x", "y"), 0, 0, tiled=True)
    own = own.reshape(4, 256, 192)
    twin = lax.ppermute(own, "c", [(0, 1), (1, 0)])

    inputs, weight = kernel_call(
        scale_body, (shape((192, 1024), BF16), shape((32, 1024), BF16)), [VMEM] * 6
    )(x_quant, x_scale, key_quant.T, key_scale.T, value_quant.T, value_scale.T)
    others = [shift(inputs, "x", by) for by in (1, 2, 3)]

    own, weight = lax.optimization_barrier((own, weight))
    weight = spread(weight, "zh").reshape(128, 1024)

    keep, *parts = kernel_call(
        weight_body,
        (shape((128, 1024), F32), shape((128, 1024), BF16))
        + (shape((64, 1024), BF16),) * 2
        + (shape((128, 1024), BF16),),
        [SMEM] + [VMEM] * 6,
        scratch=[pltpu.VMEM((2, 4, 2, 32, 1024), F32)],
        flops=10**11,
    )(place, own, twin, inputs, *others)
    parts = [shift(part, RING, by) for part, by in zip(parts, (1, 2, -2, -1))]
    weights = [weight] + [shift(weight, RING, by) for by in (1, 2, -1)]
    part = kernel_call(near_body, shape((4, 32, 1024), BF16), [VMEM] * 5)(keep, *parts)
    far = lax.all_to_all(part, "zh", 0, 0, tiled=True)

    keep, *parts = kernel_call(
        input_body,
        (shape((192, 1024), F32),) + (shape((192, 1024), BF16),) * 3,
        [SMEM] + [VMEM] * 6,
        scratch=[pltpu.VMEM((2, 4, 2, 32, 1024), BF16)],
        flops=10**11,
    )(place, own, twin, *weights)
    parts = [shift(part, "x", by) for part, by in zip(parts, (1, 2, 3))]

    weight_sum, input_sum, peaks = kernel_call(
        peak_body,
        (shape((32, 1024), F32), shape((192, 1024), F32), shape((64, 128), F32)),
        [VMEM] * 5,
    )(far, keep, *parts)
    peaks = lax.all_to_all(peaks, DP, 0, 0, tiled=True)
    peaks = spread(jnp.max(peaks, axis=0), TENSOR)
    grad_input, grad_key_weight, grad_value_weight, pair, one = kernel_call(
        final_body,
        (
            shape((192, 1024), BF16),
            shape((16, 1024), BF16),
            shape((16, 1024), BF16),
            shape((2,), F32),
            shape((1,), F32),
        ),
        [VMEM] * 3,
        (VMEM, VMEM, VMEM, SMEM, SMEM),
    )(peaks.reshape(8, 128), weight_sum, input_sum)
    return (grad_input, grad_key_weight.T, grad_value_weight.T, pair, one)


def solution(mesh):
    whole = Mesh(mesh.devices.reshape(4, 4, 4, 4, 2), (*DP, *TENSOR))
    in_specs = (
        P(DP, TENSOR),
        P(DP, TENSOR),
        P(TENSOR, DP),
        P(TENSOR, DP),
        P(TENSOR, DP),
        P(TENSOR, DP),
        P(DP, TENSOR),
        P(DP, TENSOR),
    )
    out_specs = (P(DP, TENSOR), P(TENSOR, DP), P(TENSOR, DP), P(), P())
    return jax.shard_map(
        per_device, mesh=whole, in_specs=in_specs, out_specs=out_specs, check_vma=False
    )
```

time: 227 us -> 159 us (0.70)
  waiting for transfers between devices: 103 us -> 19.1 us
  starting transfers between devices: 38.2 us -> 78.7 us
  blocking collectives: 66.7 us -> 42.4 us
  Pallas kernels: 0 us -> 8.14 us
  other arithmetic: 4.81 us -> 0.16 us
  matrix products: 4.22 us -> 0 us
    all_to_all x3 -> x1, waiting for transfers between devices: 54.7 us -> 0.01 us  [spread(): return lax.all_to_all(copies, axes, 0, 0, tiled=True)]
    ppermute x0 -> x14, starting transfers between devices: none -> 48.6 us  [the longest x13 42.8 us: shift(): lax.ppermute(value, axes, [(i, (i + by) % count) for i in range(count)])]
    all_to_all x3 -> x2, waiting for transfers between devices: 47.8 us -> 0.01 us  [the longest x1 0.01 us: per_device(): own = lax.all_to_all(own.reshape(16, 64, 192), ('x', 'y'), 0, 0, tiled=True)]
    ppermute x0 -> x14, waiting for transfers between devices: none -> 19.1 us  [the longest x13 19.1 us: shift(): lax.ppermute(value, axes, [(i, (i + by) % count) for i in range(count)])]
    all_to_all x2 -> x1, blocking collectives: 33.4 us -> 19.8 us  [spread(): return lax.all_to_all(copies, axes, 0, 0, tiled=True)]
    all_to_all x1, blocking collectives: 33.4 us -> 22.6 us  [per_device(): peaks = lax.all_to_all(peaks, DP, 0, 0, tiled=True)]
    pallas_call x0 -> x7, Pallas kernels: none -> 8.14 us  [the longest x1 2.65 us: per_device(): kernel_call(weight_body, (shape((128, 1024), F32), shape((128, 1024), BF1...]
    all_to_all x3 -> x1, starting transfers between devices: 20.2 us -> 13 us  [spread(): return lax.all_to_all(copies, axes, 0, 0, tiled=True)]
  transfers between devices with their start and end apart: 6 -> 17, of which waited for: 6 -> 4; matrix products, arithmetic and copies ran while one was open for 3% -> 1% of each run, Pallas kernels for 0% -> 4%
where the time goes in v2:
time: 159 us; the launch traced here: 158 us
  starting transfers between devices  78.7 us (49%)
  blocking collectives  42.4 us (27%)
  waiting for transfers between devices  19.1 us (12%)
  local copies, waits for them, and re-layouts  8.78 us (6%)
  Pallas kernels  8.14 us (5%)
    ppermute x13, starting transfers between devices, shift(): lax.ppermute(value, axes, [(i, (i + by) % count) for i in range(count)])  42.8 us
    all_to_all x1, blocking collectives, per_device(): peaks = lax.all_to_all(peaks, DP, 0, 0, tiled=True)  22.6 us
    all_to_all x1, blocking collectives, spread(): return lax.all_to_all(copies, axes, 0, 0, tiled=True)  19.8 us
    ppermute x13, waiting for transfers between devices, shift(): lax.ppermute(value, axes, [(i, (i + by) % count) for i in range(count)])  19.1 us
    all_to_all x1, starting transfers between devices, spread(): return lax.all_to_all(copies, axes, 0, 0, tiled=True)  13 us
    all_to_all x1, starting transfers between devices, per_device(): far = lax.all_to_all(part, 'zh', 0, 0, tiled=True)  9.42 us
    unnamed x31, local copies, waits for them, and re-layouts  8.04 us
    all_to_all x1, starting transfers between devices, per_device(): own = lax.all_to_all(own.reshape(16, 64, 192), ('x', 'y'), 0, 0, tiled=True)  7.72 us
  transfers between devices with their start and end apart: 17, of which 4 were waited for; matrix products, arithmetic and copies ran while one was open for 1% of the time, Pallas kernels for 4%

profile of v2, /device:TPU:1, one launch (start us, length us, event | category | flops | bytes accessed | tf_op | source)
XLA Modules:
  0.0 158.2 jit_solution(17898380859011793999)
XLA Ops:
  0.6 0.8 copy-done.1
  1.4 0.8 copy-done.2
  2.2 0.9 shard_map.119
  3.1 7.7 %all-to-all-start = ((bf16[16,64,192]{2,1,0:T(8,128)(2,1)}), bf16[16,64,192]{2,1,0:T(8,128)(2,1)S(1)}, u32[]{:S(2)}, u32[]{:S(2)}) async-start(bf16[16,64,192]{2,1,0:T(8,128)(2,1)} %bitcast.3), calls=%async_computation | async-start | bytes 1048576 | tf_op jit(solution)/shard_map/all_to_all | solution.py:146
  10.9 0.0 copy-start.3
  10.9 0.1 copy.18.x_scale_ref
  11.0 0.5 copy-done.12
  11.5 0.1 copy.16
  11.6 0.6 copy-done.13
  12.2 0.1 copy.17
  12.3 0.3 shard_map.120
  12.6 3.3 %collective-permute-start.1 = (bf16[192,1024]{1,0:T(8,128)(2,1)S(1)}, bf16[192,1024]{1,0:T(8,128)(2,1)S(1)}, u32[]{:S(2)}, u32[]{:S(2)}) collective-permute-start(bf16[192,1024]{1,0:T(8,128)(2,1)S(1)} %get-tuple-element.28.x0), channel_id=1, source_target_pairs={{0,8},{8,16},{16,24},{24,0},{1,9},{9,17},{17,25},{25,1},{2,10},{10... | collective-permute-start | bytes 1179656 | tf_op jit(solution)/shard_map/ppermute | solution.py:37
  15.9 4.3 %collective-permute-start.2 = (bf16[192,1024]{1,0:T(8,128)(2,1)S(1)}, bf16[192,1024]{1,0:T(8,128)(2,1)S(1)}, u32[]{:S(2)}, u32[]{:S(2)}) collective-permute-start(bf16[192,1024]{1,0:T(8,128)(2,1)S(1)} %get-tuple-element.28.x0), channel_id=1, source_target_pairs={{0,16},{8,24},{16,0},{24,8},{1,17},{9,25},{17,1},{25,9},{2,18},{10... | collective-permute-start | bytes 1179656 | tf_op jit(solution)/shard_map/ppermute | solution.py:37
  20.2 3.1 %collective-permute-start.3 = (bf16[192,1024]{1,0:T(8,128)(2,1)S(1)}, bf16[192,1024]{1,0:T(8,128)(2,1)S(1)}, u32[]{:S(2)}, u32[]{:S(2)}) collective-permute-start(bf16[192,1024]{1,0:T(8,128)(2,1)S(1)} %get-tuple-element.28.x0), channel_id=1, source_target_pairs={{0,24},{8,0},{16,8},{24,16},{1,25},{9,1},{17,9},{25,17},{2,26},{10... | collective-permute-start | bytes 1179656 | tf_op jit(solution)/shard_map/ppermute | solution.py:37
  23.3 5.8 %collective-permute-start = (bf16[4,256,192]{2,1,0:T(8,128)(2,1)S(1)}, bf16[4,256,192]{2,1,0:T(8,128)(2,1)S(1)}, u32[]{:S(2)}, u32[]{:S(2)}) collective-permute-start(bf16[4,256,192]{2,1,0:T(8,128)(2,1)S(1)} %bitcast.16), channel_id=1, source_target_pairs={{0,1},{1,0},{2,3},{3,2},{4,5},{5,4},{6,7},{7,6},{8,9},{9,8},{10,11... | collective-permute-start | bytes 1179656 | tf_op jit(solution)/shard_map/ppermute | solution.py:148
  29.2 0.1 pad_add_fusion.place
  29.2 0.7 broadcast_in_dim.4
  30.0 13.0 %all-to-all-start.2 = ((bf16[4,32,1024]{2,1,0:T(8,128)(2,1)}), bf16[4,32,1024]{2,1,0:T(8,128)(2,1)S(1)}, u32[]{:S(2)}, u32[]{:S(2)}) async-start(bf16[4,32,1024]{2,1,0:T(8,128)(2,1)} %broadcast_in_dim.4), calls=%async_computation.2 | async-start | bytes 524288 | tf_op jit(solution)/shard_map/all_to_all | solution.py:43
  43.0 0.7 copy-done.5
  43.7 1.0 copy-done.6
  44.7 2.7 %shard_map.121 = (f32[128,1024]{1,0:T(8,128)S(1)}, bf16[128,1024]{1,0:T(8,128)(2,1)}, bf16[64,1024]{1,0:T(8,128)(2,1)}, bf16[64,1024]{1,0:T(8,128)(2,1)S(1)}, bf16[128,1024]{1,0:T(8,128)(2,1)}) custom-call(s32[3]{0:T(128)S(1)} %pad_add_fusion.place, bf16[4,256,192]{2,1,0:T(8,128)(2,1)S(1)} %bitcast.17, ...), custom_call_target="tpu_custom_call" | custom-call | flops 99999997952 | tf_op jit(solution)/shard_map/pallas_call | solution.py:158
  47.4 3.1 %collective-permute-start.5 = (bf16[64,1024]{1,0:T(8,128)(2,1)}, bf16[64,1024]{1,0:T(8,128)(2,1)S(1)}, u32[]{:S(2)}, u32[]{:S(2)}) collective-permute-start(bf16[64,1024]{1,0:T(8,128)(2,1)} %get-tuple-element.31), channel_id=1, source_target_pairs={{0,64},{32,96},{64,128},{96,160},{128,192},{160,224},{192,256},{22... | collective-permute-start | bytes 393224 | tf_op jit(solution)/shard_map/ppermute | solution.py:37
  50.5 5.2 %collective-permute-start.6 = (bf16[64,1024]{1,0:T(8,128)(2,1)S(1)}, bf16[64,1024]{1,0:T(8,128)(2,1)S(1)}, u32[]{:S(2)}, u32[]{:S(2)}) collective-permute-start(bf16[64,1024]{1,0:T(8,128)(2,1)S(1)} %get-tuple-element.32), channel_id=1, source_target_pairs={{0,448},{32,480},{64,0},{96,32},{128,64},{160,96},{192,128},{224,1... | collective-permute-start | bytes 393224 | tf_op jit(solution)/shard_map/ppermute | solution.py:37
  55.7 2.6 %collective-permute-start.4 = (bf16[128,1024]{1,0:T(8,128)(2,1)}, bf16[128,1024]{1,0:T(8,128)(2,1)S(1)}, u32[]{:S(2)}, u32[]{:S(2)}) collective-permute-start(bf16[128,1024]{1,0:T(8,128)(2,1)} %get-tuple-element.30), channel_id=1, source_target_pairs={{0,32},{32,64},{64,96},{96,128},{128,160},{160,192},{192,224},{224... | collective-permute-start | bytes 786440 | tf_op jit(solution)/shard_map/ppermute | solution.py:37
  58.3 3.8 %collective-permute-start.7 = (bf16[128,1024]{1,0:T(8,128)(2,1)}, bf16[128,1024]{1,0:T(8,128)(2,1)S(1)}, u32[]{:S(2)}, u32[]{:S(2)}) collective-permute-start(bf16[128,1024]{1,0:T(8,128)(2,1)} %get-tuple-element.33), channel_id=1, source_target_pairs={{0,480},{32,0},{64,32},{96,64},{128,96},{160,128},{192,160},{224,1... | collective-permute-start | bytes 786440 | tf_op jit(solution)/shard_map/ppermute | solution.py:37
  62.2 2.6 %collective-permute-start.10 = (bf16[128,1024]{1,0:T(8,128)(2,1)S(1)}, bf16[128,1024]{1,0:T(8,128)(2,1)S(1)}, u32[]{:S(2)}, u32[]{:S(2)}) collective-permute-start(bf16[128,1024]{1,0:T(8,128)(2,1)S(1)} %bitcast.19), channel_id=1, source_target_pairs={{0,480},{32,0},{64,32},{96,64},{128,96},{160,128},{192,160},{224,1... | collective-permute-start | bytes 786440 | tf_op jit(solution)/shard_map/ppermute | solution.py:37
  64.8 2.9 %collective-permute-start.8 = (bf16[128,1024]{1,0:T(8,128)(2,1)S(1)}, bf16[128,1024]{1,0:T(8,128)(2,1)S(1)}, u32[]{:S(2)}, u32[]{:S(2)}) collective-permute-start(bf16[128,1024]{1,0:T(8,128)(2,1)S(1)} %bitcast.20), channel_id=1, source_target_pairs={{0,32},{32,64},{64,96},{96,128},{128,160},{160,192},{192,224},{224... | collective-permute-start | bytes 786440 | tf_op jit(solution)/shard_map/ppermute | solution.py:37
  67.7 2.8 %collective-permute-start.9 = (bf16[128,1024]{1,0:T(8,128)(2,1)S(1)}, bf16[128,1024]{1,0:T(8,128)(2,1)S(1)}, u32[]{:S(2)}, u32[]{:S(2)}) collective-permute-start(bf16[128,1024]{1,0:T(8,128)(2,1)S(1)} %bitcast.21), channel_id=1, source_target_pairs={{0,64},{32,96},{64,128},{96,160},{128,192},{160,224},{192,256},{22... | collective-permute-start | bytes 786440 | tf_op jit(solution)/shard_map/ppermute | solution.py:37
  70.5 0.0 collective-permute-done.4.r1
  70.6 0.8 shard_map.122
  71.4 9.4 %all-to-all-start.1 = ((bf16[4,32,1024]{2,1,0:T(8,128)(2,1)}), bf16[4,32,1024]{2,1,0:T(8,128)(2,1)S(1)}, u32[]{:S(2)}, u32[]{:S(2)}) async-start(bf16[4,32,1024]{2,1,0:T(8,128)(2,1)} %shard_map.122), calls=%async_computation.1 | async-start | bytes 524288 | tf_op jit(solution)/shard_map/all_to_all | solution.py:170
  80.8 0.7 copy-done.7
  81.5 3.9 %collective-permute-done.9.w2 = bf16[128,1024]{1,0:T(8,128)(2,1)S(1)} collective-permute-done((bf16[128,1024]{1,0:T(8,128)(2,1)S(1)}, bf16[128,1024]{1,0:T(8,128)(2,1)S(1)}, u32[]{:S(2)}, u32[]{:S(2)}) %collective-permute-start.9) | collective-permute-done | bytes 262176 | tf_op jit(solution)/shard_map/ppermute | solution.py:37
  85.4 0.7 copy-done.9
  86.1 0.9 copy-done.8
  87.0 0.9 copy-done.10
  88.0 2.2 %shard_map.123 = (f32[192,1024]{1,0:T(8,128)S(1)}, bf16[192,1024]{1,0:T(8,128)(2,1)}, bf16[192,1024]{1,0:T(8,128)(2,1)}, bf16[192,1024]{1,0:T(8,128)(2,1)S(1)}) custom-call(s32[3]{0:T(128)S(1)} %pad_add_fusion.place, bf16[4,256,192]{2,1,0:T(8,128)(2,1)S(1)} %bitcast.18, bf16[4,256,192]{2,1,0:T(8,128)(2,1)S(1)} %collective-permute-done.twin_ref, ...), custom_call_target="tpu_custom_call" | custom-call | flops 99999997952 | tf_op jit(solution)/shard_map/pallas_call | solution.py:172
  90.2 2.8 %collective-permute-start.11 = (bf16[192,1024]{1,0:T(8,128)(2,1)}, bf16[192,1024]{1,0:T(8,128)(2,1)S(1)}, u32[]{:S(2)}, u32[]{:S(2)}) collective-permute-start(bf16[192,1024]{1,0:T(8,128)(2,1)} %get-tuple-element.36), channel_id=1, source_target_pairs={{0,8},{8,16},{16,24},{24,0},{1,9},{9,17},{17,25},{25,1},{2,10},{10... | collective-permute-start | bytes 1179656 | tf_op jit(solution)/shard_map/ppermute | solution.py:37
  93.0 2.1 %collective-permute-start.12 = (bf16[192,1024]{1,0:T(8,128)(2,1)}, bf16[192,1024]{1,0:T(8,128)(2,1)S(1)}, u32[]{:S(2)}, u32[]{:S(2)}) collective-permute-start(bf16[192,1024]{1,0:T(8,128)(2,1)} %get-tuple-element.37), channel_id=1, source_target_pairs={{0,16},{8,24},{16,0},{24,8},{1,17},{9,25},{17,1},{25,9},{2,18},{10... | collective-permute-start | bytes 1179656 | tf_op jit(solution)/shard_map/ppermute | solution.py:37
  95.2 4.1 %collective-permute-start.13 = (bf16[192,1024]{1,0:T(8,128)(2,1)S(1)}, bf16[192,1024]{1,0:T(8,128)(2,1)S(1)}, u32[]{:S(2)}, u32[]{:S(2)}) collective-permute-start(bf16[192,1024]{1,0:T(8,128)(2,1)S(1)} %get-tuple-element.38), channel_id=1, source_target_pairs={{0,24},{8,0},{16,8},{24,16},{1,25},{9,1},{17,9},{25,17},{2,26},{10... | collective-permute-start | bytes 1179656 | tf_op jit(solution)/shard_map/ppermute | solution.py:37
  99.3 4.1 %collective-permute-done.11.r1 = bf16[192,1024]{1,0:T(8,128)(2,1)S(1)} collective-permute-done((bf16[192,1024]{1,0:T(8,128)(2,1)}, bf16[192,1024]{1,0:T(8,128)(2,1)S(1)}, u32[]{:S(2)}, u32[]{:S(2)}) %collective-permute-start.11) | collective-permute-done | bytes 393248 | tf_op jit(solution)/shard_map/ppermute | solution.py:37
  103.4 5.2 %collective-permute-done.12.r2 = bf16[192,1024]{1,0:T(8,128)(2,1)S(1)} collective-permute-done((bf16[192,1024]{1,0:T(8,128)(2,1)}, bf16[192,1024]{1,0:T(8,128)(2,1)S(1)}, u32[]{:S(2)}, u32[]{:S(2)}) %collective-permute-start.12) | collective-permute-done | bytes 393248 | tf_op jit(solution)/shard_map/ppermute | solution.py:37
  108.6 5.8 %collective-permute-done.13.r3 = bf16[192,1024]{1,0:T(8,128)(2,1)S(1)} collective-permute-done((bf16[192,1024]{1,0:T(8,128)(2,1)S(1)}, bf16[192,1024]{1,0:T(8,128)(2,1)S(1)}, u32[]{:S(2)}, u32[]{:S(2)}) %collective-permute-start.13) | collective-permute-done | bytes 393248 | tf_op jit(solution)/shard_map/ppermute | solution.py:37
  114.4 0.3 shard_map.124
  114.7 22.6 %all_to_all.32 = f32[64,1,128]{2,1,0:T(1,128)S(1)} all-to-all(f32[64,1,128]{2,1,0:T(1,128)S(1)} %bitcast.27), channel_id=1, replica_groups=mesh['zh'=4,'zl'=4,'x'=4,'y'=4,'c'=2] {'zh','zl','x'}, dimensions={0} | all-to-all | bytes 65536 | tf_op jit(solution)/shard_map/all_to_all | solution.py:186
  137.4 0.1 reduce_max.9
  137.5 19.8 %all_to_all.33 = f32[8,1,128]{2,1,0:T(1,128)S(1)} all-to-all(f32[8,1,128]{2,1,0:T(1,128)S(1)} %broadcast_in_dim.5), channel_id=1, replica_groups=mesh['zh'=4,'zl'=4,'x'=4,'y'=4,'c'=2] {'y','c'}, dimensions={0} | all-to-all | bytes 8192 | tf_op jit(solution)/shard_map/all_to_all | solution.py:43
  157.2 1.0 shard_map.125
  (30 shorter events, 0.1 us)
Async XLA Ops:
  0.6 0.8 copy-start.1
  1.4 0.8 copy-start.2
  3.1 7.7 %copy-start.11 = (f32[192,8]{0,1:T(8,128)S(1)}, f32[192,8]{0,1:T(8,128)}, u32[]{:S(2)}) copy-start(f32[192,8]{0,1:T(8,128)} %param.9) | copy-start | bytes 18436
  3.1 9.2 %copy-start = (bf16[192,1024]{1,0:T(8,128)(2,1)S(1)}, bf16[192,1024]{1,0:T(8,128)(2,1)}, u32[]{:S(2)}) copy-start(bf16[192,1024]{1,0:T(8,128)(2,1)} %x_ref.1) | copy-start | bytes 1179652
  3.1 20.2 %all-to-all-start = ((bf16[16,64,192]{2,1,0:T(8,128)(2,1)}), bf16[16,64,192]{2,1,0:T(8,128)(2,1)S(1)}, u32[]{:S(2)}, u32[]{:S(2)}) async-start(bf16[16,64,192]{2,1,0:T(8,128)(2,1)} %bitcast.3), calls=%async_computation | async-start | bytes 1048576 | tf_op jit(solution)/shard_map/all_to_all | solution.py:146
  10.9 0.7 copy-start.12
  10.9 1.4 copy-start.3
  10.9 1.4 copy-start.4
  11.5 0.7 copy-start.13
  12.6 30.3 %collective-permute-start.1 = (bf16[192,1024]{1,0:T(8,128)(2,1)S(1)}, bf16[192,1024]{1,0:T(8,128)(2,1)S(1)}, u32[]{:S(2)}, u32[]{:S(2)}) collective-permute-start(bf16[192,1024]{1,0:T(8,128)(2,1)S(1)} %get-tuple-element.28.x0), channel_id=1, source_target_pairs={{0,8},{8,16},{16,24},{24,0},{1,9},{9,17},{17,25},{25,1},{2,10},{10... | collective-permute-start | bytes 1179656 | tf_op jit(solution)/shard_map/ppermute | solution.py:37
  15.9 27.0 %collective-permute-start.2 = (bf16[192,1024]{1,0:T(8,128)(2,1)S(1)}, bf16[192,1024]{1,0:T(8,128)(2,1)S(1)}, u32[]{:S(2)}, u32[]{:S(2)}) collective-permute-start(bf16[192,1024]{1,0:T(8,128)(2,1)S(1)} %get-tuple-element.28.x0), channel_id=1, source_target_pairs={{0,16},{8,24},{16,0},{24,8},{1,17},{9,25},{17,1},{25,9},{2,18},{10... | collective-permute-start | bytes 1179656 | tf_op jit(solution)/shard_map/ppermute | solution.py:37
  20.2 22.7 %collective-permute-start.3 = (bf16[192,1024]{1,0:T(8,128)(2,1)S(1)}, bf16[192,1024]{1,0:T(8,128)(2,1)S(1)}, u32[]{:S(2)}, u32[]{:S(2)}) collective-permute-start(bf16[192,1024]{1,0:T(8,128)(2,1)S(1)} %get-tuple-element.28.x0), channel_id=1, source_target_pairs={{0,24},{8,0},{16,8},{24,16},{1,25},{9,1},{17,9},{25,17},{2,26},{10... | collective-permute-start | bytes 1179656 | tf_op jit(solution)/shard_map/ppermute | solution.py:37
  23.3 20.4 %collective-permute-start = (bf16[4,256,192]{2,1,0:T(8,128)(2,1)S(1)}, bf16[4,256,192]{2,1,0:T(8,128)(2,1)S(1)}, u32[]{:S(2)}, u32[]{:S(2)}) collective-permute-start(bf16[4,256,192]{2,1,0:T(8,128)(2,1)S(1)} %bitcast.16), channel_id=1, source_target_pairs={{0,1},{1,0},{2,3},{3,2},{4,5},{5,4},{6,7},{7,6},{8,9},{9,8},{10,11... | collective-permute-start | bytes 1179656 | tf_op jit(solution)/shard_map/ppermute | solution.py:148
  30.0 32.2 %all-to-all-start.2 = ((bf16[4,32,1024]{2,1,0:T(8,128)(2,1)}), bf16[4,32,1024]{2,1,0:T(8,128)(2,1)S(1)}, u32[]{:S(2)}, u32[]{:S(2)}) async-start(bf16[4,32,1024]{2,1,0:T(8,128)(2,1)} %broadcast_in_dim.4), calls=%async_computation.2 | async-start | bytes 524288 | tf_op jit(solution)/shard_map/all_to_all | solution.py:43
  43.0 0.7 copy-start.5
  43.7 1.0 copy-start.6
  47.4 17.4 %collective-permute-start.5 = (bf16[64,1024]{1,0:T(8,128)(2,1)}, bf16[64,1024]{1,0:T(8,128)(2,1)S(1)}, u32[]{:S(2)}, u32[]{:S(2)}) collective-permute-start(bf16[64,1024]{1,0:T(8,128)(2,1)} %get-tuple-element.31), channel_id=1, source_target_pairs={{0,64},{32,96},{64,128},{96,160},{128,192},{160,224},{192,256},{22... | collective-permute-start | bytes 393224 | tf_op jit(solution)/shard_map/ppermute | solution.py:37
  50.5 17.3 %collective-permute-start.6 = (bf16[64,1024]{1,0:T(8,128)(2,1)S(1)}, bf16[64,1024]{1,0:T(8,128)(2,1)S(1)}, u32[]{:S(2)}, u32[]{:S(2)}) collective-permute-start(bf16[64,1024]{1,0:T(8,128)(2,1)S(1)} %get-tuple-element.32), channel_id=1, source_target_pairs={{0,448},{32,480},{64,0},{96,32},{128,64},{160,96},{192,128},{224,1... | collective-permute-start | bytes 393224 | tf_op jit(solution)/shard_map/ppermute | solution.py:37
  55.7 14.9 %collective-permute-start.4 = (bf16[128,1024]{1,0:T(8,128)(2,1)}, bf16[128,1024]{1,0:T(8,128)(2,1)S(1)}, u32[]{:S(2)}, u32[]{:S(2)}) collective-permute-start(bf16[128,1024]{1,0:T(8,128)(2,1)} %get-tuple-element.30), channel_id=1, source_target_pairs={{0,32},{32,64},{64,96},{96,128},{128,160},{160,192},{192,224},{224... | collective-permute-start | bytes 786440 | tf_op jit(solution)/shard_map/ppermute | solution.py:37
  58.3 12.2 %collective-permute-start.7 = (bf16[128,1024]{1,0:T(8,128)(2,1)}, bf16[128,1024]{1,0:T(8,128)(2,1)S(1)}, u32[]{:S(2)}, u32[]{:S(2)}) collective-permute-start(bf16[128,1024]{1,0:T(8,128)(2,1)} %get-tuple-element.33), channel_id=1, source_target_pairs={{0,480},{32,0},{64,32},{96,64},{128,96},{160,128},{192,160},{224,1... | collective-permute-start | bytes 786440 | tf_op jit(solution)/shard_map/ppermute | solution.py:37
  62.2 18.6 %collective-permute-start.10 = (bf16[128,1024]{1,0:T(8,128)(2,1)S(1)}, bf16[128,1024]{1,0:T(8,128)(2,1)S(1)}, u32[]{:S(2)}, u32[]{:S(2)}) collective-permute-start(bf16[128,1024]{1,0:T(8,128)(2,1)S(1)} %bitcast.19), channel_id=1, source_target_pairs={{0,480},{32,0},{64,32},{96,64},{128,96},{160,128},{192,160},{224,1... | collective-permute-start | bytes 786440 | tf_op jit(solution)/shard_map/ppermute | solution.py:37
  64.8 16.0 %collective-permute-start.8 = (bf16[128,1024]{1,0:T(8,128)(2,1)S(1)}, bf16[128,1024]{1,0:T(8,128)(2,1)S(1)}, u32[]{:S(2)}, u32[]{:S(2)}) collective-permute-start(bf16[128,1024]{1,0:T(8,128)(2,1)S(1)} %bitcast.20), channel_id=1, source_target_pairs={{0,32},{32,64},{64,96},{96,128},{128,160},{160,192},{192,224},{224... | collective-permute-start | bytes 786440 | tf_op jit(solution)/shard_map/ppermute | solution.py:37
  67.7 17.6 %collective-permute-start.9 = (bf16[128,1024]{1,0:T(8,128)(2,1)S(1)}, bf16[128,1024]{1,0:T(8,128)(2,1)S(1)}, u32[]{:S(2)}, u32[]{:S(2)}) collective-permute-start(bf16[128,1024]{1,0:T(8,128)(2,1)S(1)} %bitcast.21), channel_id=1, source_target_pairs={{0,64},{32,96},{64,128},{96,160},{128,192},{160,224},{192,256},{22... | collective-permute-start | bytes 786440 | tf_op jit(solution)/shard_map/ppermute | solution.py:37
  71.4 27.9 %all-to-all-start.1 = ((bf16[4,32,1024]{2,1,0:T(8,128)(2,1)}), bf16[4,32,1024]{2,1,0:T(8,128)(2,1)S(1)}, u32[]{:S(2)}, u32[]{:S(2)}) async-start(bf16[4,32,1024]{2,1,0:T(8,128)(2,1)} %shard_map.122), calls=%async_computation.1 | async-start | bytes 524288 | tf_op jit(solution)/shard_map/all_to_all | solution.py:170
  80.8 0.7 copy-start.7
  85.4 0.7 copy-start.9
  86.1 0.9 copy-start.8
  87.0 0.9 copy-start.10
  90.2 13.2 %collective-permute-start.11 = (bf16[192,1024]{1,0:T(8,128)(2,1)}, bf16[192,1024]{1,0:T(8,128)(2,1)S(1)}, u32[]{:S(2)}, u32[]{:S(2)}) collective-permute-start(bf16[192,1024]{1,0:T(8,128)(2,1)} %get-tuple-element.36), channel_id=1, source_target_pairs={{0,8},{8,16},{16,24},{24,0},{1,9},{9,17},{17,25},{25,1},{2,10},{10... | collective-permute-start | bytes 1179656 | tf_op jit(solution)/shard_map/ppermute | solution.py:37
  93.0 15.6 %collective-permute-start.12 = (bf16[192,1024]{1,0:T(8,128)(2,1)}, bf16[192,1024]{1,0:T(8,128)(2,1)S(1)}, u32[]{:S(2)}, u32[]{:S(2)}) collective-permute-start(bf16[192,1024]{1,0:T(8,128)(2,1)} %get-tuple-element.37), channel_id=1, source_target_pairs={{0,16},{8,24},{16,0},{24,8},{1,17},{9,25},{17,1},{25,9},{2,18},{10... | collective-permute-start | bytes 1179656 | tf_op jit(solution)/shard_map/ppermute | solution.py:37
  95.2 19.2 %collective-permute-start.13 = (bf16[192,1024]{1,0:T(8,128)(2,1)S(1)}, bf16[192,1024]{1,0:T(8,128)(2,1)S(1)}, u32[]{:S(2)}, u32[]{:S(2)}) collective-permute-start(bf16[192,1024]{1,0:T(8,128)(2,1)S(1)} %get-tuple-element.38), channel_id=1, source_target_pairs={{0,24},{8,0},{16,8},{24,16},{1,25},{9,1},{17,9},{25,17},{2,26},{10... | collective-permute-start | bytes 1179656 | tf_op jit(solution)/shard_map/ppermute | solution.py:37

commit v3 on v2

v3 whole, which is shorter than its diff:
```python
import jax
import jax.numpy as jnp
from jax import lax
from jax.experimental import pallas as pl
from jax.experimental.pallas import tpu as pltpu
from jax.sharding import Mesh, PartitionSpec as P

BLOCK = 128
DP = ("zh", "zm", "zp", "x")
TENSOR = ("y", "c")
RING = ("zh", "zm", "zp")
F32, BF16 = jnp.float32, jnp.bfloat16
VMEM = pl.BlockSpec(memory_space=pltpu.VMEM)
SMEM = pl.BlockSpec(memory_space=pltpu.SMEM)


def kernel_call(body, out_shape, in_specs, out_specs=None, scratch=(), flops=0):
    if out_specs is None:
        out_specs = jax.tree.map(lambda _: VMEM, out_shape)
    return pl.pallas_call(
        body,
        out_shape=out_shape,
        in_specs=in_specs,
        out_specs=out_specs,
        scratch_shapes=list(scratch),
        cost_estimate=pl.CostEstimate(flops=flops, bytes_accessed=0, transcendentals=0),
        compiler_params=pltpu.CompilerParams(vmem_limit_bytes=16 * 2**20),
    )


def shape(dims, dtype):
    return jax.ShapeDtypeStruct(dims, dtype)


def shift(value, axes, by):
    count = lax.axis_size(axes)
    return lax.ppermute(value, axes, [(i, (i + by) % count) for i in range(count)])


def spread(block, axes):
    count = lax.axis_size(axes)
    copies = jnp.broadcast_to(block[None], (count, *block.shape))
    return lax.all_to_all(copies, axes, 0, 0, tiled=True)


def grads_body(key_ref, value_ref, out_ref):
    key, value = key_ref[...].T, value_ref[...].T
    for x in range(4):
        rows = []
        for zz in range(2):
            start = zz * 64 + x * 16
            rows += [key[start : start + 16], value[start : start + 16]]
        block = jnp.concatenate(rows, axis=0)
        for copy in range(4):
            out_ref[x, copy] = block


def scale_body(x_ref, x_scale_ref, key_ref, key_scale_ref, value_ref, value_scale_ref, out_ref, weight_ref):
    for b in range(8):
        at = slice(b * BLOCK, (b + 1) * BLOCK)
        out_ref[:, at] = (x_ref[:, at].astype(F32) * x_scale_ref[:, b : b + 1]).astype(BF16)
        for part, ref, scale in ((0, key_ref, key_scale_ref), (1, value_ref, value_scale_ref)):
            weight_ref[part * 16 : (part + 1) * 16, at] = (
                ref[:, at].astype(F32) * scale[:, b : b + 1]
            ).astype(BF16)


def weight_body(place, own, twin, x0, x1, x2, x3, keep_ref, key_ref, value_ref, total):
    x, zp, core = place[0], place[2], place[3]
    inputs = jnp.concatenate([ref[...] for ref in (x0, x1, x2, x3)], axis=0)
    for i, part in enumerate((own, twin)):
        lhs = jnp.concatenate([part[lax.rem(x + 4 - back, 4)] for back in range(4)], axis=1)
        value = jnp.dot(lhs, inputs, preferred_element_type=F32)
        total[i] = value.reshape(4, 2, 32, 1024)
        zm = lax.rem(core + i, 2)
        for zh in range(4):
            keep_ref[zh, zm] = total[i, zh, zp]
            key_ref[zh, zm] = total[i, zh, 1 - zp, :16].astype(BF16)
            value_ref[zh, zm] = total[i, zh, 1 - zp, 16:].astype(BF16)


def input_body(place, own, twin, w0, w1, w2, w3, keep_ref, out1, out2a, out2b, out3, weight):
    x, zl, core = place[0], place[1] * 2 + place[2], place[3]
    for back, ref in enumerate((w0, w1, w2, w3)):
        group = lax.rem(zl + 4 - back, 4)
        half, zp = lax.rem(group // 2 + core, 2), lax.rem(group, 2)
        for zh in range(4):
            weight[half, zh, zp] = ref[zh]
    for k, out in enumerate((keep_ref, out1, None, out3)):
        member = lax.rem(x + k, 4)
        lhs = jnp.concatenate([own[member].T, twin[member].T], axis=1)
        value = jnp.dot(lhs, weight[...].reshape(512, 1024), preferred_element_type=F32)
        if k == 2:
            out2a[...] = value[:96].astype(BF16)
            out2b[...] = value[96:].astype(BF16)
        else:
            out[...] = value.astype(out.dtype)


def near_body(keep_ref, key_ref, value_ref, out_ref):
    for zh in range(4):
        for zm in range(2):
            keep = keep_ref[zh, zm]
            out_ref[zh * 2 + zm, :16] = (keep[:16] + key_ref[zh, zm].astype(F32)).astype(BF16)
            out_ref[zh * 2 + zm, 16:] = (keep[16:] + value_ref[zh, zm].astype(F32)).astype(BF16)


def peak_body(far_ref, keep_ref, r1, r2a, r2b, r3, weight_ref, input_ref, peak_ref):
    weight = far_ref[0].astype(F32)
    for i in range(1, 8):
        weight = weight + far_ref[i].astype(F32)
    weight_ref[...] = weight
    input_peak = None
    for at, r2 in ((slice(0, 96), r2a), (slice(96, 192), r2b)):
        total = keep_ref[at] + r1[at].astype(F32) + r2[...].astype(F32) + r3[at].astype(F32)
        input_ref[at] = total
        peak = jnp.max(jnp.abs(total))
        input_peak = peak if input_peak is None else jnp.maximum(input_peak, peak)
    size = jnp.abs(weight)
    lane = lax.broadcasted_iota(jnp.int32, peak_ref.shape, 1)
    peak_ref[...] = jnp.where(
        lane == 0,
        jnp.max(size[:16]),
        jnp.where(lane == 1, jnp.max(size[16:]), input_peak),
    )


def final_body(peaks_ref, weight_ref, input_ref, out_ref, key_ref, value_ref, pair_ref, one_ref):
    peaks = jnp.max(peaks_ref[...], axis=0, keepdims=True) + 1e-06
    key_peak, value_peak, input_peak = peaks[0, 0], peaks[0, 1], peaks[0, 2]
    key_ref[...] = (weight_ref[:16] / key_peak).astype(BF16)
    value_ref[...] = (weight_ref[16:] / value_peak).astype(BF16)
    out_ref[...] = (input_ref[...] / input_peak).astype(BF16)
    pair_ref[0] = key_peak
    pair_ref[1] = value_peak
    one_ref[0] = input_peak


def per_device(
    x_quant, x_scale, key_quant, key_scale, value_quant, value_scale, grad_key, grad_value
):
    place = jnp.stack([lax.axis_index(axis) for axis in ("x", "zm", "zp", "c")]).astype(jnp.int32)

    own = kernel_call(
        grads_body,
        shape((4, 4, 64, 192), BF16),
        [VMEM] * 2,
    )(grad_key, grad_value)
    own = lax.all_to_all(own.reshape(16, 64, 192), ("x", "y"), 0, 0, tiled=True)
    own = own.reshape(4, 256, 192)
    twin = lax.ppermute(own, "c", [(0, 1), (1, 0)])

    inputs, weight = kernel_call(
        scale_body, (shape((192, 1024), BF16), shape((32, 1024), BF16)), [VMEM] * 6
    )(x_quant, x_scale, key_quant.T, key_scale.T, value_quant.T, value_scale.T)
    others = [shift(inputs, "x", by) for by in (1, 2, 3)]

    own, weight = lax.optimization_barrier((own, weight))
    weight = spread(weight, "zh")

    keep, key, value = kernel_call(
        weight_body,
        (shape((4, 2, 32, 1024), F32),) + (shape((4, 2, 16, 1024), BF16),) * 2,
        [SMEM] + [VMEM] * 6,
        scratch=[pltpu.VMEM((2, 4, 2, 32, 1024), F32)],
        flops=10**11,
    )(place, own, twin, inputs, *others)
    key, value = shift(key, RING, -1), shift(value, RING, 1)
    weights = [weight] + [shift(weight, RING, by) for by in (1, -2, -1)]
    part = kernel_call(near_body, shape((8, 32, 1024), BF16), [VMEM] * 3)(keep, key, value)
    far = lax.all_to_all(part, ("zh", "zm"), 0, 0, tiled=True)

    block, half = shape((192, 1024), BF16), shape((96, 1024), BF16)
    keep, *parts = kernel_call(
        input_body,
        (shape((192, 1024), F32), block, half, half, block),
        [SMEM] + [VMEM] * 6,
        scratch=[pltpu.VMEM((2, 4, 2, 32, 1024), BF16)],
        flops=10**11,
    )(place, own, twin, *weights)
    parts = [shift(part, "x", by) for part, by in zip(parts, (1, 2, -2, -1))]

    weight_sum, input_sum, peaks = kernel_call(
        peak_body,
        (shape((32, 1024), F32), shape((192, 1024), F32), shape((64, 128), F32)),
        [VMEM] * 6,
    )(far, keep, *parts)
    peaks = lax.all_to_all(peaks, DP, 0, 0, tiled=True)
    peaks = spread(jnp.max(peaks, axis=0), TENSOR)
    grad_input, grad_key_weight, grad_value_weight, pair, one = kernel_call(
        final_body,
        (
            shape((192, 1024), BF16),
            shape((16, 1024), BF16),
            shape((16, 1024), BF16),
            shape((2,), F32),
            shape((1,), F32),
        ),
        [VMEM] * 3,
        (VMEM, VMEM, VMEM, SMEM, SMEM),
    )(peaks.reshape(8, 128), weight_sum, input_sum)
    return (grad_input, grad_key_weight.T, grad_value_weight.T, pair, one)


def solution(mesh):
    whole = Mesh(mesh.devices.reshape(4, 2, 2, 4, 4, 2), (*DP, *TENSOR))
    in_specs = (
        P(DP, TENSOR),
        P(DP, TENSOR),
        P(TENSOR, DP),
        P(TENSOR, DP),
        P(TENSOR, DP),
        P(TENSOR, DP),
        P(DP, TENSOR),
        P(DP, TENSOR),
    )
    out_specs = (P(DP, TENSOR), P(TENSOR, DP), P(TENSOR, DP), P(), P())
    return jax.shard_map(
        per_device, mesh=whole, in_specs=in_specs, out_specs=out_specs, check_vma=False
    )
```

time: 159 us -> 152 us (0.956)
  blocking collectives: 42.4 us -> 38 us
  starting transfers between devices: 78.7 us -> 76.5 us
    ppermute x13 -> x12, waiting for transfers between devices: 19.1 us -> 10.7 us  [shift(): lax.ppermute(value, axes, [(i, (i + by) % count) for i in range(count)])]
    all_to_all x1, waiting for transfers between devices: 0.01 us -> 8.22 us  [per_device(): far = lax.all_to_all(part, ('zh', 'zm'), 0, 0, tiled=True)]
    all_to_all x1, blocking collectives: 22.6 us -> 18.1 us  [per_device(): peaks = lax.all_to_all(peaks, DP, 0, 0, tiled=True)]
    all_to_all x1, starting transfers between devices: 9.42 us -> 5.62 us  [per_device(): far = lax.all_to_all(part, ('zh', 'zm'), 0, 0, tiled=True)]
    ppermute x13 -> x12, starting transfers between devices: 42.8 us -> 44.4 us  [shift(): lax.ppermute(value, axes, [(i, (i + by) % count) for i in range(count)])]
    unnamed x31 -> x27, local copies, waits for them, and re-layouts: 8.04 us -> 6.52 us
  transfers between devices with their start and end apart: 17 -> 16, of which waited for: 4 -> 5; matrix products, arithmetic and copies ran while one was open for 1% -> 1% of each run, Pallas kernels for 4% -> 4%
where the time goes in v3:
time: 152 us; the launch traced here: 150 us
  starting transfers between devices  76.5 us (50%)
  blocking collectives  38 us (25%)
  waiting for transfers between devices  19.3 us (13%)
  Pallas kernels  8.35 us (5%)
  local copies, waits for them, and re-layouts  7.24 us (5%)
    ppermute x12, starting transfers between devices, shift(): lax.ppermute(value, axes, [(i, (i + by) % count) for i in range(count)])  44.4 us
    all_to_all x1, blocking collectives, spread(): return lax.all_to_all(copies, axes, 0, 0, tiled=True)  19.9 us
    all_to_all x1, blocking collectives, per_device(): peaks = lax.all_to_all(peaks, DP, 0, 0, tiled=True)  18.1 us
    all_to_all x1, starting transfers between devices, spread(): return lax.all_to_all(copies, axes, 0, 0, tiled=True)  13 us
    ppermute x12, waiting for transfers between devices, shift(): lax.ppermute(value, axes, [(i, (i + by) % count) for i in range(count)])  10.7 us
    all_to_all x1, waiting for transfers between devices, per_device(): far = lax.all_to_all(part, ('zh', 'zm'), 0, 0, tiled=True)  8.22 us
    all_to_all x1, starting transfers between devices, per_device(): own = lax.all_to_all(own.reshape(16, 64, 192), ('x', 'y'), 0, 0, tiled=True)  7.72 us
    unnamed x27, local copies, waits for them, and re-layouts  6.52 us
  transfers between devices with their start and end apart: 16, of which 5 were waited for; matrix products, arithmetic and copies ran while one was open for 1% of the time, Pallas kernels for 4%

profile of v3, /device:TPU:1, one launch (start us, length us, event | category | flops | bytes accessed | tf_op | source)
XLA Modules:
  0.0 150.4 jit_solution(13704725331123100371)
XLA Ops:
  0.6 0.8 copy-done.1
  1.4 0.8 copy-done.2
  2.2 0.9 shard_map.119
  3.1 7.7 %all-to-all-start = ((bf16[16,64,192]{2,1,0:T(8,128)(2,1)}), bf16[16,64,192]{2,1,0:T(8,128)(2,1)S(1)}, u32[]{:S(2)}, u32[]{:S(2)}) async-start(bf16[16,64,192]{2,1,0:T(8,128)(2,1)} %bitcast.4), calls=%async_computation | async-start | bytes 1048576 | tf_op jit(solution)/shard_map/all_to_all | solution.py:149
  10.9 0.0 copy-start.10
  10.9 0.0 copy-start.3
  10.9 0.0 copy-start.4
  10.9 0.1 copy.18.x_scale_ref
  11.0 0.5 copy-done.10
  11.6 0.1 copy.16
  11.6 0.6 copy-done.11
  12.2 0.1 copy.17
  12.3 0.3 shard_map.120
  12.6 3.3 %collective-permute-start.1 = (bf16[192,1024]{1,0:T(8,128)(2,1)S(1)}, bf16[192,1024]{1,0:T(8,128)(2,1)S(1)}, u32[]{:S(2)}, u32[]{:S(2)}) collective-permute-start(bf16[192,1024]{1,0:T(8,128)(2,1)S(1)} %get-tuple-element.27.x0), channel_id=1, source_target_pairs={{0,8},{8,16},{16,24},{24,0},{1,9},{9,17},{17,25},{25,1},{2,10},{10... | collective-permute-start | bytes 1179656 | tf_op jit(solution)/shard_map/ppermute | solution.py:37
  15.9 4.3 %collective-permute-start.2 = (bf16[192,1024]{1,0:T(8,128)(2,1)S(1)}, bf16[192,1024]{1,0:T(8,128)(2,1)S(1)}, u32[]{:S(2)}, u32[]{:S(2)}) collective-permute-start(bf16[192,1024]{1,0:T(8,128)(2,1)S(1)} %get-tuple-element.27.x0), channel_id=1, source_target_pairs={{0,16},{8,24},{16,0},{24,8},{1,17},{9,25},{17,1},{25,9},{2,18},{10... | collective-permute-start | bytes 1179656 | tf_op jit(solution)/shard_map/ppermute | solution.py:37
  20.2 3.1 %collective-permute-start.3 = (bf16[192,1024]{1,0:T(8,128)(2,1)S(1)}, bf16[192,1024]{1,0:T(8,128)(2,1)}, u32[]{:S(2)}, u32[]{:S(2)}) collective-permute-start(bf16[192,1024]{1,0:T(8,128)(2,1)S(1)} %get-tuple-element.27.x0), channel_id=1, source_target_pairs={{0,24},{8,0},{16,8},{24,16},{1,25},{9,1},{17,9},{25,17},{2,26},{10... | collective-permute-start | bytes 1179656 | tf_op jit(solution)/shard_map/ppermute | solution.py:37
  23.3 5.8 %collective-permute-start = (bf16[4,256,192]{2,1,0:T(8,128)(2,1)S(1)}, bf16[4,256,192]{2,1,0:T(8,128)(2,1)S(1)}, u32[]{:S(2)}, u32[]{:S(2)}) collective-permute-start(bf16[4,256,192]{2,1,0:T(8,128)(2,1)S(1)} %bitcast.16), channel_id=1, source_target_pairs={{0,1},{1,0},{2,3},{3,2},{4,5},{5,4},{6,7},{7,6},{8,9},{9,8},{10,11... | collective-permute-start | bytes 1179656 | tf_op jit(solution)/shard_map/ppermute | solution.py:151
  29.2 0.1 pad_add_fusion.place
  29.2 0.7 broadcast_in_dim.4
  30.0 13.0 %all-to-all-start.2 = ((bf16[4,32,1024]{2,1,0:T(8,128)(2,1)}), bf16[4,32,1024]{2,1,0:T(8,128)(2,1)S(1)}, u32[]{:S(2)}, u32[]{:S(2)}) async-start(bf16[4,32,1024]{2,1,0:T(8,128)(2,1)} %broadcast_in_dim.4), calls=%async_computation.2 | async-start | bytes 524288 | tf_op jit(solution)/shard_map/all_to_all | solution.py:43
  42.9 0.0 collective-permute-done.1.x1
  42.9 0.7 copy-done.5
  43.7 0.8 copy-done.7
  44.5 1.0 copy-done.6
  45.5 1.0 copy-done.8
  46.5 2.9 %shard_map.121 = (f32[4,2,32,1024]{3,2,1,0:T(8,128)S(1)}, bf16[4,2,16,1024]{3,2,1,0:T(8,128)(2,1)}, bf16[4,2,16,1024]{3,2,1,0:T(8,128)(2,1)}) custom-call(s32[4]{0:T(128)S(1)} %pad_add_fusion.place, bf16[4,256,192]{2,1,0:T(8,128)(2,1)S(1)} %bitcast.17, bf16[4,256,192]{2,1,0:T(8,128)(2,1)S(1)} %collective-permute-done.twin, ...), custom_call_target="tpu_custom_call" | custom-call | flops 99999997952 | tf_op jit(solution)/shard_map/pallas_call | solution.py:161
  49.4 5.9 %collective-permute-start.4 = (bf16[4,2,16,1024]{3,2,1,0:T(8,128)(2,1)}, bf16[4,2,16,1024]{3,2,1,0:T(8,128)(2,1)S(1)}, u32[]{:S(2)}, u32[]{:S(2)}) collective-permute-start(bf16[4,2,16,1024]{3,2,1,0:T(8,128)(2,1)} %get-tuple-element.29), channel_id=1, source_target_pairs={{0,480},{32,0},{64,32},{96,64},{128,96},{160,128},{192,160},{224,1... | collective-permute-start | bytes 786440 | tf_op jit(solution)/shard_map/ppermute | solution.py:37
  55.3 1.9 %collective-permute-start.5 = (bf16[4,2,16,1024]{3,2,1,0:T(8,128)(2,1)}, bf16[4,2,16,1024]{3,2,1,0:T(8,128)(2,1)S(1)}, u32[]{:S(2)}, u32[]{:S(2)}) collective-permute-start(bf16[4,2,16,1024]{3,2,1,0:T(8,128)(2,1)} %get-tuple-element.30), channel_id=1, source_target_pairs={{0,32},{32,64},{64,96},{96,128},{128,160},{160,192},{192,224},{224... | collective-permute-start | bytes 786440 | tf_op jit(solution)/shard_map/ppermute | solution.py:37
  57.2 0.4 all-to-all-done.2.w0
  57.6 7.2 %collective-permute-start.6 = (bf16[4,32,1024]{2,1,0:T(8,128)(2,1)S(1)}, bf16[4,32,1024]{2,1,0:T(8,128)(2,1)S(1)}, u32[]{:S(2)}, u32[]{:S(2)}) collective-permute-start(bf16[4,32,1024]{2,1,0:T(8,128)(2,1)S(1)} %all-to-all-done.2.w0), channel_id=1, source_target_pairs={{0,32},{32,64},{64,96},{96,128},{128,160},{160,192},{192,224},{224... | collective-permute-start | bytes 786440 | tf_op jit(solution)/shard_map/ppermute | solution.py:37
  64.8 3.2 %collective-permute-start.7 = (bf16[4,32,1024]{2,1,0:T(8,128)(2,1)S(1)}, bf16[4,32,1024]{2,1,0:T(8,128)(2,1)S(1)}, u32[]{:S(2)}, u32[]{:S(2)}) collective-permute-start(bf16[4,32,1024]{2,1,0:T(8,128)(2,1)S(1)} %all-to-all-done.2.w0), channel_id=1, source_target_pairs={{0,448},{32,480},{64,0},{96,32},{128,64},{160,96},{192,128},{224,1... | collective-permute-start | bytes 786440 | tf_op jit(solution)/shard_map/ppermute | solution.py:37
  68.0 3.4 %collective-permute-start.8 = (bf16[4,32,1024]{2,1,0:T(8,128)(2,1)S(1)}, bf16[4,32,1024]{2,1,0:T(8,128)(2,1)}, u32[]{:S(2)}, u32[]{:S(2)}) collective-permute-start(bf16[4,32,1024]{2,1,0:T(8,128)(2,1)S(1)} %all-to-all-done.2.w0), channel_id=1, source_target_pairs={{0,480},{32,0},{64,32},{96,64},{128,96},{160,128},{192,160},{224,1... | collective-permute-start | bytes 786440 | tf_op jit(solution)/shard_map/ppermute | solution.py:37
  71.4 0.9 shard_map.122
  72.3 5.6 %all-to-all-start.1 = ((bf16[8,32,1024]{2,1,0:T(8,128)(2,1)}), bf16[8,32,1024]{2,1,0:T(8,128)(2,1)S(1)}, u32[]{:S(2)}, u32[]{:S(2)}) async-start(bf16[8,32,1024]{2,1,0:T(8,128)(2,1)} %shard_map.122), calls=%async_computation.1 | async-start | bytes 1048576 | tf_op jit(solution)/shard_map/all_to_all | solution.py:171
  77.9 6.9 %collective-permute-done.8.w3 = bf16[4,32,1024]{2,1,0:T(8,128)(2,1)} collective-permute-done((bf16[4,32,1024]{2,1,0:T(8,128)(2,1)S(1)}, bf16[4,32,1024]{2,1,0:T(8,128)(2,1)}, u32[]{:S(2)}, u32[]{:S(2)}) %collective-permute-start.8) | collective-permute-done | bytes 262176 | tf_op jit(solution)/shard_map/ppermute | solution.py:37
  84.8 2.0 %shard_map.123 = (f32[192,1024]{1,0:T(8,128)S(1)}, bf16[192,1024]{1,0:T(8,128)(2,1)S(1)}, bf16[96,1024]{1,0:T(8,128)(2,1)S(1)}, bf16[96,1024]{1,0:T(8,128)(2,1)S(1)}, bf16[192,1024]{1,0:T(8,128)(2,1)S(1)}) custom-call(s32[4]{0:T(128)S(1)} %pad_add_fusion.place, bf16[4,256,192]{2,1,0:T(8,128)(2,1)S(1)} %bitcast.18, ...), custom_call_target="tpu_custom_call" | custom-call | flops 99999997952 | tf_op jit(solution)/shard_map/pallas_call | solution.py:174
  86.9 1.9 %collective-permute-start.12 = (bf16[192,1024]{1,0:T(8,128)(2,1)S(1)}, bf16[192,1024]{1,0:T(8,128)(2,1)S(1)}, u32[]{:S(2)}, u32[]{:S(2)}) collective-permute-start(bf16[192,1024]{1,0:T(8,128)(2,1)S(1)} %get-tuple-element.36), channel_id=1, source_target_pairs={{0,24},{8,0},{16,8},{24,16},{1,25},{9,1},{17,9},{25,17},{2,26},{10... | collective-permute-start | bytes 1179656 | tf_op jit(solution)/shard_map/ppermute | solution.py:37
  88.8 3.4 %collective-permute-start.9 = (bf16[192,1024]{1,0:T(8,128)(2,1)S(1)}, bf16[192,1024]{1,0:T(8,128)(2,1)S(1)}, u32[]{:S(2)}, u32[]{:S(2)}) collective-permute-start(bf16[192,1024]{1,0:T(8,128)(2,1)S(1)} %get-tuple-element.33), channel_id=1, source_target_pairs={{0,8},{8,16},{16,24},{24,0},{1,9},{9,17},{17,25},{25,1},{2,10},{10... | collective-permute-start | bytes 1179656 | tf_op jit(solution)/shard_map/ppermute | solution.py:37
  92.2 2.5 %collective-permute-start.10 = (bf16[96,1024]{1,0:T(8,128)(2,1)S(1)}, bf16[96,1024]{1,0:T(8,128)(2,1)S(1)}, u32[]{:S(2)}, u32[]{:S(2)}) collective-permute-start(bf16[96,1024]{1,0:T(8,128)(2,1)S(1)} %get-tuple-element.34), channel_id=1, source_target_pairs={{0,16},{8,24},{16,0},{24,8},{1,17},{9,25},{17,1},{25,9},{2,18},{10... | collective-permute-start | bytes 589832 | tf_op jit(solution)/shard_map/ppermute | solution.py:37
  94.7 4.3 %collective-permute-start.11 = (bf16[96,1024]{1,0:T(8,128)(2,1)S(1)}, bf16[96,1024]{1,0:T(8,128)(2,1)S(1)}, u32[]{:S(2)}, u32[]{:S(2)}) collective-permute-start(bf16[96,1024]{1,0:T(8,128)(2,1)S(1)} %get-tuple-element.35), channel_id=1, source_target_pairs={{0,16},{8,24},{16,0},{24,8},{1,17},{9,25},{17,1},{25,9},{2,18},{10... | collective-permute-start | bytes 589832 | tf_op jit(solution)/shard_map/ppermute | solution.py:37
  99.0 1.5 collective-permute-done.10.r2a
  100.4 2.4 %collective-permute-done.11.r2b = bf16[96,1024]{1,0:T(8,128)(2,1)S(1)} collective-permute-done((bf16[96,1024]{1,0:T(8,128)(2,1)S(1)}, bf16[96,1024]{1,0:T(8,128)(2,1)S(1)}, u32[]{:S(2)}, u32[]{:S(2)}) %collective-permute-start.11) | collective-permute-done | bytes 196640 | tf_op jit(solution)/shard_map/ppermute | solution.py:37
  102.8 8.2 %all-to-all-done.1.far_ref = bf16[8,32,1024]{2,1,0:T(8,128)(2,1)S(1)} async-done(((bf16[8,32,1024]{2,1,0:T(8,128)(2,1)}), bf16[8,32,1024]{2,1,0:T(8,128)(2,1)S(1)}, u32[]{:S(2)}, u32[]{:S(2)}) %all-to-all-start.1) | async-done | bytes 524320 | tf_op jit(solution)/shard_map/all_to_all | solution.py:171
  111.0 0.4 shard_map.124
  111.4 18.1 %all_to_all.32 = f32[64,1,128]{2,1,0:T(1,128)S(1)} all-to-all(f32[64,1,128]{2,1,0:T(1,128)S(1)} %bitcast.23), channel_id=1, replica_groups=mesh['zh'=4,'zm'=2,'zp'=2,'x'=4,'y'=4,'c'=2] {'zh','zm','zp','x'}, dimensions={0} | all-to-all | bytes 65536 | tf_op jit(solution)/shard_map/all_to_all | solution.py:188
  129.5 0.1 reduce_max.9
  129.6 19.9 %all_to_all.33 = f32[8,1,128]{2,1,0:T(1,128)S(1)} all-to-all(f32[8,1,128]{2,1,0:T(1,128)S(1)} %broadcast_in_dim.5), channel_id=1, replica_groups=mesh['zh'=4,'zm'=2,'zp'=2,'x'=4,'y'=4,'c'=2] {'y','c'}, dimensions={0} | all-to-all | bytes 8192 | tf_op jit(solution)/shard_map/all_to_all | solution.py:43
  149.5 1.0 shard_map.125
  (24 shorter events, 0.1 us)
Async XLA Ops:
  0.6 0.8 copy-start.1
  1.4 0.8 copy-start.2
  3.1 7.7 %copy-start.9 = (f32[192,8]{0,1:T(8,128)S(1)}, f32[192,8]{0,1:T(8,128)}, u32[]{:S(2)}) copy-start(f32[192,8]{0,1:T(8,128)} %param.9) | copy-start | bytes 18436
  3.1 9.2 %copy-start = (bf16[192,1024]{1,0:T(8,128)(2,1)S(1)}, bf16[192,1024]{1,0:T(8,128)(2,1)}, u32[]{:S(2)}) copy-start(bf16[192,1024]{1,0:T(8,128)(2,1)} %x_ref.1) | copy-start | bytes 1179652
  3.1 20.2 %all-to-all-start = ((bf16[16,64,192]{2,1,0:T(8,128)(2,1)}), bf16[16,64,192]{2,1,0:T(8,128)(2,1)S(1)}, u32[]{:S(2)}, u32[]{:S(2)}) async-start(bf16[16,64,192]{2,1,0:T(8,128)(2,1)} %bitcast.4), calls=%async_computation | async-start | bytes 1048576 | tf_op jit(solution)/shard_map/all_to_all | solution.py:149
  10.9 0.7 copy-start.10
  10.9 1.4 copy-start.3
  10.9 1.4 copy-start.4
  11.5 0.7 copy-start.11
  12.6 30.3 %collective-permute-start.1 = (bf16[192,1024]{1,0:T(8,128)(2,1)S(1)}, bf16[192,1024]{1,0:T(8,128)(2,1)S(1)}, u32[]{:S(2)}, u32[]{:S(2)}) collective-permute-start(bf16[192,1024]{1,0:T(8,128)(2,1)S(1)} %get-tuple-element.27.x0), channel_id=1, source_target_pairs={{0,8},{8,16},{16,24},{24,0},{1,9},{9,17},{17,25},{25,1},{2,10},{10... | collective-permute-start | bytes 1179656 | tf_op jit(solution)/shard_map/ppermute | solution.py:37
  15.9 27.8 %collective-permute-start.2 = (bf16[192,1024]{1,0:T(8,128)(2,1)S(1)}, bf16[192,1024]{1,0:T(8,128)(2,1)S(1)}, u32[]{:S(2)}, u32[]{:S(2)}) collective-permute-start(bf16[192,1024]{1,0:T(8,128)(2,1)S(1)} %get-tuple-element.27.x0), channel_id=1, source_target_pairs={{0,16},{8,24},{16,0},{24,8},{1,17},{9,25},{17,1},{25,9},{2,18},{10... | collective-permute-start | bytes 1179656 | tf_op jit(solution)/shard_map/ppermute | solution.py:37
  20.2 24.2 %collective-permute-start.3 = (bf16[192,1024]{1,0:T(8,128)(2,1)S(1)}, bf16[192,1024]{1,0:T(8,128)(2,1)}, u32[]{:S(2)}, u32[]{:S(2)}) collective-permute-start(bf16[192,1024]{1,0:T(8,128)(2,1)S(1)} %get-tuple-element.27.x0), channel_id=1, source_target_pairs={{0,24},{8,0},{16,8},{24,16},{1,25},{9,1},{17,9},{25,17},{2,26},{10... | collective-permute-start | bytes 1179656 | tf_op jit(solution)/shard_map/ppermute | solution.py:37
  23.3 21.1 %collective-permute-start = (bf16[4,256,192]{2,1,0:T(8,128)(2,1)S(1)}, bf16[4,256,192]{2,1,0:T(8,128)(2,1)S(1)}, u32[]{:S(2)}, u32[]{:S(2)}) collective-permute-start(bf16[4,256,192]{2,1,0:T(8,128)(2,1)S(1)} %bitcast.16), channel_id=1, source_target_pairs={{0,1},{1,0},{2,3},{3,2},{4,5},{5,4},{6,7},{7,6},{8,9},{9,8},{10,11... | collective-permute-start | bytes 1179656 | tf_op jit(solution)/shard_map/ppermute | solution.py:151
  30.0 27.6 %all-to-all-start.2 = ((bf16[4,32,1024]{2,1,0:T(8,128)(2,1)}), bf16[4,32,1024]{2,1,0:T(8,128)(2,1)S(1)}, u32[]{:S(2)}, u32[]{:S(2)}) async-start(bf16[4,32,1024]{2,1,0:T(8,128)(2,1)} %broadcast_in_dim.4), calls=%async_computation.2 | async-start | bytes 524288 | tf_op jit(solution)/shard_map/all_to_all | solution.py:43
  42.9 0.7 copy-start.5
  43.7 0.8 copy-start.7
  44.5 1.0 copy-start.6
  45.5 1.0 copy-start.8
  49.4 22.0 %collective-permute-start.4 = (bf16[4,2,16,1024]{3,2,1,0:T(8,128)(2,1)}, bf16[4,2,16,1024]{3,2,1,0:T(8,128)(2,1)S(1)}, u32[]{:S(2)}, u32[]{:S(2)}) collective-permute-start(bf16[4,2,16,1024]{3,2,1,0:T(8,128)(2,1)} %get-tuple-element.29), channel_id=1, source_target_pairs={{0,480},{32,0},{64,32},{96,64},{128,96},{160,128},{192,160},{224,1... | collective-permute-start | bytes 786440 | tf_op jit(solution)/shard_map/ppermute | solution.py:37
  55.3 16.1 %collective-permute-start.5 = (bf16[4,2,16,1024]{3,2,1,0:T(8,128)(2,1)}, bf16[4,2,16,1024]{3,2,1,0:T(8,128)(2,1)S(1)}, u32[]{:S(2)}, u32[]{:S(2)}) collective-permute-start(bf16[4,2,16,1024]{3,2,1,0:T(8,128)(2,1)} %get-tuple-element.30), channel_id=1, source_target_pairs={{0,32},{32,64},{64,96},{96,128},{128,160},{160,192},{192,224},{224... | collective-permute-start | bytes 786440 | tf_op jit(solution)/shard_map/ppermute | solution.py:37
  57.6 20.3 %collective-permute-start.6 = (bf16[4,32,1024]{2,1,0:T(8,128)(2,1)S(1)}, bf16[4,32,1024]{2,1,0:T(8,128)(2,1)S(1)}, u32[]{:S(2)}, u32[]{:S(2)}) collective-permute-start(bf16[4,32,1024]{2,1,0:T(8,128)(2,1)S(1)} %all-to-all-done.2.w0), channel_id=1, source_target_pairs={{0,32},{32,64},{64,96},{96,128},{128,160},{160,192},{192,224},{224... | collective-permute-start | bytes 786440 | tf_op jit(solution)/shard_map/ppermute | solution.py:37
  64.8 13.1 %collective-permute-start.7 = (bf16[4,32,1024]{2,1,0:T(8,128)(2,1)S(1)}, bf16[4,32,1024]{2,1,0:T(8,128)(2,1)S(1)}, u32[]{:S(2)}, u32[]{:S(2)}) collective-permute-start(bf16[4,32,1024]{2,1,0:T(8,128)(2,1)S(1)} %all-to-all-done.2.w0), channel_id=1, source_target_pairs={{0,448},{32,480},{64,0},{96,32},{128,64},{160,96},{192,128},{224,1... | collective-permute-start | bytes 786440 | tf_op jit(solution)/shard_map/ppermute | solution.py:37
  68.0 16.8 %collective-permute-start.8 = (bf16[4,32,1024]{2,1,0:T(8,128)(2,1)S(1)}, bf16[4,32,1024]{2,1,0:T(8,128)(2,1)}, u32[]{:S(2)}, u32[]{:S(2)}) collective-permute-start(bf16[4,32,1024]{2,1,0:T(8,128)(2,1)S(1)} %all-to-all-done.2.w0), channel_id=1, source_target_pairs={{0,480},{32,0},{64,32},{96,64},{128,96},{160,128},{192,160},{224,1... | collective-permute-start | bytes 786440 | tf_op jit(solution)/shard_map/ppermute | solution.py:37
  72.3 38.7 %all-to-all-start.1 = ((bf16[8,32,1024]{2,1,0:T(8,128)(2,1)}), bf16[8,32,1024]{2,1,0:T(8,128)(2,1)S(1)}, u32[]{:S(2)}, u32[]{:S(2)}) async-start(bf16[8,32,1024]{2,1,0:T(8,128)(2,1)} %shard_map.122), calls=%async_computation.1 | async-start | bytes 1048576 | tf_op jit(solution)/shard_map/all_to_all | solution.py:171
  86.9 15.9 %collective-permute-start.12 = (bf16[192,1024]{1,0:T(8,128)(2,1)S(1)}, bf16[192,1024]{1,0:T(8,128)(2,1)S(1)}, u32[]{:S(2)}, u32[]{:S(2)}) collective-permute-start(bf16[192,1024]{1,0:T(8,128)(2,1)S(1)} %get-tuple-element.36), channel_id=1, source_target_pairs={{0,24},{8,0},{16,8},{24,16},{1,25},{9,1},{17,9},{25,17},{2,26},{10... | collective-permute-start | bytes 1179656 | tf_op jit(solution)/shard_map/ppermute | solution.py:37
  88.8 14.0 %collective-permute-start.9 = (bf16[192,1024]{1,0:T(8,128)(2,1)S(1)}, bf16[192,1024]{1,0:T(8,128)(2,1)S(1)}, u32[]{:S(2)}, u32[]{:S(2)}) collective-permute-start(bf16[192,1024]{1,0:T(8,128)(2,1)S(1)} %get-tuple-element.33), channel_id=1, source_target_pairs={{0,8},{8,16},{16,24},{24,0},{1,9},{9,17},{17,25},{25,1},{2,10},{10... | collective-permute-start | bytes 1179656 | tf_op jit(solution)/shard_map/ppermute | solution.py:37
  92.2 8.3 %collective-permute-start.10 = (bf16[96,1024]{1,0:T(8,128)(2,1)S(1)}, bf16[96,1024]{1,0:T(8,128)(2,1)S(1)}, u32[]{:S(2)}, u32[]{:S(2)}) collective-permute-start(bf16[96,1024]{1,0:T(8,128)(2,1)S(1)} %get-tuple-element.34), channel_id=1, source_target_pairs={{0,16},{8,24},{16,0},{24,8},{1,17},{9,25},{17,1},{25,9},{2,18},{10... | collective-permute-start | bytes 589832 | tf_op jit(solution)/shard_map/ppermute | solution.py:37
  94.7 8.1 %collective-permute-start.11 = (bf16[96,1024]{1,0:T(8,128)(2,1)S(1)}, bf16[96,1024]{1,0:T(8,128)(2,1)S(1)}, u32[]{:S(2)}, u32[]{:S(2)}) collective-permute-start(bf16[96,1024]{1,0:T(8,128)(2,1)S(1)} %get-tuple-element.35), channel_id=1, source_target_pairs={{0,16},{8,24},{16,0},{24,8},{1,17},{9,25},{17,1},{25,9},{2,18},{10... | collective-permute-start | bytes 589832 | tf_op jit(solution)/shard_map/ppermute | solution.py:37

commit v4 on v3

--- a/solution.py
+++ b/solution.py
@@ -12,6 +12,7 @@
 F32, BF16 = jnp.float32, jnp.bfloat16
 VMEM = pl.BlockSpec(memory_space=pltpu.VMEM)
 SMEM = pl.BlockSpec(memory_space=pltpu.SMEM)
+HBM = pl.BlockSpec(memory_space=pltpu.HBM)
 
 
 def kernel_call(body, out_shape, in_specs, out_specs=None, scratch=(), flops=0):
@@ -37,14 +38,32 @@
     return lax.ppermute(value, axes, [(i, (i + by) % count) for i in range(count)])
 
 
+def shift_by_core(value, by):
+    count = lax.axis_size(RING)
+    pairs = [
+        (z * 2 + core, (z + (by, -by)[core]) % count * 2 + core)
+        for z in range(count)
+        for core in range(2)
+    ]
+    return lax.ppermute(value, (*RING, "c"), pairs)
+
+
 def spread(block, axes):
     count = lax.axis_size(axes)
     copies = jnp.broadcast_to(block[None], (count, *block.shape))
     return lax.all_to_all(copies, axes, 0, 0, tiled=True)
 
 
-def grads_body(key_ref, value_ref, out_ref):
-    key, value = key_ref[...].T, value_ref[...].T
+def grads_body(key_ref, value_ref, out_ref, key, value, sems):
+    copies = [
+        pltpu.make_async_copy(source, target, sems.at[i])
+        for i, (source, target) in enumerate(((key_ref, key), (value_ref, value)))
+    ]
+    for copy in copies:
+        copy.start()
+    for copy in copies:
+        copy.wait()
+    key, value = key[...].T, value[...].T
     for x in range(4):
         rows = []
         for zz in range(2):
@@ -60,9 +79,9 @@
         at = slice(b * BLOCK, (b + 1) * BLOCK)
         out_ref[:, at] = (x_ref[:, at].astype(F32) * x_scale_ref[:, b : b + 1]).astype(BF16)
         for part, ref, scale in ((0, key_ref, key_scale_ref), (1, value_ref, value_scale_ref)):
-            weight_ref[part * 16 : (part + 1) * 16, at] = (
-                ref[:, at].astype(F32) * scale[:, b : b + 1]
-            ).astype(BF16)
+            scaled = (ref[:, at].astype(F32) * scale[:, b : b + 1]).astype(BF16)
+            for copy in range(4):
+                weight_ref[copy, part * 16 : (part + 1) * 16, at] = scaled
 
 
 def weight_body(place, own, twin, x0, x1, x2, x3, keep_ref, key_ref, value_ref, total):
@@ -79,22 +98,19 @@
             value_ref[zh, zm] = total[i, zh, 1 - zp, 16:].astype(BF16)
 
 
-def input_body(place, own, twin, w0, w1, w2, w3, keep_ref, out1, out2a, out2b, out3, weight):
+def input_body(place, own, twin, w0, w1, w2, w3, keep_ref, out1, out2, out3, weight):
     x, zl, core = place[0], place[1] * 2 + place[2], place[3]
     for back, ref in enumerate((w0, w1, w2, w3)):
         group = lax.rem(zl + 4 - back, 4)
         half, zp = lax.rem(group // 2 + core, 2), lax.rem(group, 2)
         for zh in range(4):
             weight[half, zh, zp] = ref[zh]
-    for k, out in enumerate((keep_ref, out1, None, out3)):
+    for k, out in enumerate((keep_ref, out1, out2, out3)):
         member = lax.rem(x + k, 4)
         lhs = jnp.concatenate([own[member].T, twin[member].T], axis=1)
-        value = jnp.dot(lhs, weight[...].reshape(512, 1024), preferred_element_type=F32)
-        if k == 2:
-            out2a[...] = value[:96].astype(BF16)
-            out2b[...] = value[96:].astype(BF16)
-        else:
-            out[...] = value.astype(out.dtype)
+        out[...] = jnp.dot(
+            lhs, weight[...].reshape(512, 1024), preferred_element_type=F32
+        ).astype(out.dtype)
 
 
 def near_body(keep_ref, key_ref, value_ref, out_ref):
@@ -105,17 +121,14 @@
             out_ref[zh * 2 + zm, 16:] = (keep[16:] + value_ref[zh, zm].astype(F32)).astype(BF16)
 
 
-def peak_body(far_ref, keep_ref, r1, r2a, r2b, r3, weight_ref, input_ref, peak_ref):
+def peak_body(far_ref, keep_ref, r1, r2, r3, weight_ref, input_ref, peak_ref):
     weight = far_ref[0].astype(F32)
     for i in range(1, 8):
         weight = weight + far_ref[i].astype(F32)
     weight_ref[...] = weight
-    input_peak = None
-    for at, r2 in ((slice(0, 96), r2a), (slice(96, 192), r2b)):
-        total = keep_ref[at] + r1[at].astype(F32) + r2[...].astype(F32) + r3[at].astype(F32)
-        input_ref[at] = total
-        peak = jnp.max(jnp.abs(total))
-        input_peak = peak if input_peak is None else jnp.maximum(input_peak, peak)
+    total = keep_ref[...] + r1[...].astype(F32) + r2[...].astype(F32) + r3[...].astype(F32)
+    input_ref[...] = total
+    input_peak = jnp.max(jnp.abs(total))
     size = jnp.abs(weight)
     lane = lax.broadcasted_iota(jnp.int32, peak_ref.shape, 1)
     peak_ref[...] = jnp.where(
@@ -144,19 +157,20 @@
     own = kernel_call(
         grads_body,
         shape((4, 4, 64, 192), BF16),
-        [VMEM] * 2,
+        [HBM] * 2,
+        scratch=[pltpu.VMEM((192, 128), BF16)] * 2 + [pltpu.SemaphoreType.DMA((2,))],
     )(grad_key, grad_value)
     own = lax.all_to_all(own.reshape(16, 64, 192), ("x", "y"), 0, 0, tiled=True)
     own = own.reshape(4, 256, 192)
     twin = lax.ppermute(own, "c", [(0, 1), (1, 0)])
 
     inputs, weight = kernel_call(
-        scale_body, (shape((192, 1024), BF16), shape((32, 1024), BF16)), [VMEM] * 6
+        scale_body, (shape((192, 1024), BF16), shape((4, 32, 1024), BF16)), [VMEM] * 6
     )(x_quant, x_scale, key_quant.T, key_scale.T, value_quant.T, value_scale.T)
     others = [shift(inputs, "x", by) for by in (1, 2, 3)]
 
     own, weight = lax.optimization_barrier((own, weight))
-    weight = spread(weight, "zh")
+    weight = lax.all_to_all(weight, "zh", 0, 0, tiled=True)
 
     keep, key, value = kernel_call(
         weight_body,
@@ -166,27 +180,26 @@
         flops=10**11,
     )(place, own, twin, inputs, *others)
     key, value = shift(key, RING, -1), shift(value, RING, 1)
-    weights = [weight] + [shift(weight, RING, by) for by in (1, -2, -1)]
+    weights = [weight, shift(weight, RING, 1), shift_by_core(weight, 2), shift(weight, RING, -1)]
     part = kernel_call(near_body, shape((8, 32, 1024), BF16), [VMEM] * 3)(keep, key, value)
     far = lax.all_to_all(part, ("zh", "zm"), 0, 0, tiled=True)
 
-    block, half = shape((192, 1024), BF16), shape((96, 1024), BF16)
     keep, *parts = kernel_call(
         input_body,
-        (shape((192, 1024), F32), block, half, half, block),
+        (shape((192, 1024), F32),) + (shape((192, 1024), BF16),) * 3,
         [SMEM] + [VMEM] * 6,
         scratch=[pltpu.VMEM((2, 4, 2, 32, 1024), BF16)],
         flops=10**11,
     )(place, own, twin, *weights)
-    parts = [shift(part, "x", by) for part, by in zip(parts, (1, 2, -2, -1))]
+    parts = [shift(part, "x", by) for part, by in zip(parts, (1, 2, 3))]
 
     weight_sum, input_sum, peaks = kernel_call(
         peak_body,
-        (shape((32, 1024), F32), shape((192, 1024), F32), shape((64, 128), F32)),
-        [VMEM] * 6,
+        (shape((32, 1024), F32), shape((192, 1024), F32), shape((32, 128), F32)),
+        [VMEM] * 5,
     )(far, keep, *parts)
-    peaks = lax.all_to_all(peaks, DP, 0, 0, tiled=True)
-    peaks = spread(jnp.max(peaks, axis=0), TENSOR)
+    peaks = lax.all_to_all(peaks, ("x", *TENSOR), 0, 0, tiled=True)
+    peaks = spread(jnp.max(peaks, axis=0), RING)
     grad_input, grad_key_weight, grad_value_weight, pair, one = kernel_call(
         final_body,
         (
@@ -198,7 +211,7 @@
         ),
         [VMEM] * 3,
         (VMEM, VMEM, VMEM, SMEM, SMEM),
-    )(peaks.reshape(8, 128), weight_sum, input_sum)
+    )(peaks.reshape(16, 128), weight_sum, input_sum)
     return (grad_input, grad_key_weight.T, grad_value_weight.T, pair, one)
 
 

time: 152 us -> 140 us (0.921)
  blocking collectives: 38 us -> 29.3 us
  starting transfers between devices: 76.5 us -> 71.9 us
    ppermute x12 -> x10, starting transfers between devices: 44.4 us -> 36.6 us  [shift(): lax.ppermute(value, axes, [(i, (i + by) % count) for i in range(count)])]
    all_to_all x1, blocking collectives: 18.1 us -> 13.3 us  [per_device(): peaks = lax.all_to_all(peaks, ('x', *TENSOR), 0, 0, tiled=True)]
    all_to_all x1, blocking collectives: 19.9 us -> 16 us  [spread(): return lax.all_to_all(copies, axes, 0, 0, tiled=True)]
    ppermute x0 -> x1, starting transfers between devices: none -> 3.22 us  [shift_by_core(): return lax.ppermute(value, (*RING, 'c'), pairs)]
    unnamed x27 -> x31, local copies, waits for them, and re-layouts: 6.52 us -> 8.25 us
    ppermute x12 -> x10, waiting for transfers between devices: 10.7 us -> 12.3 us  [shift(): lax.ppermute(value, axes, [(i, (i + by) % count) for i in range(count)])]
  transfers between devices with their start and end apart: 16 -> 15, of which waited for: 5 -> 5; matrix products, arithmetic and copies ran while one was open for 1% -> 0% of each run, Pallas kernels for 4% -> 5%
where the time goes in v4:
time: 140 us; the launch traced here: 139 us
  starting transfers between devices  71.9 us (51%)
  blocking collectives  29.3 us (21%)
  waiting for transfers between devices  20.1 us (14%)
  Pallas kernels  8.69 us (6%)
  local copies, waits for them, and re-layouts  8.26 us (6%)
    ppermute x10, starting transfers between devices, shift(): lax.ppermute(value, axes, [(i, (i + by) % count) for i in range(count)])  36.6 us
    all_to_all x1, blocking collectives, spread(): return lax.all_to_all(copies, axes, 0, 0, tiled=True)  16 us
    all_to_all x1, blocking collectives, per_device(): peaks = lax.all_to_all(peaks, ('x', *TENSOR), 0, 0, tiled=True)  13.3 us
    all_to_all x1, starting transfers between devices, per_device(): weight = lax.all_to_all(weight, 'zh', 0, 0, tiled=True)  13 us
    ppermute x10, waiting for transfers between devices, shift(): lax.ppermute(value, axes, [(i, (i + by) % count) for i in range(count)])  12.3 us
    unnamed x31, local copies, waits for them, and re-layouts  8.25 us
    all_to_all x1, waiting for transfers between devices, per_device(): far = lax.all_to_all(part, ('zh', 'zm'), 0, 0, tiled=True)  7.74 us
    all_to_all x1, starting transfers between devices, per_device(): own = lax.all_to_all(own.reshape(16, 64, 192), ('x', 'y'), 0, 0, tiled=True)  7.73 us
  transfers between devices with their start and end apart: 15, of which 5 were waited for; matrix products, arithmetic and copies ran while one was open for 0% of the time, Pallas kernels for 5%

profile of v4, /device:TPU:1, one launch (start us, length us, event | category | flops | bytes accessed | tf_op | source)
XLA Modules:
  0.0 139.3 jit_solution(7211954929251226736)
XLA Ops:
  0.6 0.8 copy-done.1
  1.4 0.8 copy-done.2
  2.2 1.0 shard_map.119
  3.2 0.0 copy-start.11
  3.3 0.0 copy-start
  3.3 7.7 %all-to-all-start = ((bf16[16,64,192]{2,1,0:T(8,128)(2,1)}), bf16[16,64,192]{2,1,0:T(8,128)(2,1)S(1)}, u32[]{:S(2)}, u32[]{:S(2)}) async-start(bf16[16,64,192]{2,1,0:T(8,128)(2,1)} %bitcast.4), calls=%async_computation | async-start | bytes 1048576 | tf_op jit(solution)/shard_map/all_to_all | solution.py:163
  11.0 0.0 copy-start.3
  11.0 0.0 copy-start.4
  11.0 0.1 copy.18.x_scale_ref
  11.2 0.5 copy-done.12
  11.7 0.1 copy.16
  11.8 0.6 copy-done.13
  12.4 0.1 copy.17
  12.5 1.0 shard_map.120
  13.5 3.3 %collective-permute-start.1 = (bf16[192,1024]{1,0:T(8,128)(2,1)S(1)}, bf16[192,1024]{1,0:T(8,128)(2,1)S(1)}, u32[]{:S(2)}, u32[]{:S(2)}) collective-permute-start(bf16[192,1024]{1,0:T(8,128)(2,1)S(1)} %get-tuple-element.26.x0), channel_id=1, source_target_pairs={{0,8},{8,16},{16,24},{24,0},{1,9},{9,17},{17,25},{25,1},{2,10},{10... | collective-permute-start | bytes 1179656 | tf_op jit(solution)/shard_map/ppermute | solution.py:38
  16.8 4.3 %collective-permute-start.2 = (bf16[192,1024]{1,0:T(8,128)(2,1)S(1)}, bf16[192,1024]{1,0:T(8,128)(2,1)S(1)}, u32[]{:S(2)}, u32[]{:S(2)}) collective-permute-start(bf16[192,1024]{1,0:T(8,128)(2,1)S(1)} %get-tuple-element.26.x0), channel_id=1, source_target_pairs={{0,16},{8,24},{16,0},{24,8},{1,17},{9,25},{17,1},{25,9},{2,18},{10... | collective-permute-start | bytes 1179656 | tf_op jit(solution)/shard_map/ppermute | solution.py:38
  21.1 3.1 %collective-permute-start.3 = (bf16[192,1024]{1,0:T(8,128)(2,1)S(1)}, bf16[192,1024]{1,0:T(8,128)(2,1)S(1)}, u32[]{:S(2)}, u32[]{:S(2)}) collective-permute-start(bf16[192,1024]{1,0:T(8,128)(2,1)S(1)} %get-tuple-element.26.x0), channel_id=1, source_target_pairs={{0,24},{8,0},{16,8},{24,16},{1,25},{9,1},{17,9},{25,17},{2,26},{10... | collective-permute-start | bytes 1179656 | tf_op jit(solution)/shard_map/ppermute | solution.py:38
  24.2 5.8 %collective-permute-start = (bf16[4,256,192]{2,1,0:T(8,128)(2,1)S(1)}, bf16[4,256,192]{2,1,0:T(8,128)(2,1)S(1)}, u32[]{:S(2)}, u32[]{:S(2)}) collective-permute-start(bf16[4,256,192]{2,1,0:T(8,128)(2,1)S(1)} %bitcast.16), channel_id=1, source_target_pairs={{0,1},{1,0},{2,3},{3,2},{4,5},{5,4},{6,7},{7,6},{8,9},{9,8},{10,11... | collective-permute-start | bytes 1179656 | tf_op jit(solution)/shard_map/ppermute | solution.py:165
  30.0 0.1 pad_add_fusion.place
  30.1 13.0 %all-to-all-start.2 = ((bf16[4,32,1024]{2,1,0:T(8,128)(2,1)}), bf16[4,32,1024]{2,1,0:T(8,128)(2,1)S(1)}, u32[]{:S(2)}, u32[]{:S(2)}) async-start(bf16[4,32,1024]{2,1,0:T(8,128)(2,1)} %get-tuple-element.30), calls=%async_computation.2 | async-start | bytes 524288 | tf_op jit(solution)/shard_map/all_to_all | solution.py:173
  43.1 0.7 copy-done.5
  43.8 0.7 copy-done.7
  44.6 0.8 copy-done.9
  45.3 1.0 copy-done.6
  46.3 1.0 copy-done.8
  47.3 1.0 copy-done.10
  48.3 2.4 %shard_map.121 = (f32[4,2,32,1024]{3,2,1,0:T(8,128)S(1)}, bf16[4,2,16,1024]{3,2,1,0:T(8,128)(2,1)}, bf16[4,2,16,1024]{3,2,1,0:T(8,128)(2,1)}) custom-call(s32[4]{0:T(128)S(1)} %pad_add_fusion.place, bf16[4,256,192]{2,1,0:T(8,128)(2,1)S(1)} %bitcast.17, bf16[4,256,192]{2,1,0:T(8,128)(2,1)S(1)} %collective-permute-done.twin, ...), custom_call_target="tpu_custom_call" | custom-call | flops 99999997952 | tf_op jit(solution)/shard_map/pallas_call | solution.py:175
  50.7 5.9 %collective-permute-start.4 = (bf16[4,2,16,1024]{3,2,1,0:T(8,128)(2,1)}, bf16[4,2,16,1024]{3,2,1,0:T(8,128)(2,1)S(1)}, u32[]{:S(2)}, u32[]{:S(2)}) collective-permute-start(bf16[4,2,16,1024]{3,2,1,0:T(8,128)(2,1)} %get-tuple-element.28), channel_id=1, source_target_pairs={{0,480},{32,0},{64,32},{96,64},{128,96},{160,128},{192,160},{224,1... | collective-permute-start | bytes 786440 | tf_op jit(solution)/shard_map/ppermute | solution.py:38
  56.7 1.9 %collective-permute-start.5 = (bf16[4,2,16,1024]{3,2,1,0:T(8,128)(2,1)}, bf16[4,2,16,1024]{3,2,1,0:T(8,128)(2,1)S(1)}, u32[]{:S(2)}, u32[]{:S(2)}) collective-permute-start(bf16[4,2,16,1024]{3,2,1,0:T(8,128)(2,1)} %get-tuple-element.29), channel_id=1, source_target_pairs={{0,32},{32,64},{64,96},{96,128},{128,160},{160,192},{192,224},{224... | collective-permute-start | bytes 786440 | tf_op jit(solution)/shard_map/ppermute | solution.py:38
  58.6 6.3 %collective-permute-start.6 = (bf16[4,32,1024]{2,1,0:T(8,128)(2,1)S(1)}, bf16[4,32,1024]{2,1,0:T(8,128)(2,1)S(1)}, u32[]{:S(2)}, u32[]{:S(2)}) collective-permute-start(bf16[4,32,1024]{2,1,0:T(8,128)(2,1)S(1)} %all-to-all-done.2.w0), channel_id=1, source_target_pairs={{0,32},{32,64},{64,96},{96,128},{128,160},{160,192},{192,224},{224... | collective-permute-start | bytes 786440 | tf_op jit(solution)/shard_map/ppermute | solution.py:38
  64.9 3.2 %collective-permute-start.7 = (bf16[4,32,1024]{2,1,0:T(8,128)(2,1)S(1)}, bf16[4,32,1024]{2,1,0:T(8,128)(2,1)S(1)}, u32[]{:S(2)}, u32[]{:S(2)}) collective-permute-start(bf16[4,32,1024]{2,1,0:T(8,128)(2,1)S(1)} %all-to-all-done.2.w0), channel_id=1, source_target_pairs={{0,64},{1,449},{32,96},{33,481},{64,128},{65,1},{96,160},{97,33},{... | collective-permute-start | bytes 786440 | tf_op jit(solution)/shard_map/ppermute | solution.py:48
  68.1 3.4 %collective-permute-start.8 = (bf16[4,32,1024]{2,1,0:T(8,128)(2,1)S(1)}, bf16[4,32,1024]{2,1,0:T(8,128)(2,1)}, u32[]{:S(2)}, u32[]{:S(2)}) collective-permute-start(bf16[4,32,1024]{2,1,0:T(8,128)(2,1)S(1)} %all-to-all-done.2.w0), channel_id=1, source_target_pairs={{0,480},{32,0},{64,32},{96,64},{128,96},{160,128},{192,160},{224,1... | collective-permute-start | bytes 786440 | tf_op jit(solution)/shard_map/ppermute | solution.py:38
  71.5 0.9 shard_map.122
  72.4 5.6 %all-to-all-start.1 = ((bf16[8,32,1024]{2,1,0:T(8,128)(2,1)}), bf16[8,32,1024]{2,1,0:T(8,128)(2,1)S(1)}, u32[]{:S(2)}, u32[]{:S(2)}) async-start(bf16[8,32,1024]{2,1,0:T(8,128)(2,1)} %shard_map.122), calls=%async_computation.1 | async-start | bytes 1048576 | tf_op jit(solution)/shard_map/all_to_all | solution.py:185
  78.1 1.6 %collective-permute-done.8.w3 = bf16[4,32,1024]{2,1,0:T(8,128)(2,1)} collective-permute-done((bf16[4,32,1024]{2,1,0:T(8,128)(2,1)S(1)}, bf16[4,32,1024]{2,1,0:T(8,128)(2,1)}, u32[]{:S(2)}, u32[]{:S(2)}) %collective-permute-start.8) | collective-permute-done | bytes 262176 | tf_op jit(solution)/shard_map/ppermute | solution.py:38
  79.7 2.0 %shard_map.123 = (f32[192,1024]{1,0:T(8,128)S(1)}, bf16[192,1024]{1,0:T(8,128)(2,1)S(1)}, bf16[192,1024]{1,0:T(8,128)(2,1)S(1)}, bf16[192,1024]{1,0:T(8,128)(2,1)S(1)}) custom-call(s32[4]{0:T(128)S(1)} %pad_add_fusion.place, bf16[4,256,192]{2,1,0:T(8,128)(2,1)S(1)} %bitcast.18, bf16[4,256,192]{2,1,0:T(8,128)(2,1)S(1)} %collective-permute-done.twin, ...), custom_call_target="tpu_custom_call" | custom-call | flops 99999997952 | tf_op jit(solution)/shard_map/pallas_call | solution.py:187
  81.7 1.9 %collective-permute-start.10 = (bf16[192,1024]{1,0:T(8,128)(2,1)S(1)}, bf16[192,1024]{1,0:T(8,128)(2,1)S(1)}, u32[]{:S(2)}, u32[]{:S(2)}) collective-permute-start(bf16[192,1024]{1,0:T(8,128)(2,1)S(1)} %get-tuple-element.33), channel_id=1, source_target_pairs={{0,16},{8,24},{16,0},{24,8},{1,17},{9,25},{17,1},{25,9},{2,18},{10... | collective-permute-start | bytes 1179656 | tf_op jit(solution)/shard_map/ppermute | solution.py:38
  83.6 4.6 %collective-permute-start.11 = (bf16[192,1024]{1,0:T(8,128)(2,1)S(1)}, bf16[192,1024]{1,0:T(8,128)(2,1)S(1)}, u32[]{:S(2)}, u32[]{:S(2)}) collective-permute-start(bf16[192,1024]{1,0:T(8,128)(2,1)S(1)} %get-tuple-element.34), channel_id=1, source_target_pairs={{0,24},{8,0},{16,8},{24,16},{1,25},{9,1},{17,9},{25,17},{2,26},{10... | collective-permute-start | bytes 1179656 | tf_op jit(solution)/shard_map/ppermute | solution.py:38
  88.2 1.9 %collective-permute-start.9 = (bf16[192,1024]{1,0:T(8,128)(2,1)S(1)}, bf16[192,1024]{1,0:T(8,128)(2,1)S(1)}, u32[]{:S(2)}, u32[]{:S(2)}) collective-permute-start(bf16[192,1024]{1,0:T(8,128)(2,1)S(1)} %get-tuple-element.32), channel_id=1, source_target_pairs={{0,8},{8,16},{16,24},{24,0},{1,9},{9,17},{17,25},{25,1},{2,10},{10... | collective-permute-start | bytes 1179656 | tf_op jit(solution)/shard_map/ppermute | solution.py:38
  90.2 3.0 %collective-permute-done.10.r2 = bf16[192,1024]{1,0:T(8,128)(2,1)S(1)} collective-permute-done((bf16[192,1024]{1,0:T(8,128)(2,1)S(1)}, bf16[192,1024]{1,0:T(8,128)(2,1)S(1)}, u32[]{:S(2)}, u32[]{:S(2)}) %collective-permute-start.10) | collective-permute-done | bytes 393248 | tf_op jit(solution)/shard_map/ppermute | solution.py:38
  93.2 0.4 collective-permute-done.11.r3
  93.6 7.3 %collective-permute-done.9.r1 = bf16[192,1024]{1,0:T(8,128)(2,1)S(1)} collective-permute-done((bf16[192,1024]{1,0:T(8,128)(2,1)S(1)}, bf16[192,1024]{1,0:T(8,128)(2,1)S(1)}, u32[]{:S(2)}, u32[]{:S(2)}) %collective-permute-start.9) | collective-permute-done | bytes 393248 | tf_op jit(solution)/shard_map/ppermute | solution.py:38
  100.9 7.7 %all-to-all-done.1.far_ref = bf16[8,32,1024]{2,1,0:T(8,128)(2,1)S(1)} async-done(((bf16[8,32,1024]{2,1,0:T(8,128)(2,1)}), bf16[8,32,1024]{2,1,0:T(8,128)(2,1)S(1)}, u32[]{:S(2)}, u32[]{:S(2)}) %all-to-all-start.1) | async-done | bytes 524320 | tf_op jit(solution)/shard_map/all_to_all | solution.py:185
  108.6 0.4 shard_map.124
  109.0 13.3 %all_to_all.32 = f32[32,1,128]{2,1,0:T(1,128)S(1)} all-to-all(f32[32,1,128]{2,1,0:T(1,128)S(1)} %bitcast.24), channel_id=1, replica_groups=mesh['zh'=4,'zm'=2,'zp'=2,'x'=4,'y'=4,'c'=2] {'x','y','c'}, dimensions={0} | all-to-all | bytes 32768 | tf_op jit(solution)/shard_map/all_to_all | solution.py:201
  122.3 0.1 reduce_max.9
  122.4 16.0 %all_to_all.33 = f32[16,1,128]{2,1,0:T(1,128)S(1)} all-to-all(f32[16,1,128]{2,1,0:T(1,128)S(1)} %broadcast_in_dim.2), channel_id=1, replica_groups=mesh['zh'=4,'zm'=2,'zp'=2,'x'=4,'y'=4,'c'=2] {'zh','zm','zp'}, dimensions={0} | all-to-all | bytes 16384 | tf_op jit(solution)/shard_map/all_to_all | solution.py:54
  138.4 1.0 shard_map.125
  (25 shorter events, 0.1 us)
Async XLA Ops:
  0.6 0.8 copy-start.1
  1.4 0.8 copy-start.2
  3.2 7.8 %copy-start.11 = (f32[192,8]{0,1:T(8,128)S(1)}, f32[192,8]{0,1:T(8,128)}, u32[]{:S(2)}) copy-start(f32[192,8]{0,1:T(8,128)} %param.9) | copy-start | bytes 18436
  3.3 9.2 %copy-start = (bf16[192,1024]{1,0:T(8,128)(2,1)S(1)}, bf16[192,1024]{1,0:T(8,128)(2,1)}, u32[]{:S(2)}) copy-start(bf16[192,1024]{1,0:T(8,128)(2,1)} %x_ref.1) | copy-start | bytes 1179652
  3.3 20.9 %all-to-all-start = ((bf16[16,64,192]{2,1,0:T(8,128)(2,1)}), bf16[16,64,192]{2,1,0:T(8,128)(2,1)S(1)}, u32[]{:S(2)}, u32[]{:S(2)}) async-start(bf16[16,64,192]{2,1,0:T(8,128)(2,1)} %bitcast.4), calls=%async_computation | async-start | bytes 1048576 | tf_op jit(solution)/shard_map/all_to_all | solution.py:163
  11.0 0.7 copy-start.12
  11.0 1.4 %copy-start.3 = (bf16[1024,16]{0,1:T(8,128)(2,1)S(1)}, bf16[1024,16]{0,1:T(8,128)(2,1)}, u32[]{:S(2)}) copy-start(bf16[1024,16]{0,1:T(8,128)(2,1)} %param.10) | copy-start | bytes 98308
  11.0 1.4 %copy-start.4 = (bf16[1024,16]{0,1:T(8,128)(2,1)S(1)}, bf16[1024,16]{0,1:T(8,128)(2,1)}, u32[]{:S(2)}) copy-start(bf16[1024,16]{0,1:T(8,128)(2,1)} %param.12) | copy-start | bytes 98308
  11.7 0.7 copy-start.13
  13.5 29.6 %collective-permute-start.1 = (bf16[192,1024]{1,0:T(8,128)(2,1)S(1)}, bf16[192,1024]{1,0:T(8,128)(2,1)S(1)}, u32[]{:S(2)}, u32[]{:S(2)}) collective-permute-start(bf16[192,1024]{1,0:T(8,128)(2,1)S(1)} %get-tuple-element.26.x0), channel_id=1, source_target_pairs={{0,8},{8,16},{16,24},{24,0},{1,9},{9,17},{17,25},{25,1},{2,10},{10... | collective-permute-start | bytes 1179656 | tf_op jit(solution)/shard_map/ppermute | solution.py:38
  16.8 27.1 %collective-permute-start.2 = (bf16[192,1024]{1,0:T(8,128)(2,1)S(1)}, bf16[192,1024]{1,0:T(8,128)(2,1)S(1)}, u32[]{:S(2)}, u32[]{:S(2)}) collective-permute-start(bf16[192,1024]{1,0:T(8,128)(2,1)S(1)} %get-tuple-element.26.x0), channel_id=1, source_target_pairs={{0,16},{8,24},{16,0},{24,8},{1,17},{9,25},{17,1},{25,9},{2,18},{10... | collective-permute-start | bytes 1179656 | tf_op jit(solution)/shard_map/ppermute | solution.py:38
  21.1 23.5 %collective-permute-start.3 = (bf16[192,1024]{1,0:T(8,128)(2,1)S(1)}, bf16[192,1024]{1,0:T(8,128)(2,1)S(1)}, u32[]{:S(2)}, u32[]{:S(2)}) collective-permute-start(bf16[192,1024]{1,0:T(8,128)(2,1)S(1)} %get-tuple-element.26.x0), channel_id=1, source_target_pairs={{0,24},{8,0},{16,8},{24,16},{1,25},{9,1},{17,9},{25,17},{2,26},{10... | collective-permute-start | bytes 1179656 | tf_op jit(solution)/shard_map/ppermute | solution.py:38
  24.2 21.1 %collective-permute-start = (bf16[4,256,192]{2,1,0:T(8,128)(2,1)S(1)}, bf16[4,256,192]{2,1,0:T(8,128)(2,1)S(1)}, u32[]{:S(2)}, u32[]{:S(2)}) collective-permute-start(bf16[4,256,192]{2,1,0:T(8,128)(2,1)S(1)} %bitcast.16), channel_id=1, source_target_pairs={{0,1},{1,0},{2,3},{3,2},{4,5},{5,4},{6,7},{7,6},{8,9},{9,8},{10,11... | collective-permute-start | bytes 1179656 | tf_op jit(solution)/shard_map/ppermute | solution.py:165
  30.1 28.5 %all-to-all-start.2 = ((bf16[4,32,1024]{2,1,0:T(8,128)(2,1)}), bf16[4,32,1024]{2,1,0:T(8,128)(2,1)S(1)}, u32[]{:S(2)}, u32[]{:S(2)}) async-start(bf16[4,32,1024]{2,1,0:T(8,128)(2,1)} %get-tuple-element.30), calls=%async_computation.2 | async-start | bytes 524288 | tf_op jit(solution)/shard_map/all_to_all | solution.py:173
  43.1 0.7 copy-start.5
  43.8 0.7 copy-start.7
  44.6 0.8 copy-start.9
  45.3 1.0 copy-start.6
  46.3 1.0 copy-start.8
  47.3 1.0 copy-start.10
  50.7 20.8 %collective-permute-start.4 = (bf16[4,2,16,1024]{3,2,1,0:T(8,128)(2,1)}, bf16[4,2,16,1024]{3,2,1,0:T(8,128)(2,1)S(1)}, u32[]{:S(2)}, u32[]{:S(2)}) collective-permute-start(bf16[4,2,16,1024]{3,2,1,0:T(8,128)(2,1)} %get-tuple-element.28), channel_id=1, source_target_pairs={{0,480},{32,0},{64,32},{96,64},{128,96},{160,128},{192,160},{224,1... | collective-permute-start | bytes 786440 | tf_op jit(solution)/shard_map/ppermute | solution.py:38
  56.7 14.9 %collective-permute-start.5 = (bf16[4,2,16,1024]{3,2,1,0:T(8,128)(2,1)}, bf16[4,2,16,1024]{3,2,1,0:T(8,128)(2,1)S(1)}, u32[]{:S(2)}, u32[]{:S(2)}) collective-permute-start(bf16[4,2,16,1024]{3,2,1,0:T(8,128)(2,1)} %get-tuple-element.29), channel_id=1, source_target_pairs={{0,32},{32,64},{64,96},{96,128},{128,160},{160,192},{192,224},{224... | collective-permute-start | bytes 786440 | tf_op jit(solution)/shard_map/ppermute | solution.py:38
  58.6 19.4 %collective-permute-start.6 = (bf16[4,32,1024]{2,1,0:T(8,128)(2,1)S(1)}, bf16[4,32,1024]{2,1,0:T(8,128)(2,1)S(1)}, u32[]{:S(2)}, u32[]{:S(2)}) collective-permute-start(bf16[4,32,1024]{2,1,0:T(8,128)(2,1)S(1)} %all-to-all-done.2.w0), channel_id=1, source_target_pairs={{0,32},{32,64},{64,96},{96,128},{128,160},{160,192},{192,224},{224... | collective-permute-start | bytes 786440 | tf_op jit(solution)/shard_map/ppermute | solution.py:38
  64.9 13.1 %collective-permute-start.7 = (bf16[4,32,1024]{2,1,0:T(8,128)(2,1)S(1)}, bf16[4,32,1024]{2,1,0:T(8,128)(2,1)S(1)}, u32[]{:S(2)}, u32[]{:S(2)}) collective-permute-start(bf16[4,32,1024]{2,1,0:T(8,128)(2,1)S(1)} %all-to-all-done.2.w0), channel_id=1, source_target_pairs={{0,64},{1,449},{32,96},{33,481},{64,128},{65,1},{96,160},{97,33},{... | collective-permute-start | bytes 786440 | tf_op jit(solution)/shard_map/ppermute | solution.py:48
  68.1 11.5 %collective-permute-start.8 = (bf16[4,32,1024]{2,1,0:T(8,128)(2,1)S(1)}, bf16[4,32,1024]{2,1,0:T(8,128)(2,1)}, u32[]{:S(2)}, u32[]{:S(2)}) collective-permute-start(bf16[4,32,1024]{2,1,0:T(8,128)(2,1)S(1)} %all-to-all-done.2.w0), channel_id=1, source_target_pairs={{0,480},{32,0},{64,32},{96,64},{128,96},{160,128},{192,160},{224,1... | collective-permute-start | bytes 786440 | tf_op jit(solution)/shard_map/ppermute | solution.py:38
  72.4 36.2 %all-to-all-start.1 = ((bf16[8,32,1024]{2,1,0:T(8,128)(2,1)}), bf16[8,32,1024]{2,1,0:T(8,128)(2,1)S(1)}, u32[]{:S(2)}, u32[]{:S(2)}) async-start(bf16[8,32,1024]{2,1,0:T(8,128)(2,1)} %shard_map.122), calls=%async_computation.1 | async-start | bytes 1048576 | tf_op jit(solution)/shard_map/all_to_all | solution.py:185
  81.7 11.5 %collective-permute-start.10 = (bf16[192,1024]{1,0:T(8,128)(2,1)S(1)}, bf16[192,1024]{1,0:T(8,128)(2,1)S(1)}, u32[]{:S(2)}, u32[]{:S(2)}) collective-permute-start(bf16[192,1024]{1,0:T(8,128)(2,1)S(1)} %get-tuple-element.33), channel_id=1, source_target_pairs={{0,16},{8,24},{16,0},{24,8},{1,17},{9,25},{17,1},{25,9},{2,18},{10... | collective-permute-start | bytes 1179656 | tf_op jit(solution)/shard_map/ppermute | solution.py:38
  83.6 9.9 %collective-permute-start.11 = (bf16[192,1024]{1,0:T(8,128)(2,1)S(1)}, bf16[192,1024]{1,0:T(8,128)(2,1)S(1)}, u32[]{:S(2)}, u32[]{:S(2)}) collective-permute-start(bf16[192,1024]{1,0:T(8,128)(2,1)S(1)} %get-tuple-element.34), channel_id=1, source_target_pairs={{0,24},{8,0},{16,8},{24,16},{1,25},{9,1},{17,9},{25,17},{2,26},{10... | collective-permute-start | bytes 1179656 | tf_op jit(solution)/shard_map/ppermute | solution.py:38
  88.2 12.7 %collective-permute-start.9 = (bf16[192,1024]{1,0:T(8,128)(2,1)S(1)}, bf16[192,1024]{1,0:T(8,128)(2,1)S(1)}, u32[]{:S(2)}, u32[]{:S(2)}) collective-permute-start(bf16[192,1024]{1,0:T(8,128)(2,1)S(1)} %get-tuple-element.32), channel_id=1, source_target_pairs={{0,8},{8,16},{16,24},{24,0},{1,9},{9,17},{17,25},{25,1},{2,10},{10... | collective-permute-start | bytes 1179656 | tf_op jit(solution)/shard_map/ppermute | solution.py:38

commit v5 on v4

--- a/solution.py
+++ b/solution.py
@@ -15,7 +15,7 @@
 HBM = pl.BlockSpec(memory_space=pltpu.HBM)
 
 
-def kernel_call(body, out_shape, in_specs, out_specs=None, scratch=(), flops=0):
+def kernel_call(body, out_shape, in_specs, out_specs=None, scratch=(), flops=0, mib=16):
     if out_specs is None:
         out_specs = jax.tree.map(lambda _: VMEM, out_shape)
     return pl.pallas_call(
@@ -25,7 +25,7 @@
         out_specs=out_specs,
         scratch_shapes=list(scratch),
         cost_estimate=pl.CostEstimate(flops=flops, bytes_accessed=0, transcendentals=0),
-        compiler_params=pltpu.CompilerParams(vmem_limit_bytes=16 * 2**20),
+        compiler_params=pltpu.CompilerParams(vmem_limit_bytes=mib * 2**20),
     )
 
 
@@ -38,14 +38,14 @@
     return lax.ppermute(value, axes, [(i, (i + by) % count) for i in range(count)])
 
 
-def shift_by_core(value, by):
-    count = lax.axis_size(RING)
+def shift_by_core(value, axes, by):
+    count = lax.axis_size(axes)
     pairs = [
-        (z * 2 + core, (z + (by, -by)[core]) % count * 2 + core)
-        for z in range(count)
+        (i * 2 + core, (i + (by, -by)[core]) % count * 2 + core)
+        for i in range(count)
         for core in range(2)
     ]
-    return lax.ppermute(value, (*RING, "c"), pairs)
+    return lax.ppermute(value, (*axes, "c"), pairs)
 
 
 def spread(block, axes):
@@ -75,20 +75,23 @@
 
 
 def scale_body(x_ref, x_scale_ref, key_ref, key_scale_ref, value_ref, value_scale_ref, out_ref, weight_ref):
+    x_scale = x_scale_ref[...].T
+    scales = (key_scale_ref[...].T, value_scale_ref[...].T)
     for b in range(8):
         at = slice(b * BLOCK, (b + 1) * BLOCK)
-        out_ref[:, at] = (x_ref[:, at].astype(F32) * x_scale_ref[:, b : b + 1]).astype(BF16)
-        for part, ref, scale in ((0, key_ref, key_scale_ref), (1, value_ref, value_scale_ref)):
-            scaled = (ref[:, at].astype(F32) * scale[:, b : b + 1]).astype(BF16)
+        out_ref[:, at] = (x_ref[:, at].astype(F32) * x_scale[:, b : b + 1]).astype(BF16)
+        for part, ref in enumerate((key_ref, value_ref)):
+            scaled = (ref[:, at].astype(F32) * scales[part][:, b : b + 1]).astype(BF16)
             for copy in range(4):
                 weight_ref[copy, part * 16 : (part + 1) * 16, at] = scaled
 
 
 def weight_body(place, own, twin, x0, x1, x2, x3, keep_ref, key_ref, value_ref, total):
     x, zp, core = place[0], place[2], place[3]
+    members = [lax.rem(x + k, 4) for k in (0, 3 - 2 * core, 2, 1 + 2 * core)]
     inputs = jnp.concatenate([ref[...] for ref in (x0, x1, x2, x3)], axis=0)
     for i, part in enumerate((own, twin)):
-        lhs = jnp.concatenate([part[lax.rem(x + 4 - back, 4)] for back in range(4)], axis=1)
+        lhs = jnp.concatenate([part[member] for member in members], axis=1)
         value = jnp.dot(lhs, inputs, preferred_element_type=F32)
         total[i] = value.reshape(4, 2, 32, 1024)
         zm = lax.rem(core + i, 2)
@@ -100,12 +103,12 @@
 
 def input_body(place, own, twin, w0, w1, w2, w3, keep_ref, out1, out2, out3, weight):
     x, zl, core = place[0], place[1] * 2 + place[2], place[3]
-    for back, ref in enumerate((w0, w1, w2, w3)):
-        group = lax.rem(zl + 4 - back, 4)
+    for k, ref in ((0, w0), (3 - 2 * core, w1), (2, w2), (1 + 2 * core, w3)):
+        group = lax.rem(zl + k, 4)
         half, zp = lax.rem(group // 2 + core, 2), lax.rem(group, 2)
         for zh in range(4):
             weight[half, zh, zp] = ref[zh]
-    for k, out in enumerate((keep_ref, out1, out2, out3)):
+    for k, out in ((0, keep_ref), (1 + 2 * core, out1), (2, out2), (3 - 2 * core, out3)):
         member = lax.rem(x + k, 4)
         lhs = jnp.concatenate([own[member].T, twin[member].T], axis=1)
         out[...] = jnp.dot(
@@ -159,6 +162,7 @@
         shape((4, 4, 64, 192), BF16),
         [HBM] * 2,
         scratch=[pltpu.VMEM((192, 128), BF16)] * 2 + [pltpu.SemaphoreType.DMA((2,))],
+        mib=60,
     )(grad_key, grad_value)
     own = lax.all_to_all(own.reshape(16, 64, 192), ("x", "y"), 0, 0, tiled=True)
     own = own.reshape(4, 256, 192)
@@ -166,8 +170,13 @@
 
     inputs, weight = kernel_call(
         scale_body, (shape((192, 1024), BF16), shape((4, 32, 1024), BF16)), [VMEM] * 6
-    )(x_quant, x_scale, key_quant.T, key_scale.T, value_quant.T, value_scale.T)
-    others = [shift(inputs, "x", by) for by in (1, 2, 3)]
+    )(x_quant, x_scale.T, key_quant.T, key_scale, value_quant.T, value_scale)
+    line = ("x",)
+    others = [
+        shift_by_core(inputs, line, 1),
+        shift(inputs, "x", 2),
+        shift_by_core(inputs, line, -1),
+    ]
 
     own, weight = lax.optimization_barrier((own, weight))
     weight = lax.all_to_all(weight, "zh", 0, 0, tiled=True)
@@ -179,19 +188,23 @@
         scratch=[pltpu.VMEM((2, 4, 2, 32, 1024), F32)],
         flops=10**11,
     )(place, own, twin, inputs, *others)
-    key, value = shift(key, RING, -1), shift(value, RING, 1)
-    weights = [weight, shift(weight, RING, 1), shift_by_core(weight, 2), shift(weight, RING, -1)]
+    key, value = shift_by_core(key, RING, -1), shift_by_core(value, RING, 1)
+    weights = [weight] + [shift_by_core(weight, RING, by) for by in (1, 2, -1)]
     part = kernel_call(near_body, shape((8, 32, 1024), BF16), [VMEM] * 3)(keep, key, value)
     far = lax.all_to_all(part, ("zh", "zm"), 0, 0, tiled=True)
 
-    keep, *parts = kernel_call(
+    keep, ahead, across, behind = kernel_call(
         input_body,
         (shape((192, 1024), F32),) + (shape((192, 1024), BF16),) * 3,
         [SMEM] + [VMEM] * 6,
         scratch=[pltpu.VMEM((2, 4, 2, 32, 1024), BF16)],
         flops=10**11,
     )(place, own, twin, *weights)
-    parts = [shift(part, "x", by) for part, by in zip(parts, (1, 2, 3))]
+    parts = [
+        shift_by_core(ahead, line, 1),
+        shift(across, "x", 2),
+        shift_by_core(behind, line, -1),
+    ]
 
     weight_sum, input_sum, peaks = kernel_call(
         peak_body,

time: 140 us -> 139 us (level)
  local copies, waits for them, and re-layouts: 8.26 us -> 5.93 us
  waiting for transfers between devices: 20.1 us -> 18 us
  blocking collectives: 29.3 us -> 31.4 us
    ppermute x10 -> x2, starting transfers between devices: 36.6 us -> 4.4 us  [shift(): lax.ppermute(value, axes, [(i, (i + by) % count) for i in range(count)])]
    ppermute x1 -> x9, starting transfers between devices: 3.22 us -> 34.2 us  [shift_by_core(): return lax.ppermute(value, (*axes, 'c'), pairs)]
    ppermute x1 -> x9, waiting for transfers between devices: 0.01 us -> 12.2 us  [shift_by_core(): return lax.ppermute(value, (*axes, 'c'), pairs)]
    all_to_all x1, waiting for transfers between devices: 7.74 us -> 0.01 us  [per_device(): far = lax.all_to_all(part, ('zh', 'zm'), 0, 0, tiled=True)]
    ppermute x10 -> x2, waiting for transfers between devices: 12.3 us -> 5.73 us  [shift(): lax.ppermute(value, axes, [(i, (i + by) % count) for i in range(count)])]
    unnamed x31 -> x24, local copies, waits for them, and re-layouts: 8.25 us -> 5.92 us
    all_to_all x1, blocking collectives: 16 us -> 18 us  [spread(): return lax.all_to_all(copies, axes, 0, 0, tiled=True)]
  transfers between devices with their start and end apart: 15 -> 15, of which waited for: 5 -> 3; matrix products, arithmetic and copies ran while one was open for 0% -> 0% of each run, Pallas kernels for 5% -> 5%
where the time goes in v5:
time: 139 us; the launch traced here: 138 us
  starting transfers between devices  71.9 us (52%)
  blocking collectives  31.4 us (23%)
  waiting for transfers between devices  18 us (13%)
  Pallas kernels  9.57 us (7%)
  local copies, waits for them, and re-layouts  5.93 us (4%)
    ppermute x9, starting transfers between devices, shift_by_core(): return lax.ppermute(value, (*axes, 'c'), pairs)  34.2 us
    all_to_all x1, blocking collectives, spread(): return lax.all_to_all(copies, axes, 0, 0, tiled=True)  18 us
    all_to_all x1, blocking collectives, per_device(): peaks = lax.all_to_all(peaks, ('x', *TENSOR), 0, 0, tiled=True)  13.4 us
    all_to_all x1, starting transfers between devices, per_device(): weight = lax.all_to_all(weight, 'zh', 0, 0, tiled=True)  13 us
    ppermute x9, waiting for transfers between devices, shift_by_core(): return lax.ppermute(value, (*axes, 'c'), pairs)  12.2 us
    all_to_all x1, starting transfers between devices, per_device(): own = lax.all_to_all(own.reshape(16, 64, 192), ('x', 'y'), 0, 0, tiled=True)  7.73 us
    ppermute x1, starting transfers between devices, per_device(): twin = lax.ppermute(own, 'c', [(0, 1), (1, 0)])  7.03 us
    unnamed x24, local copies, waits for them, and re-layouts  5.92 us
  transfers between devices with their start and end apart: 15, of which 3 were waited for; matrix products, arithmetic and copies ran while one was open for 0% of the time, Pallas kernels for 5%

profile of v5, /device:TPU:1, one launch (start us, length us, event | category | flops | bytes accessed | tf_op | source)
XLA Modules:
  0.0 137.8 jit_solution(12917142844097795768)
XLA Ops:
  0.6 1.7 %shard_map.119 = bf16[4,4,64,192]{3,2,1,0:T(8,128)(2,1)} custom-call(bf16[192,128]{1,0:T(8,128)(2,1)} %key_ref.1, bf16[192,128]{1,0:T(8,128)(2,1)} %value_ref.1), custom_call_target="tpu_custom_call" | custom-call | tf_op jit(solution)/shard_map/pallas_call | solution.py:160
  2.4 0.0 copy-start
  2.4 0.0 copy-start.1
  2.4 0.0 copy-start.2
  2.4 0.0 copy-start.3
  2.4 0.0 copy-start.5
  2.4 7.7 %all-to-all-start = ((bf16[16,64,192]{2,1,0:T(8,128)(2,1)}), bf16[16,64,192]{2,1,0:T(8,128)(2,1)S(1)}, u32[]{:S(2)}, u32[]{:S(2)}) async-start(bf16[16,64,192]{2,1,0:T(8,128)(2,1)} %bitcast.23), calls=%async_computation | async-start | bytes 1048576 | tf_op jit(solution)/shard_map/all_to_all | solution.py:167
  10.2 0.0 copy-start.4
  10.2 0.6 copy-done.4
  10.9 1.1 shard_map.120
  12.0 4.5 %collective-permute-start.1 = (bf16[192,1024]{1,0:T(8,128)(2,1)S(1)}, bf16[192,1024]{1,0:T(8,128)(2,1)S(1)}, u32[]{:S(2)}, u32[]{:S(2)}) collective-permute-start(bf16[192,1024]{1,0:T(8,128)(2,1)S(1)} %get-tuple-element.26.x0), channel_id=1, source_target_pairs={{0,8},{1,25},{8,16},{9,1},{16,24},{17,9},{24,0},{25,17},{2,10},{3,... | collective-permute-start | bytes 1179656 | tf_op jit(solution)/shard_map/ppermute | solution.py:48
  16.5 2.5 %collective-permute-start.2 = (bf16[192,1024]{1,0:T(8,128)(2,1)S(1)}, bf16[192,1024]{1,0:T(8,128)(2,1)S(1)}, u32[]{:S(2)}, u32[]{:S(2)}) collective-permute-start(bf16[192,1024]{1,0:T(8,128)(2,1)S(1)} %get-tuple-element.26.x0), channel_id=1, source_target_pairs={{0,16},{8,24},{16,0},{24,8},{1,17},{9,25},{17,1},{25,9},{2,18},{10... | collective-permute-start | bytes 1179656 | tf_op jit(solution)/shard_map/ppermute | solution.py:38
  19.0 2.5 %collective-permute-start.3 = (bf16[192,1024]{1,0:T(8,128)(2,1)S(1)}, bf16[192,1024]{1,0:T(8,128)(2,1)S(1)}, u32[]{:S(2)}, u32[]{:S(2)}) collective-permute-start(bf16[192,1024]{1,0:T(8,128)(2,1)S(1)} %get-tuple-element.26.x0), channel_id=1, source_target_pairs={{0,24},{1,9},{8,0},{9,17},{16,8},{17,25},{24,16},{25,1},{2,26},{3,... | collective-permute-start | bytes 1179656 | tf_op jit(solution)/shard_map/ppermute | solution.py:48
  21.5 0.0 all-to-all-done
  21.5 7.0 %collective-permute-start = (bf16[4,256,192]{2,1,0:T(8,128)(2,1)S(1)}, bf16[4,256,192]{2,1,0:T(8,128)(2,1)S(1)}, u32[]{:S(2)}, u32[]{:S(2)}) collective-permute-start(bf16[4,256,192]{2,1,0:T(8,128)(2,1)S(1)} %bitcast.15), channel_id=1, source_target_pairs={{0,1},{1,0},{2,3},{3,2},{4,5},{5,4},{6,7},{7,6},{8,9},{9,8},{10,11... | collective-permute-start | bytes 1179656 | tf_op jit(solution)/shard_map/ppermute | solution.py:169
  28.5 0.1 pad_add_fusion.place
  28.6 13.0 %all-to-all-start.2 = ((bf16[4,32,1024]{2,1,0:T(8,128)(2,1)}), bf16[4,32,1024]{2,1,0:T(8,128)(2,1)S(1)}, u32[]{:S(2)}, u32[]{:S(2)}) async-start(bf16[4,32,1024]{2,1,0:T(8,128)(2,1)} %get-tuple-element.30), calls=%async_computation.2 | async-start | bytes 524288 | tf_op jit(solution)/shard_map/all_to_all | solution.py:182
  41.6 0.0 collective-permute-done.1.x1
  41.6 0.7 copy-done.6
  42.3 0.0 collective-permute-done.2.x2
  42.3 0.8 copy-done.8
  43.1 0.0 collective-permute-done.3.x3
  43.1 0.8 copy-done.10
  43.9 0.0 collective-permute-done.twin
  43.9 1.0 copy-done.7
  44.9 1.0 copy-done.9
  45.9 1.0 copy-done.11
  46.9 2.4 %shard_map.121 = (f32[4,2,32,1024]{3,2,1,0:T(8,128)S(1)}, bf16[4,2,16,1024]{3,2,1,0:T(8,128)(2,1)}, bf16[4,2,16,1024]{3,2,1,0:T(8,128)(2,1)}) custom-call(s32[4]{0:T(128)S(1)} %pad_add_fusion.place, bf16[4,256,192]{2,1,0:T(8,128)(2,1)S(1)} %bitcast.16, bf16[4,256,192]{2,1,0:T(8,128)(2,1)S(1)} %collective-permute-done.twin, ...), custom_call_target="tpu_custom_call" | custom-call | flops 99999997952 | tf_op jit(solution)/shard_map/pallas_call | solution.py:184
  49.3 2.6 %collective-permute-start.4 = (bf16[4,2,16,1024]{3,2,1,0:T(8,128)(2,1)}, bf16[4,2,16,1024]{3,2,1,0:T(8,128)(2,1)S(1)}, u32[]{:S(2)}, u32[]{:S(2)}) collective-permute-start(bf16[4,2,16,1024]{3,2,1,0:T(8,128)(2,1)} %get-tuple-element.28), channel_id=1, source_target_pairs={{0,480},{1,33},{32,0},{33,65},{64,32},{65,97},{96,64},{97,129},{12... | collective-permute-start | bytes 786440 | tf_op jit(solution)/shard_map/ppermute | solution.py:48
  51.9 5.2 %collective-permute-start.5 = (bf16[4,2,16,1024]{3,2,1,0:T(8,128)(2,1)}, bf16[4,2,16,1024]{3,2,1,0:T(8,128)(2,1)S(1)}, u32[]{:S(2)}, u32[]{:S(2)}) collective-permute-start(bf16[4,2,16,1024]{3,2,1,0:T(8,128)(2,1)} %get-tuple-element.29), channel_id=1, source_target_pairs={{0,32},{1,481},{32,64},{33,1},{64,96},{65,33},{96,128},{97,65},{12... | collective-permute-start | bytes 786440 | tf_op jit(solution)/shard_map/ppermute | solution.py:48
  57.1 0.0 all-to-all-done.2.w0
  57.2 3.4 %collective-permute-start.6 = (bf16[4,32,1024]{2,1,0:T(8,128)(2,1)S(1)}, bf16[4,32,1024]{2,1,0:T(8,128)(2,1)S(1)}, u32[]{:S(2)}, u32[]{:S(2)}) collective-permute-start(bf16[4,32,1024]{2,1,0:T(8,128)(2,1)S(1)} %all-to-all-done.2.w0), channel_id=1, source_target_pairs={{0,32},{1,481},{32,64},{33,1},{64,96},{65,33},{96,128},{97,65},{12... | collective-permute-start | bytes 786440 | tf_op jit(solution)/shard_map/ppermute | solution.py:48
  60.5 6.1 %collective-permute-start.7 = (bf16[4,32,1024]{2,1,0:T(8,128)(2,1)S(1)}, bf16[4,32,1024]{2,1,0:T(8,128)(2,1)S(1)}, u32[]{:S(2)}, u32[]{:S(2)}) collective-permute-start(bf16[4,32,1024]{2,1,0:T(8,128)(2,1)S(1)} %all-to-all-done.2.w0), channel_id=1, source_target_pairs={{0,64},{1,449},{32,96},{33,481},{64,128},{65,1},{96,160},{97,33},{... | collective-permute-start | bytes 786440 | tf_op jit(solution)/shard_map/ppermute | solution.py:48
  66.7 3.4 %collective-permute-start.8 = (bf16[4,32,1024]{2,1,0:T(8,128)(2,1)S(1)}, bf16[4,32,1024]{2,1,0:T(8,128)(2,1)}, u32[]{:S(2)}, u32[]{:S(2)}) collective-permute-start(bf16[4,32,1024]{2,1,0:T(8,128)(2,1)S(1)} %all-to-all-done.2.w0), channel_id=1, source_target_pairs={{0,480},{1,33},{32,0},{33,65},{64,32},{65,97},{96,64},{97,129},{12... | collective-permute-start | bytes 786440 | tf_op jit(solution)/shard_map/ppermute | solution.py:48
  70.1 0.9 shard_map.122
  71.0 5.6 %all-to-all-start.1 = ((bf16[8,32,1024]{2,1,0:T(8,128)(2,1)}), bf16[8,32,1024]{2,1,0:T(8,128)(2,1)S(1)}, u32[]{:S(2)}, u32[]{:S(2)}) async-start(bf16[8,32,1024]{2,1,0:T(8,128)(2,1)} %shard_map.122), calls=%async_computation.1 | async-start | bytes 1048576 | tf_op jit(solution)/shard_map/all_to_all | solution.py:194
  76.6 3.5 %collective-permute-done.8.w3 = bf16[4,32,1024]{2,1,0:T(8,128)(2,1)} collective-permute-done((bf16[4,32,1024]{2,1,0:T(8,128)(2,1)S(1)}, bf16[4,32,1024]{2,1,0:T(8,128)(2,1)}, u32[]{:S(2)}, u32[]{:S(2)}) %collective-permute-start.8) | collective-permute-done | bytes 262176 | tf_op jit(solution)/shard_map/ppermute | solution.py:48
  80.1 2.1 %shard_map.123 = (f32[192,1024]{1,0:T(8,128)S(1)}, bf16[192,1024]{1,0:T(8,128)(2,1)S(1)}, bf16[192,1024]{1,0:T(8,128)(2,1)S(1)}, bf16[192,1024]{1,0:T(8,128)(2,1)S(1)}) custom-call(s32[4]{0:T(128)S(1)} %pad_add_fusion.place, bf16[4,256,192]{2,1,0:T(8,128)(2,1)S(1)} %bitcast.17, bf16[4,256,192]{2,1,0:T(8,128)(2,1)S(1)} %collective-permute-done.twin, ...), custom_call_target="tpu_custom_call" | custom-call | flops 99999997952 | tf_op jit(solution)/shard_map/pallas_call | solution.py:196
  82.2 1.9 %collective-permute-start.10 = (bf16[192,1024]{1,0:T(8,128)(2,1)S(1)}, bf16[192,1024]{1,0:T(8,128)(2,1)S(1)}, u32[]{:S(2)}, u32[]{:S(2)}) collective-permute-start(bf16[192,1024]{1,0:T(8,128)(2,1)S(1)} %get-tuple-element.33), channel_id=1, source_target_pairs={{0,16},{8,24},{16,0},{24,8},{1,17},{9,25},{17,1},{25,9},{2,18},{10... | collective-permute-start | bytes 1179656 | tf_op jit(solution)/shard_map/ppermute | solution.py:38
  84.1 2.2 %collective-permute-start.11 = (bf16[192,1024]{1,0:T(8,128)(2,1)S(1)}, bf16[192,1024]{1,0:T(8,128)(2,1)S(1)}, u32[]{:S(2)}, u32[]{:S(2)}) collective-permute-start(bf16[192,1024]{1,0:T(8,128)(2,1)S(1)} %get-tuple-element.34), channel_id=1, source_target_pairs={{0,24},{1,9},{8,0},{9,17},{16,8},{17,25},{24,16},{25,1},{2,26},{3,... | collective-permute-start | bytes 1179656 | tf_op jit(solution)/shard_map/ppermute | solution.py:48
  86.3 4.3 %collective-permute-start.9 = (bf16[192,1024]{1,0:T(8,128)(2,1)S(1)}, bf16[192,1024]{1,0:T(8,128)(2,1)S(1)}, u32[]{:S(2)}, u32[]{:S(2)}) collective-permute-start(bf16[192,1024]{1,0:T(8,128)(2,1)S(1)} %get-tuple-element.32), channel_id=1, source_target_pairs={{0,8},{1,25},{8,16},{9,1},{16,24},{17,9},{24,0},{25,17},{2,10},{3,... | collective-permute-start | bytes 1179656 | tf_op jit(solution)/shard_map/ppermute | solution.py:48
  90.6 5.7 %collective-permute-done.10.r2 = bf16[192,1024]{1,0:T(8,128)(2,1)S(1)} collective-permute-done((bf16[192,1024]{1,0:T(8,128)(2,1)S(1)}, bf16[192,1024]{1,0:T(8,128)(2,1)S(1)}, u32[]{:S(2)}, u32[]{:S(2)}) %collective-permute-start.10) | collective-permute-done | bytes 393248 | tf_op jit(solution)/shard_map/ppermute | solution.py:38
  96.3 8.7 %collective-permute-done.11.r3 = bf16[192,1024]{1,0:T(8,128)(2,1)S(1)} collective-permute-done((bf16[192,1024]{1,0:T(8,128)(2,1)S(1)}, bf16[192,1024]{1,0:T(8,128)(2,1)S(1)}, u32[]{:S(2)}, u32[]{:S(2)}) %collective-permute-start.11) | collective-permute-done | bytes 393248 | tf_op jit(solution)/shard_map/ppermute | solution.py:48
  105.0 0.4 shard_map.124
  105.4 13.4 %all_to_all.32 = f32[32,1,128]{2,1,0:T(1,128)S(1)} all-to-all(f32[32,1,128]{2,1,0:T(1,128)S(1)} %bitcast.21), channel_id=1, replica_groups=mesh['zh'=4,'zm'=2,'zp'=2,'x'=4,'y'=4,'c'=2] {'x','y','c'}, dimensions={0} | all-to-all | bytes 32768 | tf_op jit(solution)/shard_map/all_to_all | solution.py:214
  118.8 0.1 reduce_max.9
  118.9 18.0 %all_to_all.33 = f32[16,1,128]{2,1,0:T(1,128)S(1)} all-to-all(f32[16,1,128]{2,1,0:T(1,128)S(1)} %broadcast_in_dim.2), channel_id=1, replica_groups=mesh['zh'=4,'zm'=2,'zp'=2,'x'=4,'y'=4,'c'=2] {'zh','zm','zp'}, dimensions={0} | all-to-all | bytes 16384 | tf_op jit(solution)/shard_map/all_to_all | solution.py:54
  136.9 1.0 shard_map.125
  (18 shorter events, 0.0 us)
Async XLA Ops:
  2.4 7.8 %copy-start = (bf16[192,1024]{1,0:T(8,128)(2,1)S(1)}, bf16[192,1024]{1,0:T(8,128)(2,1)}, u32[]{:S(2)}) copy-start(bf16[192,1024]{1,0:T(8,128)(2,1)} %x_ref.1) | copy-start | bytes 1179652
  2.4 7.8 %copy-start.1 = (bf16[1024,16]{0,1:T(8,128)(2,1)S(1)}, bf16[1024,16]{0,1:T(8,128)(2,1)}, u32[]{:S(2)}) copy-start(bf16[1024,16]{0,1:T(8,128)(2,1)} %param.10) | copy-start | bytes 98308
  2.4 7.8 %copy-start.2 = (bf16[1024,16]{0,1:T(8,128)(2,1)S(1)}, bf16[1024,16]{0,1:T(8,128)(2,1)}, u32[]{:S(2)}) copy-start(bf16[1024,16]{0,1:T(8,128)(2,1)} %param.12) | copy-start | bytes 98308
  2.4 7.8 %copy-start.3 = (f32[192,8]{0,1:T(8,128)S(1)}, f32[192,8]{0,1:T(8,128)}, u32[]{:S(2)}) copy-start(f32[192,8]{0,1:T(8,128)} %param.9) | copy-start | bytes 18436
  2.4 7.8 %copy-start.5 = (f32[8,16]{1,0:T(8,128)S(1)}, f32[8,16]{1,0:T(8,128)}, u32[]{:S(2)}) copy-start(f32[8,16]{1,0:T(8,128)} %value_scale_ref.1) | copy-start | bytes 1540
  2.4 19.0 %all-to-all-start = ((bf16[16,64,192]{2,1,0:T(8,128)(2,1)}), bf16[16,64,192]{2,1,0:T(8,128)(2,1)S(1)}, u32[]{:S(2)}, u32[]{:S(2)}) async-start(bf16[16,64,192]{2,1,0:T(8,128)(2,1)} %bitcast.23), calls=%async_computation | async-start | bytes 1048576 | tf_op jit(solution)/shard_map/all_to_all | solution.py:167
  10.2 0.7 copy-start.4
  12.0 29.6 %collective-permute-start.1 = (bf16[192,1024]{1,0:T(8,128)(2,1)S(1)}, bf16[192,1024]{1,0:T(8,128)(2,1)S(1)}, u32[]{:S(2)}, u32[]{:S(2)}) collective-permute-start(bf16[192,1024]{1,0:T(8,128)(2,1)S(1)} %get-tuple-element.26.x0), channel_id=1, source_target_pairs={{0,8},{1,25},{8,16},{9,1},{16,24},{17,9},{24,0},{25,17},{2,10},{3,... | collective-permute-start | bytes 1179656 | tf_op jit(solution)/shard_map/ppermute | solution.py:48
  16.5 25.8 %collective-permute-start.2 = (bf16[192,1024]{1,0:T(8,128)(2,1)S(1)}, bf16[192,1024]{1,0:T(8,128)(2,1)S(1)}, u32[]{:S(2)}, u32[]{:S(2)}) collective-permute-start(bf16[192,1024]{1,0:T(8,128)(2,1)S(1)} %get-tuple-element.26.x0), channel_id=1, source_target_pairs={{0,16},{8,24},{16,0},{24,8},{1,17},{9,25},{17,1},{25,9},{2,18},{10... | collective-permute-start | bytes 1179656 | tf_op jit(solution)/shard_map/ppermute | solution.py:38
  19.0 24.1 %collective-permute-start.3 = (bf16[192,1024]{1,0:T(8,128)(2,1)S(1)}, bf16[192,1024]{1,0:T(8,128)(2,1)S(1)}, u32[]{:S(2)}, u32[]{:S(2)}) collective-permute-start(bf16[192,1024]{1,0:T(8,128)(2,1)S(1)} %get-tuple-element.26.x0), channel_id=1, source_target_pairs={{0,24},{1,9},{8,0},{9,17},{16,8},{17,25},{24,16},{25,1},{2,26},{3,... | collective-permute-start | bytes 1179656 | tf_op jit(solution)/shard_map/ppermute | solution.py:48
  21.5 22.4 %collective-permute-start = (bf16[4,256,192]{2,1,0:T(8,128)(2,1)S(1)}, bf16[4,256,192]{2,1,0:T(8,128)(2,1)S(1)}, u32[]{:S(2)}, u32[]{:S(2)}) collective-permute-start(bf16[4,256,192]{2,1,0:T(8,128)(2,1)S(1)} %bitcast.15), channel_id=1, source_target_pairs={{0,1},{1,0},{2,3},{3,2},{4,5},{5,4},{6,7},{7,6},{8,9},{9,8},{10,11... | collective-permute-start | bytes 1179656 | tf_op jit(solution)/shard_map/ppermute | solution.py:169
  28.6 28.5 %all-to-all-start.2 = ((bf16[4,32,1024]{2,1,0:T(8,128)(2,1)}), bf16[4,32,1024]{2,1,0:T(8,128)(2,1)S(1)}, u32[]{:S(2)}, u32[]{:S(2)}) async-start(bf16[4,32,1024]{2,1,0:T(8,128)(2,1)} %get-tuple-element.30), calls=%async_computation.2 | async-start | bytes 524288 | tf_op jit(solution)/shard_map/all_to_all | solution.py:182
  41.6 0.7 copy-start.6
  42.3 0.8 copy-start.8
  43.1 0.8 copy-start.10
  43.9 1.0 copy-start.7
  44.9 1.0 copy-start.9
  45.9 1.0 copy-start.11
  49.3 20.8 %collective-permute-start.4 = (bf16[4,2,16,1024]{3,2,1,0:T(8,128)(2,1)}, bf16[4,2,16,1024]{3,2,1,0:T(8,128)(2,1)S(1)}, u32[]{:S(2)}, u32[]{:S(2)}) collective-permute-start(bf16[4,2,16,1024]{3,2,1,0:T(8,128)(2,1)} %get-tuple-element.28), channel_id=1, source_target_pairs={{0,480},{1,33},{32,0},{33,65},{64,32},{65,97},{96,64},{97,129},{12... | collective-permute-start | bytes 786440 | tf_op jit(solution)/shard_map/ppermute | solution.py:48
  51.9 18.1 %collective-permute-start.5 = (bf16[4,2,16,1024]{3,2,1,0:T(8,128)(2,1)}, bf16[4,2,16,1024]{3,2,1,0:T(8,128)(2,1)S(1)}, u32[]{:S(2)}, u32[]{:S(2)}) collective-permute-start(bf16[4,2,16,1024]{3,2,1,0:T(8,128)(2,1)} %get-tuple-element.29), channel_id=1, source_target_pairs={{0,32},{1,481},{32,64},{33,1},{64,96},{65,33},{96,128},{97,65},{12... | collective-permute-start | bytes 786440 | tf_op jit(solution)/shard_map/ppermute | solution.py:48
  57.2 19.4 %collective-permute-start.6 = (bf16[4,32,1024]{2,1,0:T(8,128)(2,1)S(1)}, bf16[4,32,1024]{2,1,0:T(8,128)(2,1)S(1)}, u32[]{:S(2)}, u32[]{:S(2)}) collective-permute-start(bf16[4,32,1024]{2,1,0:T(8,128)(2,1)S(1)} %all-to-all-done.2.w0), channel_id=1, source_target_pairs={{0,32},{1,481},{32,64},{33,1},{64,96},{65,33},{96,128},{97,65},{12... | collective-permute-start | bytes 786440 | tf_op jit(solution)/shard_map/ppermute | solution.py:48
  60.5 16.1 %collective-permute-start.7 = (bf16[4,32,1024]{2,1,0:T(8,128)(2,1)S(1)}, bf16[4,32,1024]{2,1,0:T(8,128)(2,1)S(1)}, u32[]{:S(2)}, u32[]{:S(2)}) collective-permute-start(bf16[4,32,1024]{2,1,0:T(8,128)(2,1)S(1)} %all-to-all-done.2.w0), channel_id=1, source_target_pairs={{0,64},{1,449},{32,96},{33,481},{64,128},{65,1},{96,160},{97,33},{... | collective-permute-start | bytes 786440 | tf_op jit(solution)/shard_map/ppermute | solution.py:48
  66.7 13.4 %collective-permute-start.8 = (bf16[4,32,1024]{2,1,0:T(8,128)(2,1)S(1)}, bf16[4,32,1024]{2,1,0:T(8,128)(2,1)}, u32[]{:S(2)}, u32[]{:S(2)}) collective-permute-start(bf16[4,32,1024]{2,1,0:T(8,128)(2,1)S(1)} %all-to-all-done.2.w0), channel_id=1, source_target_pairs={{0,480},{1,33},{32,0},{33,65},{64,32},{65,97},{96,64},{97,129},{12... | collective-permute-start | bytes 786440 | tf_op jit(solution)/shard_map/ppermute | solution.py:48
  71.0 34.1 %all-to-all-start.1 = ((bf16[8,32,1024]{2,1,0:T(8,128)(2,1)}), bf16[8,32,1024]{2,1,0:T(8,128)(2,1)S(1)}, u32[]{:S(2)}, u32[]{:S(2)}) async-start(bf16[8,32,1024]{2,1,0:T(8,128)(2,1)} %shard_map.122), calls=%async_computation.1 | async-start | bytes 1048576 | tf_op jit(solution)/shard_map/all_to_all | solution.py:194
  82.2 14.2 %collective-permute-start.10 = (bf16[192,1024]{1,0:T(8,128)(2,1)S(1)}, bf16[192,1024]{1,0:T(8,128)(2,1)S(1)}, u32[]{:S(2)}, u32[]{:S(2)}) collective-permute-start(bf16[192,1024]{1,0:T(8,128)(2,1)S(1)} %get-tuple-element.33), channel_id=1, source_target_pairs={{0,16},{8,24},{16,0},{24,8},{1,17},{9,25},{17,1},{25,9},{2,18},{10... | collective-permute-start | bytes 1179656 | tf_op jit(solution)/shard_map/ppermute | solution.py:38
  84.1 20.9 %collective-permute-start.11 = (bf16[192,1024]{1,0:T(8,128)(2,1)S(1)}, bf16[192,1024]{1,0:T(8,128)(2,1)S(1)}, u32[]{:S(2)}, u32[]{:S(2)}) collective-permute-start(bf16[192,1024]{1,0:T(8,128)(2,1)S(1)} %get-tuple-element.34), channel_id=1, source_target_pairs={{0,24},{1,9},{8,0},{9,17},{16,8},{17,25},{24,16},{25,1},{2,26},{3,... | collective-permute-start | bytes 1179656 | tf_op jit(solution)/shard_map/ppermute | solution.py:48
  86.3 18.7 %collective-permute-start.9 = (bf16[192,1024]{1,0:T(8,128)(2,1)S(1)}, bf16[192,1024]{1,0:T(8,128)(2,1)S(1)}, u32[]{:S(2)}, u32[]{:S(2)}) collective-permute-start(bf16[192,1024]{1,0:T(8,128)(2,1)S(1)} %get-tuple-element.32), channel_id=1, source_target_pairs={{0,8},{1,25},{8,16},{9,1},{16,24},{17,9},{24,0},{25,17},{2,10},{3,... | collective-permute-start | bytes 1179656 | tf_op jit(solution)/shard_map/ppermute | solution.py:48

commit v6 on v5

--- a/solution.py
+++ b/solution.py
@@ -54,16 +54,19 @@
     return lax.all_to_all(copies, axes, 0, 0, tiled=True)
 
 
-def grads_body(key_ref, value_ref, out_ref, key, value, sems):
+def prepare_body(*refs):
+    sources, (grads_ref, out_ref, weight_ref) = refs[:8], refs[8:11]
+    targets, sems = refs[11:19], refs[19]
     copies = [
         pltpu.make_async_copy(source, target, sems.at[i])
-        for i, (source, target) in enumerate(((key_ref, key), (value_ref, value)))
+        for i, (source, target) in enumerate(zip(sources, targets))
     ]
     for copy in copies:
         copy.start()
     for copy in copies:
         copy.wait()
-    key, value = key[...].T, value[...].T
+    grad_key, grad_value, x_ref, x_scale_ref, key_ref, key_scale_ref, value_ref, value_scale_ref = targets
+    key, value = grad_key[...].T, grad_value[...].T
     for x in range(4):
         rows = []
         for zz in range(2):
@@ -71,10 +74,7 @@
             rows += [key[start : start + 16], value[start : start + 16]]
         block = jnp.concatenate(rows, axis=0)
         for copy in range(4):
-            out_ref[x, copy] = block
-
-
-def scale_body(x_ref, x_scale_ref, key_ref, key_scale_ref, value_ref, value_scale_ref, out_ref, weight_ref):
+            grads_ref[x, copy] = block
     x_scale = x_scale_ref[...].T
     scales = (key_scale_ref[...].T, value_scale_ref[...].T)
     for b in range(8):
@@ -157,20 +157,22 @@
 ):
     place = jnp.stack([lax.axis_index(axis) for axis in ("x", "zm", "zp", "c")]).astype(jnp.int32)
 
-    own = kernel_call(
-        grads_body,
-        shape((4, 4, 64, 192), BF16),
-        [HBM] * 2,
-        scratch=[pltpu.VMEM((192, 128), BF16)] * 2 + [pltpu.SemaphoreType.DMA((2,))],
+    operands = (
+        grad_key, grad_value, x_quant, x_scale.T, key_quant.T, key_scale, value_quant.T, value_scale
+    )
+    own, inputs, weight = kernel_call(
+        prepare_body,
+        (shape((4, 4, 64, 192), BF16), shape((192, 1024), BF16), shape((4, 32, 1024), BF16)),
+        [HBM] * 8,
+        scratch=[pltpu.VMEM(operand.shape, operand.dtype) for operand in operands]
+        + [pltpu.SemaphoreType.DMA((8,))],
         mib=60,
-    )(grad_key, grad_value)
+    )(*operands)
+
     own = lax.all_to_all(own.reshape(16, 64, 192), ("x", "y"), 0, 0, tiled=True)
     own = own.reshape(4, 256, 192)
     twin = lax.ppermute(own, "c", [(0, 1), (1, 0)])
 
-    inputs, weight = kernel_call(
-        scale_body, (shape((192, 1024), BF16), shape((4, 32, 1024), BF16)), [VMEM] * 6
-    )(x_quant, x_scale.T, key_quant.T, key_scale, value_quant.T, value_scale)
     line = ("x",)
     others = [
         shift_by_core(inputs, line, 1),

time: 139 us -> 138 us (level)
  starting transfers between devices: 71.9 us -> 73.3 us
    unnamed x24 -> x14, local copies, waits for them, and re-layouts: 5.92 us -> 5.23 us
    pallas_call x2 -> x1, Pallas kernels: 2.88 us -> 2.41 us  [per_device(): kernel_call(prepare_body, (shape((4, 4, 64, 192), BF16), shape((192, 1024...]
  transfers between devices with their start and end apart: 15 -> 15, of which waited for: 3 -> 4; matrix products, arithmetic and copies ran while one was open for 0% -> 0% of each run, Pallas kernels for 5% -> 4%
where the time goes in v6:
time: 138 us; the launch traced here: 137 us
  starting transfers between devices  73.3 us (53%)
  blocking collectives  31.3 us (23%)
  waiting for transfers between devices  16.7 us (12%)
  Pallas kernels  9.1 us (7%)
  local copies, waits for them, and re-layouts  5.24 us (4%)
    ppermute x9, starting transfers between devices, shift_by_core(): return lax.ppermute(value, (*axes, 'c'), pairs)  34.2 us
    all_to_all x1, blocking collectives, spread(): return lax.all_to_all(copies, axes, 0, 0, tiled=True)  17.7 us
    all_to_all x1, blocking collectives, per_device(): peaks = lax.all_to_all(peaks, ('x', *TENSOR), 0, 0, tiled=True)  13.6 us
    all_to_all x1, starting transfers between devices, per_device(): weight = lax.all_to_all(weight, 'zh', 0, 0, tiled=True)  13 us
    ppermute x9, waiting for transfers between devices, shift_by_core(): return lax.ppermute(value, (*axes, 'c'), pairs)  12.2 us
    all_to_all x1, starting transfers between devices, per_device(): own = lax.all_to_all(own.reshape(16, 64, 192), ('x', 'y'), 0, 0, tiled=True)  7.73 us
    ppermute x1, starting transfers between devices, per_device(): twin = lax.ppermute(own, 'c', [(0, 1), (1, 0)])  7.03 us
    ppermute x2, starting transfers between devices, shift(): lax.ppermute(value, axes, [(i, (i + by) % count) for i in range(count)])  5.74 us
  transfers between devices with their start and end apart: 15, of which 4 were waited for; matrix products, arithmetic and copies ran while one was open for 0% of the time, Pallas kernels for 4%

profile of v6, /device:TPU:1, one launch (start us, length us, event | category | flops | bytes accessed | tf_op | source)
XLA Modules:
  0.0 136.6 jit_solution(13492881576821551316)
XLA Ops:
  0.6 2.4 %shard_map.119 = (bf16[4,4,64,192]{3,2,1,0:T(8,128)(2,1)}, bf16[192,1024]{1,0:T(8,128)(2,1)}, bf16[4,32,1024]{2,1,0:T(8,128)(2,1)}) custom-call(bf16[192,128]{1,0:T(8,128)(2,1)} %refs_0_.1, bf16[192,128]{1,0:T(8,128)(2,1)} %refs_1_.1, bf16[192,1024]{1,0:T(8,128)(2,1)} %refs_2_.1, f32[8,192]{1,0:T(8,128)} %bitcast.23, bf16[16,1024]{1,0:T(8,128)(2,1)} %bitcast.21, ...), custom_call_target="tpu_custom_call" | custom-call | tf_op jit(solution)/shard_map/pallas_call | solution.py:163
  3.0 0.0 copy-start
  3.1 7.7 %all-to-all-start = ((bf16[16,64,192]{2,1,0:T(8,128)(2,1)}), bf16[16,64,192]{2,1,0:T(8,128)(2,1)S(1)}, u32[]{:S(2)}, u32[]{:S(2)}) async-start(bf16[16,64,192]{2,1,0:T(8,128)(2,1)} %bitcast.20), calls=%async_computation | async-start | bytes 1048576 | tf_op jit(solution)/shard_map/all_to_all | solution.py:172
  10.8 0.0 copy-done
  10.8 4.5 %collective-permute-start.1 = (bf16[192,1024]{1,0:T(8,128)(2,1)S(1)}, bf16[192,1024]{1,0:T(8,128)(2,1)S(1)}, u32[]{:S(2)}, u32[]{:S(2)}) collective-permute-start(bf16[192,1024]{1,0:T(8,128)(2,1)S(1)} %copy-done), channel_id=1, source_target_pairs={{0,8},{1,25},{8,16},{9,1},{16,24},{17,9},{24,0},{25,17},{2,10},{3,... | collective-permute-start | bytes 1179656 | tf_op jit(solution)/shard_map/ppermute | solution.py:48
  15.3 2.5 %collective-permute-start.2 = (bf16[192,1024]{1,0:T(8,128)(2,1)S(1)}, bf16[192,1024]{1,0:T(8,128)(2,1)S(1)}, u32[]{:S(2)}, u32[]{:S(2)}) collective-permute-start(bf16[192,1024]{1,0:T(8,128)(2,1)S(1)} %copy-done), channel_id=1, source_target_pairs={{0,16},{8,24},{16,0},{24,8},{1,17},{9,25},{17,1},{25,9},{2,18},{10... | collective-permute-start | bytes 1179656 | tf_op jit(solution)/shard_map/ppermute | solution.py:38
  17.8 2.5 %collective-permute-start.3 = (bf16[192,1024]{1,0:T(8,128)(2,1)S(1)}, bf16[192,1024]{1,0:T(8,128)(2,1)S(1)}, u32[]{:S(2)}, u32[]{:S(2)}) collective-permute-start(bf16[192,1024]{1,0:T(8,128)(2,1)S(1)} %copy-done), channel_id=1, source_target_pairs={{0,24},{1,9},{8,0},{9,17},{16,8},{17,25},{24,16},{25,1},{2,26},{3,... | collective-permute-start | bytes 1179656 | tf_op jit(solution)/shard_map/ppermute | solution.py:48
  20.3 0.0 all-to-all-done
  20.3 7.0 %collective-permute-start = (bf16[4,256,192]{2,1,0:T(8,128)(2,1)S(1)}, bf16[4,256,192]{2,1,0:T(8,128)(2,1)S(1)}, u32[]{:S(2)}, u32[]{:S(2)}) collective-permute-start(bf16[4,256,192]{2,1,0:T(8,128)(2,1)S(1)} %bitcast.15), channel_id=1, source_target_pairs={{0,1},{1,0},{2,3},{3,2},{4,5},{5,4},{6,7},{7,6},{8,9},{9,8},{10,11... | collective-permute-start | bytes 1179656 | tf_op jit(solution)/shard_map/ppermute | solution.py:174
  27.3 0.1 pad_add_fusion.place
  27.4 13.0 %all-to-all-start.2 = ((bf16[4,32,1024]{2,1,0:T(8,128)(2,1)}), bf16[4,32,1024]{2,1,0:T(8,128)(2,1)S(1)}, u32[]{:S(2)}, u32[]{:S(2)}) async-start(bf16[4,32,1024]{2,1,0:T(8,128)(2,1)} %get-tuple-element.32), calls=%async_computation.2 | async-start | bytes 524288 | tf_op jit(solution)/shard_map/all_to_all | solution.py:184
  40.4 0.0 collective-permute-done.1.x1
  40.4 0.7 copy-done.1
  41.1 0.0 collective-permute-done.2.x2
  41.1 0.7 copy-done.3
  41.9 0.0 collective-permute-done.3.x3
  41.9 0.7 copy-done.5
  42.6 0.0 collective-permute-done.twin
  42.6 1.0 copy-done.2
  43.6 1.0 copy-done.4
  44.6 1.0 copy-done.6
  45.6 2.4 %shard_map.120 = (f32[4,2,32,1024]{3,2,1,0:T(8,128)S(1)}, bf16[4,2,16,1024]{3,2,1,0:T(8,128)(2,1)}, bf16[4,2,16,1024]{3,2,1,0:T(8,128)(2,1)}) custom-call(s32[4]{0:T(128)S(1)} %pad_add_fusion.place, bf16[4,256,192]{2,1,0:T(8,128)(2,1)S(1)} %bitcast.16, bf16[4,256,192]{2,1,0:T(8,128)(2,1)S(1)} %collective-permute-done.twin, bf16[192,1024]{1,0:T(8,128)(2,1)S(1)} %copy-done, ...), custom_call_target="tpu_custom_call" | custom-call | flops 99999997952 | tf_op jit(solution)/shard_map/pallas_call | solution.py:186
  48.1 2.6 %collective-permute-start.4 = (bf16[4,2,16,1024]{3,2,1,0:T(8,128)(2,1)}, bf16[4,2,16,1024]{3,2,1,0:T(8,128)(2,1)S(1)}, u32[]{:S(2)}, u32[]{:S(2)}) collective-permute-start(bf16[4,2,16,1024]{3,2,1,0:T(8,128)(2,1)} %get-tuple-element.30), channel_id=1, source_target_pairs={{0,480},{1,33},{32,0},{33,65},{64,32},{65,97},{96,64},{97,129},{12... | collective-permute-start | bytes 786440 | tf_op jit(solution)/shard_map/ppermute | solution.py:48
  50.7 5.8 %collective-permute-start.5 = (bf16[4,2,16,1024]{3,2,1,0:T(8,128)(2,1)}, bf16[4,2,16,1024]{3,2,1,0:T(8,128)(2,1)S(1)}, u32[]{:S(2)}, u32[]{:S(2)}) collective-permute-start(bf16[4,2,16,1024]{3,2,1,0:T(8,128)(2,1)} %get-tuple-element.31), channel_id=1, source_target_pairs={{0,32},{1,481},{32,64},{33,1},{64,96},{65,33},{96,128},{97,65},{12... | collective-permute-start | bytes 786440 | tf_op jit(solution)/shard_map/ppermute | solution.py:48
  56.5 0.0 all-to-all-done.2.w0
  56.5 3.4 %collective-permute-start.6 = (bf16[4,32,1024]{2,1,0:T(8,128)(2,1)S(1)}, bf16[4,32,1024]{2,1,0:T(8,128)(2,1)S(1)}, u32[]{:S(2)}, u32[]{:S(2)}) collective-permute-start(bf16[4,32,1024]{2,1,0:T(8,128)(2,1)S(1)} %all-to-all-done.2.w0), channel_id=1, source_target_pairs={{0,32},{1,481},{32,64},{33,1},{64,96},{65,33},{96,128},{97,65},{12... | collective-permute-start | bytes 786440 | tf_op jit(solution)/shard_map/ppermute | solution.py:48
  59.9 5.6 %collective-permute-start.7 = (bf16[4,32,1024]{2,1,0:T(8,128)(2,1)S(1)}, bf16[4,32,1024]{2,1,0:T(8,128)(2,1)S(1)}, u32[]{:S(2)}, u32[]{:S(2)}) collective-permute-start(bf16[4,32,1024]{2,1,0:T(8,128)(2,1)S(1)} %all-to-all-done.2.w0), channel_id=1, source_target_pairs={{0,64},{1,449},{32,96},{33,481},{64,128},{65,1},{96,160},{97,33},{... | collective-permute-start | bytes 786440 | tf_op jit(solution)/shard_map/ppermute | solution.py:48
  65.5 3.4 %collective-permute-start.8 = (bf16[4,32,1024]{2,1,0:T(8,128)(2,1)S(1)}, bf16[4,32,1024]{2,1,0:T(8,128)(2,1)}, u32[]{:S(2)}, u32[]{:S(2)}) collective-permute-start(bf16[4,32,1024]{2,1,0:T(8,128)(2,1)S(1)} %all-to-all-done.2.w0), channel_id=1, source_target_pairs={{0,480},{1,33},{32,0},{33,65},{64,32},{65,97},{96,64},{97,129},{12... | collective-permute-start | bytes 786440 | tf_op jit(solution)/shard_map/ppermute | solution.py:48
  68.8 0.0 collective-permute-done.4.key_ref
  68.9 0.0 collective-permute-done.5.value_ref
  68.9 0.9 shard_map.121
  69.8 5.6 %all-to-all-start.1 = ((bf16[8,32,1024]{2,1,0:T(8,128)(2,1)}), bf16[8,32,1024]{2,1,0:T(8,128)(2,1)S(1)}, u32[]{:S(2)}, u32[]{:S(2)}) async-start(bf16[8,32,1024]{2,1,0:T(8,128)(2,1)} %shard_map.121), calls=%async_computation.1 | async-start | bytes 1048576 | tf_op jit(solution)/shard_map/all_to_all | solution.py:196
  75.4 0.0 collective-permute-done.6.w1
  75.4 0.0 collective-permute-done.7.w2
  75.4 3.5 %collective-permute-done.8.w3 = bf16[4,32,1024]{2,1,0:T(8,128)(2,1)} collective-permute-done((bf16[4,32,1024]{2,1,0:T(8,128)(2,1)S(1)}, bf16[4,32,1024]{2,1,0:T(8,128)(2,1)}, u32[]{:S(2)}, u32[]{:S(2)}) %collective-permute-start.8) | collective-permute-done | bytes 262176 | tf_op jit(solution)/shard_map/ppermute | solution.py:48
  78.9 2.1 %shard_map.122 = (f32[192,1024]{1,0:T(8,128)S(1)}, bf16[192,1024]{1,0:T(8,128)(2,1)S(1)}, bf16[192,1024]{1,0:T(8,128)(2,1)S(1)}, bf16[192,1024]{1,0:T(8,128)(2,1)S(1)}) custom-call(s32[4]{0:T(128)S(1)} %pad_add_fusion.place, bf16[4,256,192]{2,1,0:T(8,128)(2,1)S(1)} %bitcast.17, bf16[4,256,192]{2,1,0:T(8,128)(2,1)S(1)} %collective-permute-done.twin, ...), custom_call_target="tpu_custom_call" | custom-call | flops 99999997952 | tf_op jit(solution)/shard_map/pallas_call | solution.py:198
  81.0 3.3 %collective-permute-start.10 = (bf16[192,1024]{1,0:T(8,128)(2,1)S(1)}, bf16[192,1024]{1,0:T(8,128)(2,1)S(1)}, u32[]{:S(2)}, u32[]{:S(2)}) collective-permute-start(bf16[192,1024]{1,0:T(8,128)(2,1)S(1)} %get-tuple-element.35), channel_id=1, source_target_pairs={{0,16},{8,24},{16,0},{24,8},{1,17},{9,25},{17,1},{25,9},{2,18},{10... | collective-permute-start | bytes 1179656 | tf_op jit(solution)/shard_map/ppermute | solution.py:38
  84.2 1.9 %collective-permute-start.11 = (bf16[192,1024]{1,0:T(8,128)(2,1)S(1)}, bf16[192,1024]{1,0:T(8,128)(2,1)S(1)}, u32[]{:S(2)}, u32[]{:S(2)}) collective-permute-start(bf16[192,1024]{1,0:T(8,128)(2,1)S(1)} %get-tuple-element.36), channel_id=1, source_target_pairs={{0,24},{1,9},{8,0},{9,17},{16,8},{17,25},{24,16},{25,1},{2,26},{3,... | collective-permute-start | bytes 1179656 | tf_op jit(solution)/shard_map/ppermute | solution.py:48
  86.2 4.6 %collective-permute-start.9 = (bf16[192,1024]{1,0:T(8,128)(2,1)S(1)}, bf16[192,1024]{1,0:T(8,128)(2,1)S(1)}, u32[]{:S(2)}, u32[]{:S(2)}) collective-permute-start(bf16[192,1024]{1,0:T(8,128)(2,1)S(1)} %get-tuple-element.34), channel_id=1, source_target_pairs={{0,8},{1,25},{8,16},{9,1},{16,24},{17,9},{24,0},{25,17},{2,10},{3,... | collective-permute-start | bytes 1179656 | tf_op jit(solution)/shard_map/ppermute | solution.py:48
  90.7 4.4 %collective-permute-done.10.r2 = bf16[192,1024]{1,0:T(8,128)(2,1)S(1)} collective-permute-done((bf16[192,1024]{1,0:T(8,128)(2,1)S(1)}, bf16[192,1024]{1,0:T(8,128)(2,1)S(1)}, u32[]{:S(2)}, u32[]{:S(2)}) %collective-permute-start.10) | collective-permute-done | bytes 393248 | tf_op jit(solution)/shard_map/ppermute | solution.py:38
  95.1 8.7 %collective-permute-done.11.r3 = bf16[192,1024]{1,0:T(8,128)(2,1)S(1)} collective-permute-done((bf16[192,1024]{1,0:T(8,128)(2,1)S(1)}, bf16[192,1024]{1,0:T(8,128)(2,1)S(1)}, u32[]{:S(2)}, u32[]{:S(2)}) %collective-permute-start.11) | collective-permute-done | bytes 393248 | tf_op jit(solution)/shard_map/ppermute | solution.py:48
  103.8 0.0 collective-permute-done.9.r1
  103.8 0.1 all-to-all-done.1.far_ref
  103.9 0.4 shard_map.123
  104.3 13.6 %all_to_all.32 = f32[32,1,128]{2,1,0:T(1,128)S(1)} all-to-all(f32[32,1,128]{2,1,0:T(1,128)S(1)} %bitcast.19), channel_id=1, replica_groups=mesh['zh'=4,'zm'=2,'zp'=2,'x'=4,'y'=4,'c'=2] {'x','y','c'}, dimensions={0} | all-to-all | bytes 32768 | tf_op jit(solution)/shard_map/all_to_all | solution.py:216
  117.9 0.1 reduce_max.9
  118.0 17.7 %all_to_all.33 = f32[16,1,128]{2,1,0:T(1,128)S(1)} all-to-all(f32[16,1,128]{2,1,0:T(1,128)S(1)} %broadcast_in_dim.2), channel_id=1, replica_groups=mesh['zh'=4,'zm'=2,'zp'=2,'x'=4,'y'=4,'c'=2] {'zh','zm','zp'}, dimensions={0} | all-to-all | bytes 16384 | tf_op jit(solution)/shard_map/all_to_all | solution.py:54
  135.7 1.0 shard_map.124
  (7 shorter events, 0.0 us)
Async XLA Ops:
  3.0 7.8 %copy-start = (bf16[192,1024]{1,0:T(8,128)(2,1)S(1)}, bf16[192,1024]{1,0:T(8,128)(2,1)}, u32[]{:S(2)}) copy-start(bf16[192,1024]{1,0:T(8,128)(2,1)} %get-tuple-element.28.x0) | copy-start | bytes 1179652
  3.1 17.2 %all-to-all-start = ((bf16[16,64,192]{2,1,0:T(8,128)(2,1)}), bf16[16,64,192]{2,1,0:T(8,128)(2,1)S(1)}, u32[]{:S(2)}, u32[]{:S(2)}) async-start(bf16[16,64,192]{2,1,0:T(8,128)(2,1)} %bitcast.20), calls=%async_computation | async-start | bytes 1048576 | tf_op jit(solution)/shard_map/all_to_all | solution.py:172
  10.8 29.6 %collective-permute-start.1 = (bf16[192,1024]{1,0:T(8,128)(2,1)S(1)}, bf16[192,1024]{1,0:T(8,128)(2,1)S(1)}, u32[]{:S(2)}, u32[]{:S(2)}) collective-permute-start(bf16[192,1024]{1,0:T(8,128)(2,1)S(1)} %copy-done), channel_id=1, source_target_pairs={{0,8},{1,25},{8,16},{9,1},{16,24},{17,9},{24,0},{25,17},{2,10},{3,... | collective-permute-start | bytes 1179656 | tf_op jit(solution)/shard_map/ppermute | solution.py:48
  15.3 25.8 %collective-permute-start.2 = (bf16[192,1024]{1,0:T(8,128)(2,1)S(1)}, bf16[192,1024]{1,0:T(8,128)(2,1)S(1)}, u32[]{:S(2)}, u32[]{:S(2)}) collective-permute-start(bf16[192,1024]{1,0:T(8,128)(2,1)S(1)} %copy-done), channel_id=1, source_target_pairs={{0,16},{8,24},{16,0},{24,8},{1,17},{9,25},{17,1},{25,9},{2,18},{10... | collective-permute-start | bytes 1179656 | tf_op jit(solution)/shard_map/ppermute | solution.py:38
  17.8 24.1 %collective-permute-start.3 = (bf16[192,1024]{1,0:T(8,128)(2,1)S(1)}, bf16[192,1024]{1,0:T(8,128)(2,1)S(1)}, u32[]{:S(2)}, u32[]{:S(2)}) collective-permute-start(bf16[192,1024]{1,0:T(8,128)(2,1)S(1)} %copy-done), channel_id=1, source_target_pairs={{0,24},{1,9},{8,0},{9,17},{16,8},{17,25},{24,16},{25,1},{2,26},{3,... | collective-permute-start | bytes 1179656 | tf_op jit(solution)/shard_map/ppermute | solution.py:48
  20.3 22.3 %collective-permute-start = (bf16[4,256,192]{2,1,0:T(8,128)(2,1)S(1)}, bf16[4,256,192]{2,1,0:T(8,128)(2,1)S(1)}, u32[]{:S(2)}, u32[]{:S(2)}) collective-permute-start(bf16[4,256,192]{2,1,0:T(8,128)(2,1)S(1)} %bitcast.15), channel_id=1, source_target_pairs={{0,1},{1,0},{2,3},{3,2},{4,5},{5,4},{6,7},{7,6},{8,9},{9,8},{10,11... | collective-permute-start | bytes 1179656 | tf_op jit(solution)/shard_map/ppermute | solution.py:174
  27.4 29.1 %all-to-all-start.2 = ((bf16[4,32,1024]{2,1,0:T(8,128)(2,1)}), bf16[4,32,1024]{2,1,0:T(8,128)(2,1)S(1)}, u32[]{:S(2)}, u32[]{:S(2)}) async-start(bf16[4,32,1024]{2,1,0:T(8,128)(2,1)} %get-tuple-element.32), calls=%async_computation.2 | async-start | bytes 524288 | tf_op jit(solution)/shard_map/all_to_all | solution.py:184
  40.4 0.7 copy-start.1
  41.1 0.7 copy-start.3
  41.9 0.7 copy-start.5
  42.6 1.0 copy-start.2
  43.6 1.0 copy-start.4
  44.6 1.0 copy-start.6
  48.1 20.8 %collective-permute-start.4 = (bf16[4,2,16,1024]{3,2,1,0:T(8,128)(2,1)}, bf16[4,2,16,1024]{3,2,1,0:T(8,128)(2,1)S(1)}, u32[]{:S(2)}, u32[]{:S(2)}) collective-permute-start(bf16[4,2,16,1024]{3,2,1,0:T(8,128)(2,1)} %get-tuple-element.30), channel_id=1, source_target_pairs={{0,480},{1,33},{32,0},{33,65},{64,32},{65,97},{96,64},{97,129},{12... | collective-permute-start | bytes 786440 | tf_op jit(solution)/shard_map/ppermute | solution.py:48
  50.7 18.2 %collective-permute-start.5 = (bf16[4,2,16,1024]{3,2,1,0:T(8,128)(2,1)}, bf16[4,2,16,1024]{3,2,1,0:T(8,128)(2,1)S(1)}, u32[]{:S(2)}, u32[]{:S(2)}) collective-permute-start(bf16[4,2,16,1024]{3,2,1,0:T(8,128)(2,1)} %get-tuple-element.31), channel_id=1, source_target_pairs={{0,32},{1,481},{32,64},{33,1},{64,96},{65,33},{96,128},{97,65},{12... | collective-permute-start | bytes 786440 | tf_op jit(solution)/shard_map/ppermute | solution.py:48
  56.5 18.9 %collective-permute-start.6 = (bf16[4,32,1024]{2,1,0:T(8,128)(2,1)S(1)}, bf16[4,32,1024]{2,1,0:T(8,128)(2,1)S(1)}, u32[]{:S(2)}, u32[]{:S(2)}) collective-permute-start(bf16[4,32,1024]{2,1,0:T(8,128)(2,1)S(1)} %all-to-all-done.2.w0), channel_id=1, source_target_pairs={{0,32},{1,481},{32,64},{33,1},{64,96},{65,33},{96,128},{97,65},{12... | collective-permute-start | bytes 786440 | tf_op jit(solution)/shard_map/ppermute | solution.py:48
  59.9 15.5 %collective-permute-start.7 = (bf16[4,32,1024]{2,1,0:T(8,128)(2,1)S(1)}, bf16[4,32,1024]{2,1,0:T(8,128)(2,1)S(1)}, u32[]{:S(2)}, u32[]{:S(2)}) collective-permute-start(bf16[4,32,1024]{2,1,0:T(8,128)(2,1)S(1)} %all-to-all-done.2.w0), channel_id=1, source_target_pairs={{0,64},{1,449},{32,96},{33,481},{64,128},{65,1},{96,160},{97,33},{... | collective-permute-start | bytes 786440 | tf_op jit(solution)/shard_map/ppermute | solution.py:48
  65.5 13.4 %collective-permute-start.8 = (bf16[4,32,1024]{2,1,0:T(8,128)(2,1)S(1)}, bf16[4,32,1024]{2,1,0:T(8,128)(2,1)}, u32[]{:S(2)}, u32[]{:S(2)}) collective-permute-start(bf16[4,32,1024]{2,1,0:T(8,128)(2,1)S(1)} %all-to-all-done.2.w0), channel_id=1, source_target_pairs={{0,480},{1,33},{32,0},{33,65},{64,32},{65,97},{96,64},{97,129},{12... | collective-permute-start | bytes 786440 | tf_op jit(solution)/shard_map/ppermute | solution.py:48
  69.8 34.2 %all-to-all-start.1 = ((bf16[8,32,1024]{2,1,0:T(8,128)(2,1)}), bf16[8,32,1024]{2,1,0:T(8,128)(2,1)S(1)}, u32[]{:S(2)}, u32[]{:S(2)}) async-start(bf16[8,32,1024]{2,1,0:T(8,128)(2,1)} %shard_map.121), calls=%async_computation.1 | async-start | bytes 1048576 | tf_op jit(solution)/shard_map/all_to_all | solution.py:196
  81.0 14.1 %collective-permute-start.10 = (bf16[192,1024]{1,0:T(8,128)(2,1)S(1)}, bf16[192,1024]{1,0:T(8,128)(2,1)S(1)}, u32[]{:S(2)}, u32[]{:S(2)}) collective-permute-start(bf16[192,1024]{1,0:T(8,128)(2,1)S(1)} %get-tuple-element.35), channel_id=1, source_target_pairs={{0,16},{8,24},{16,0},{24,8},{1,17},{9,25},{17,1},{25,9},{2,18},{10... | collective-permute-start | bytes 1179656 | tf_op jit(solution)/shard_map/ppermute | solution.py:38
  84.2 19.6 %collective-permute-start.11 = (bf16[192,1024]{1,0:T(8,128)(2,1)S(1)}, bf16[192,1024]{1,0:T(8,128)(2,1)S(1)}, u32[]{:S(2)}, u32[]{:S(2)}) collective-permute-start(bf16[192,1024]{1,0:T(8,128)(2,1)S(1)} %get-tuple-element.36), channel_id=1, source_target_pairs={{0,24},{1,9},{8,0},{9,17},{16,8},{17,25},{24,16},{25,1},{2,26},{3,... | collective-permute-start | bytes 1179656 | tf_op jit(solution)/shard_map/ppermute | solution.py:48
  86.2 17.7 %collective-permute-start.9 = (bf16[192,1024]{1,0:T(8,128)(2,1)S(1)}, bf16[192,1024]{1,0:T(8,128)(2,1)S(1)}, u32[]{:S(2)}, u32[]{:S(2)}) collective-permute-start(bf16[192,1024]{1,0:T(8,128)(2,1)S(1)} %get-tuple-element.34), channel_id=1, source_target_pairs={{0,8},{1,25},{8,16},{9,1},{16,24},{17,9},{24,0},{25,17},{2,10},{3,... | collective-permute-start | bytes 1179656 | tf_op jit(solution)/shard_map/ppermute | solution.py:48

commit v7 on v6

--- a/solution.py
+++ b/solution.py
@@ -191,7 +191,7 @@
         flops=10**11,
     )(place, own, twin, inputs, *others)
     key, value = shift_by_core(key, RING, -1), shift_by_core(value, RING, 1)
-    weights = [weight] + [shift_by_core(weight, RING, by) for by in (1, 2, -1)]
+    weights = [weight] + [shift_by_core(weight, RING, by) for by in (1, -2, -1)]
     part = kernel_call(near_body, shape((8, 32, 1024), BF16), [VMEM] * 3)(keep, key, value)
     far = lax.all_to_all(part, ("zh", "zm"), 0, 0, tiled=True)
 

time: 138 us -> 137 us (level)
  blocking collectives: 31.3 us -> 35 us
  waiting for transfers between devices: 16.7 us -> 13.5 us
    ppermute x2, waiting for transfers between devices: 4.38 us -> 0.55 us  [shift(): lax.ppermute(value, axes, [(i, (i + by) % count) for i in range(count)])]
    all_to_all x1, blocking collectives: 13.6 us -> 16.4 us  [per_device(): peaks = lax.all_to_all(peaks, ('x', *TENSOR), 0, 0, tiled=True)]
where the time goes in v7:
time: 137 us; the launch traced here: 136 us
  starting transfers between devices  72.3 us (53%)
  blocking collectives  35 us (26%)
  waiting for transfers between devices  13.5 us (10%)
  Pallas kernels  9.1 us (7%)
  local copies, waits for them, and re-layouts  5.24 us (4%)
    ppermute x9, starting transfers between devices, shift_by_core(): return lax.ppermute(value, (*axes, 'c'), pairs)  33.3 us
    all_to_all x1, blocking collectives, spread(): return lax.all_to_all(copies, axes, 0, 0, tiled=True)  18.6 us
    all_to_all x1, blocking collectives, per_device(): peaks = lax.all_to_all(peaks, ('x', *TENSOR), 0, 0, tiled=True)  16.4 us
    ppermute x9, waiting for transfers between devices, shift_by_core(): return lax.ppermute(value, (*axes, 'c'), pairs)  13 us
    all_to_all x1, starting transfers between devices, per_device(): weight = lax.all_to_all(weight, 'zh', 0, 0, tiled=True)  13 us
    all_to_all x1, starting transfers between devices, per_device(): own = lax.all_to_all(own.reshape(16, 64, 192), ('x', 'y'), 0, 0, tiled=True)  7.73 us
    ppermute x1, starting transfers between devices, per_device(): twin = lax.ppermute(own, 'c', [(0, 1), (1, 0)])  7.03 us
    ppermute x2, starting transfers between devices, shift(): lax.ppermute(value, axes, [(i, (i + by) % count) for i in range(count)])  5.74 us
  transfers between devices with their start and end apart: 15, of which 4 were waited for; matrix products, arithmetic and copies ran while one was open for 0% of the time, Pallas kernels for 4%

profile of v7, /device:TPU:1, one launch (start us, length us, event | category | flops | bytes accessed | tf_op | source)
XLA Modules:
  0.0 136.2 jit_solution(15742969475768867713)
XLA Ops:
  0.6 2.4 %shard_map.119 = (bf16[4,4,64,192]{3,2,1,0:T(8,128)(2,1)}, bf16[192,1024]{1,0:T(8,128)(2,1)}, bf16[4,32,1024]{2,1,0:T(8,128)(2,1)}) custom-call(bf16[192,128]{1,0:T(8,128)(2,1)} %refs_0_.1, bf16[192,128]{1,0:T(8,128)(2,1)} %refs_1_.1, bf16[192,1024]{1,0:T(8,128)(2,1)} %refs_2_.1, f32[8,192]{1,0:T(8,128)} %bitcast.23, bf16[16,1024]{1,0:T(8,128)(2,1)} %bitcast.21, ...), custom_call_target="tpu_custom_call" | custom-call | tf_op jit(solution)/shard_map/pallas_call | solution.py:163
  3.0 0.0 copy-start
  3.1 7.7 %all-to-all-start = ((bf16[16,64,192]{2,1,0:T(8,128)(2,1)}), bf16[16,64,192]{2,1,0:T(8,128)(2,1)S(1)}, u32[]{:S(2)}, u32[]{:S(2)}) async-start(bf16[16,64,192]{2,1,0:T(8,128)(2,1)} %bitcast.20), calls=%async_computation | async-start | bytes 1048576 | tf_op jit(solution)/shard_map/all_to_all | solution.py:172
  10.8 0.0 copy-done
  10.8 4.5 %collective-permute-start.1 = (bf16[192,1024]{1,0:T(8,128)(2,1)S(1)}, bf16[192,1024]{1,0:T(8,128)(2,1)S(1)}, u32[]{:S(2)}, u32[]{:S(2)}) collective-permute-start(bf16[192,1024]{1,0:T(8,128)(2,1)S(1)} %copy-done), channel_id=1, source_target_pairs={{0,8},{1,25},{8,16},{9,1},{16,24},{17,9},{24,0},{25,17},{2,10},{3,... | collective-permute-start | bytes 1179656 | tf_op jit(solution)/shard_map/ppermute | solution.py:48
  15.3 2.5 %collective-permute-start.2 = (bf16[192,1024]{1,0:T(8,128)(2,1)S(1)}, bf16[192,1024]{1,0:T(8,128)(2,1)S(1)}, u32[]{:S(2)}, u32[]{:S(2)}) collective-permute-start(bf16[192,1024]{1,0:T(8,128)(2,1)S(1)} %copy-done), channel_id=1, source_target_pairs={{0,16},{8,24},{16,0},{24,8},{1,17},{9,25},{17,1},{25,9},{2,18},{10... | collective-permute-start | bytes 1179656 | tf_op jit(solution)/shard_map/ppermute | solution.py:38
  17.8 2.5 %collective-permute-start.3 = (bf16[192,1024]{1,0:T(8,128)(2,1)S(1)}, bf16[192,1024]{1,0:T(8,128)(2,1)S(1)}, u32[]{:S(2)}, u32[]{:S(2)}) collective-permute-start(bf16[192,1024]{1,0:T(8,128)(2,1)S(1)} %copy-done), channel_id=1, source_target_pairs={{0,24},{1,9},{8,0},{9,17},{16,8},{17,25},{24,16},{25,1},{2,26},{3,... | collective-permute-start | bytes 1179656 | tf_op jit(solution)/shard_map/ppermute | solution.py:48
  20.3 0.0 all-to-all-done
  20.3 7.0 %collective-permute-start = (bf16[4,256,192]{2,1,0:T(8,128)(2,1)S(1)}, bf16[4,256,192]{2,1,0:T(8,128)(2,1)S(1)}, u32[]{:S(2)}, u32[]{:S(2)}) collective-permute-start(bf16[4,256,192]{2,1,0:T(8,128)(2,1)S(1)} %bitcast.15), channel_id=1, source_target_pairs={{0,1},{1,0},{2,3},{3,2},{4,5},{5,4},{6,7},{7,6},{8,9},{9,8},{10,11... | collective-permute-start | bytes 1179656 | tf_op jit(solution)/shard_map/ppermute | solution.py:174
  27.3 0.1 pad_add_fusion.place
  27.4 13.0 %all-to-all-start.2 = ((bf16[4,32,1024]{2,1,0:T(8,128)(2,1)}), bf16[4,32,1024]{2,1,0:T(8,128)(2,1)S(1)}, u32[]{:S(2)}, u32[]{:S(2)}) async-start(bf16[4,32,1024]{2,1,0:T(8,128)(2,1)} %get-tuple-element.32), calls=%async_computation.2 | async-start | bytes 524288 | tf_op jit(solution)/shard_map/all_to_all | solution.py:184
  40.4 0.0 collective-permute-done.1.x1
  40.4 0.7 copy-done.1
  41.1 0.0 collective-permute-done.2.x2
  41.1 0.7 copy-done.3
  41.9 0.0 collective-permute-done.3.x3
  41.9 0.7 copy-done.5
  42.6 0.0 collective-permute-done.twin
  42.6 1.0 copy-done.2
  43.6 1.0 copy-done.4
  44.6 1.0 copy-done.6
  45.6 2.4 %shard_map.120 = (f32[4,2,32,1024]{3,2,1,0:T(8,128)S(1)}, bf16[4,2,16,1024]{3,2,1,0:T(8,128)(2,1)}, bf16[4,2,16,1024]{3,2,1,0:T(8,128)(2,1)}) custom-call(s32[4]{0:T(128)S(1)} %pad_add_fusion.place, bf16[4,256,192]{2,1,0:T(8,128)(2,1)S(1)} %bitcast.16, bf16[4,256,192]{2,1,0:T(8,128)(2,1)S(1)} %collective-permute-done.twin, bf16[192,1024]{1,0:T(8,128)(2,1)S(1)} %copy-done, ...), custom_call_target="tpu_custom_call" | custom-call | flops 99999997952 | tf_op jit(solution)/shard_map/pallas_call | solution.py:186
  48.1 2.6 %collective-permute-start.4 = (bf16[4,2,16,1024]{3,2,1,0:T(8,128)(2,1)}, bf16[4,2,16,1024]{3,2,1,0:T(8,128)(2,1)S(1)}, u32[]{:S(2)}, u32[]{:S(2)}) collective-permute-start(bf16[4,2,16,1024]{3,2,1,0:T(8,128)(2,1)} %get-tuple-element.30), channel_id=1, source_target_pairs={{0,480},{1,33},{32,0},{33,65},{64,32},{65,97},{96,64},{97,129},{12... | collective-permute-start | bytes 786440 | tf_op jit(solution)/shard_map/ppermute | solution.py:48
  50.7 5.8 %collective-permute-start.5 = (bf16[4,2,16,1024]{3,2,1,0:T(8,128)(2,1)}, bf16[4,2,16,1024]{3,2,1,0:T(8,128)(2,1)S(1)}, u32[]{:S(2)}, u32[]{:S(2)}) collective-permute-start(bf16[4,2,16,1024]{3,2,1,0:T(8,128)(2,1)} %get-tuple-element.31), channel_id=1, source_target_pairs={{0,32},{1,481},{32,64},{33,1},{64,96},{65,33},{96,128},{97,65},{12... | collective-permute-start | bytes 786440 | tf_op jit(solution)/shard_map/ppermute | solution.py:48
  56.5 0.0 all-to-all-done.2.w0
  56.5 3.4 %collective-permute-start.6 = (bf16[4,32,1024]{2,1,0:T(8,128)(2,1)S(1)}, bf16[4,32,1024]{2,1,0:T(8,128)(2,1)S(1)}, u32[]{:S(2)}, u32[]{:S(2)}) collective-permute-start(bf16[4,32,1024]{2,1,0:T(8,128)(2,1)S(1)} %all-to-all-done.2.w0), channel_id=1, source_target_pairs={{0,32},{1,481},{32,64},{33,1},{64,96},{65,33},{96,128},{97,65},{12... | collective-permute-start | bytes 786440 | tf_op jit(solution)/shard_map/ppermute | solution.py:48
  59.9 5.5 %collective-permute-start.7 = (bf16[4,32,1024]{2,1,0:T(8,128)(2,1)S(1)}, bf16[4,32,1024]{2,1,0:T(8,128)(2,1)S(1)}, u32[]{:S(2)}, u32[]{:S(2)}) collective-permute-start(bf16[4,32,1024]{2,1,0:T(8,128)(2,1)S(1)} %all-to-all-done.2.w0), channel_id=1, source_target_pairs={{0,448},{1,65},{32,480},{33,97},{64,0},{65,129},{96,32},{97,161},{... | collective-permute-start | bytes 786440 | tf_op jit(solution)/shard_map/ppermute | solution.py:48
  65.3 2.6 %collective-permute-start.8 = (bf16[4,32,1024]{2,1,0:T(8,128)(2,1)S(1)}, bf16[4,32,1024]{2,1,0:T(8,128)(2,1)}, u32[]{:S(2)}, u32[]{:S(2)}) collective-permute-start(bf16[4,32,1024]{2,1,0:T(8,128)(2,1)S(1)} %all-to-all-done.2.w0), channel_id=1, source_target_pairs={{0,480},{1,33},{32,0},{33,65},{64,32},{65,97},{96,64},{97,129},{12... | collective-permute-start | bytes 786440 | tf_op jit(solution)/shard_map/ppermute | solution.py:48
  68.0 0.0 collective-permute-done.4.key_ref
  68.0 0.0 collective-permute-done.5.value_ref
  68.0 0.9 shard_map.121
  68.9 5.5 %all-to-all-start.1 = ((bf16[8,32,1024]{2,1,0:T(8,128)(2,1)}), bf16[8,32,1024]{2,1,0:T(8,128)(2,1)S(1)}, u32[]{:S(2)}, u32[]{:S(2)}) async-start(bf16[8,32,1024]{2,1,0:T(8,128)(2,1)} %shard_map.121), calls=%async_computation.1 | async-start | bytes 1048576 | tf_op jit(solution)/shard_map/all_to_all | solution.py:196
  74.4 0.0 collective-permute-done.6.w1
  74.4 0.0 collective-permute-done.7.w2
  74.5 2.6 %collective-permute-done.8.w3 = bf16[4,32,1024]{2,1,0:T(8,128)(2,1)} collective-permute-done((bf16[4,32,1024]{2,1,0:T(8,128)(2,1)S(1)}, bf16[4,32,1024]{2,1,0:T(8,128)(2,1)}, u32[]{:S(2)}, u32[]{:S(2)}) %collective-permute-start.8) | collective-permute-done | bytes 262176 | tf_op jit(solution)/shard_map/ppermute | solution.py:48
  77.1 2.1 %shard_map.122 = (f32[192,1024]{1,0:T(8,128)S(1)}, bf16[192,1024]{1,0:T(8,128)(2,1)S(1)}, bf16[192,1024]{1,0:T(8,128)(2,1)S(1)}, bf16[192,1024]{1,0:T(8,128)(2,1)S(1)}) custom-call(s32[4]{0:T(128)S(1)} %pad_add_fusion.place, bf16[4,256,192]{2,1,0:T(8,128)(2,1)S(1)} %bitcast.17, bf16[4,256,192]{2,1,0:T(8,128)(2,1)S(1)} %collective-permute-done.twin, ...), custom_call_target="tpu_custom_call" | custom-call | flops 99999997952 | tf_op jit(solution)/shard_map/pallas_call | solution.py:198
  79.2 3.3 %collective-permute-start.10 = (bf16[192,1024]{1,0:T(8,128)(2,1)S(1)}, bf16[192,1024]{1,0:T(8,128)(2,1)S(1)}, u32[]{:S(2)}, u32[]{:S(2)}) collective-permute-start(bf16[192,1024]{1,0:T(8,128)(2,1)S(1)} %get-tuple-element.35), channel_id=1, source_target_pairs={{0,16},{8,24},{16,0},{24,8},{1,17},{9,25},{17,1},{25,9},{2,18},{10... | collective-permute-start | bytes 1179656 | tf_op jit(solution)/shard_map/ppermute | solution.py:38
  82.4 1.9 %collective-permute-start.11 = (bf16[192,1024]{1,0:T(8,128)(2,1)S(1)}, bf16[192,1024]{1,0:T(8,128)(2,1)S(1)}, u32[]{:S(2)}, u32[]{:S(2)}) collective-permute-start(bf16[192,1024]{1,0:T(8,128)(2,1)S(1)} %get-tuple-element.36), channel_id=1, source_target_pairs={{0,24},{1,9},{8,0},{9,17},{16,8},{17,25},{24,16},{25,1},{2,26},{3,... | collective-permute-start | bytes 1179656 | tf_op jit(solution)/shard_map/ppermute | solution.py:48
  84.3 4.6 %collective-permute-start.9 = (bf16[192,1024]{1,0:T(8,128)(2,1)S(1)}, bf16[192,1024]{1,0:T(8,128)(2,1)S(1)}, u32[]{:S(2)}, u32[]{:S(2)}) collective-permute-start(bf16[192,1024]{1,0:T(8,128)(2,1)S(1)} %get-tuple-element.34), channel_id=1, source_target_pairs={{0,8},{1,25},{8,16},{9,1},{16,24},{17,9},{24,0},{25,17},{2,10},{3,... | collective-permute-start | bytes 1179656 | tf_op jit(solution)/shard_map/ppermute | solution.py:48
  88.9 0.5 collective-permute-done.10.r2
  89.5 6.9 %collective-permute-done.11.r3 = bf16[192,1024]{1,0:T(8,128)(2,1)S(1)} collective-permute-done((bf16[192,1024]{1,0:T(8,128)(2,1)S(1)}, bf16[192,1024]{1,0:T(8,128)(2,1)S(1)}, u32[]{:S(2)}, u32[]{:S(2)}) %collective-permute-start.11) | collective-permute-done | bytes 393248 | tf_op jit(solution)/shard_map/ppermute | solution.py:48
  96.4 3.4 %collective-permute-done.9.r1 = bf16[192,1024]{1,0:T(8,128)(2,1)S(1)} collective-permute-done((bf16[192,1024]{1,0:T(8,128)(2,1)S(1)}, bf16[192,1024]{1,0:T(8,128)(2,1)S(1)}, u32[]{:S(2)}, u32[]{:S(2)}) %collective-permute-start.9) | collective-permute-done | bytes 393248 | tf_op jit(solution)/shard_map/ppermute | solution.py:48
  99.8 0.0 all-to-all-done.1.far_ref
  99.8 0.4 shard_map.123
  100.2 16.4 %all_to_all.32 = f32[32,1,128]{2,1,0:T(1,128)S(1)} all-to-all(f32[32,1,128]{2,1,0:T(1,128)S(1)} %bitcast.19), channel_id=1, replica_groups=mesh['zh'=4,'zm'=2,'zp'=2,'x'=4,'y'=4,'c'=2] {'x','y','c'}, dimensions={0} | all-to-all | bytes 32768 | tf_op jit(solution)/shard_map/all_to_all | solution.py:216
  116.6 0.1 reduce_max.9
  116.6 18.6 %all_to_all.33 = f32[16,1,128]{2,1,0:T(1,128)S(1)} all-to-all(f32[16,1,128]{2,1,0:T(1,128)S(1)} %broadcast_in_dim.2), channel_id=1, replica_groups=mesh['zh'=4,'zm'=2,'zp'=2,'x'=4,'y'=4,'c'=2] {'zh','zm','zp'}, dimensions={0} | all-to-all | bytes 16384 | tf_op jit(solution)/shard_map/all_to_all | solution.py:54
  135.2 1.0 shard_map.124
  (7 shorter events, 0.0 us)
Async XLA Ops:
  3.0 7.8 %copy-start = (bf16[192,1024]{1,0:T(8,128)(2,1)S(1)}, bf16[192,1024]{1,0:T(8,128)(2,1)}, u32[]{:S(2)}) copy-start(bf16[192,1024]{1,0:T(8,128)(2,1)} %get-tuple-element.28.x0) | copy-start | bytes 1179652
  3.1 17.2 %all-to-all-start = ((bf16[16,64,192]{2,1,0:T(8,128)(2,1)}), bf16[16,64,192]{2,1,0:T(8,128)(2,1)S(1)}, u32[]{:S(2)}, u32[]{:S(2)}) async-start(bf16[16,64,192]{2,1,0:T(8,128)(2,1)} %bitcast.20), calls=%async_computation | async-start | bytes 1048576 | tf_op jit(solution)/shard_map/all_to_all | solution.py:172
  10.8 29.6 %collective-permute-start.1 = (bf16[192,1024]{1,0:T(8,128)(2,1)S(1)}, bf16[192,1024]{1,0:T(8,128)(2,1)S(1)}, u32[]{:S(2)}, u32[]{:S(2)}) collective-permute-start(bf16[192,1024]{1,0:T(8,128)(2,1)S(1)} %copy-done), channel_id=1, source_target_pairs={{0,8},{1,25},{8,16},{9,1},{16,24},{17,9},{24,0},{25,17},{2,10},{3,... | collective-permute-start | bytes 1179656 | tf_op jit(solution)/shard_map/ppermute | solution.py:48
  15.3 25.8 %collective-permute-start.2 = (bf16[192,1024]{1,0:T(8,128)(2,1)S(1)}, bf16[192,1024]{1,0:T(8,128)(2,1)S(1)}, u32[]{:S(2)}, u32[]{:S(2)}) collective-permute-start(bf16[192,1024]{1,0:T(8,128)(2,1)S(1)} %copy-done), channel_id=1, source_target_pairs={{0,16},{8,24},{16,0},{24,8},{1,17},{9,25},{17,1},{25,9},{2,18},{10... | collective-permute-start | bytes 1179656 | tf_op jit(solution)/shard_map/ppermute | solution.py:38
  17.8 24.1 %collective-permute-start.3 = (bf16[192,1024]{1,0:T(8,128)(2,1)S(1)}, bf16[192,1024]{1,0:T(8,128)(2,1)S(1)}, u32[]{:S(2)}, u32[]{:S(2)}) collective-permute-start(bf16[192,1024]{1,0:T(8,128)(2,1)S(1)} %copy-done), channel_id=1, source_target_pairs={{0,24},{1,9},{8,0},{9,17},{16,8},{17,25},{24,16},{25,1},{2,26},{3,... | collective-permute-start | bytes 1179656 | tf_op jit(solution)/shard_map/ppermute | solution.py:48
  20.3 22.3 %collective-permute-start = (bf16[4,256,192]{2,1,0:T(8,128)(2,1)S(1)}, bf16[4,256,192]{2,1,0:T(8,128)(2,1)S(1)}, u32[]{:S(2)}, u32[]{:S(2)}) collective-permute-start(bf16[4,256,192]{2,1,0:T(8,128)(2,1)S(1)} %bitcast.15), channel_id=1, source_target_pairs={{0,1},{1,0},{2,3},{3,2},{4,5},{5,4},{6,7},{7,6},{8,9},{9,8},{10,11... | collective-permute-start | bytes 1179656 | tf_op jit(solution)/shard_map/ppermute | solution.py:174
  27.4 29.1 %all-to-all-start.2 = ((bf16[4,32,1024]{2,1,0:T(8,128)(2,1)}), bf16[4,32,1024]{2,1,0:T(8,128)(2,1)S(1)}, u32[]{:S(2)}, u32[]{:S(2)}) async-start(bf16[4,32,1024]{2,1,0:T(8,128)(2,1)} %get-tuple-element.32), calls=%async_computation.2 | async-start | bytes 524288 | tf_op jit(solution)/shard_map/all_to_all | solution.py:184
  40.4 0.7 copy-start.1
  41.1 0.7 copy-start.3
  41.9 0.7 copy-start.5
  42.6 1.0 copy-start.2
  43.6 1.0 copy-start.4
  44.6 1.0 copy-start.6
  48.1 19.9 %collective-permute-start.4 = (bf16[4,2,16,1024]{3,2,1,0:T(8,128)(2,1)}, bf16[4,2,16,1024]{3,2,1,0:T(8,128)(2,1)S(1)}, u32[]{:S(2)}, u32[]{:S(2)}) collective-permute-start(bf16[4,2,16,1024]{3,2,1,0:T(8,128)(2,1)} %get-tuple-element.30), channel_id=1, source_target_pairs={{0,480},{1,33},{32,0},{33,65},{64,32},{65,97},{96,64},{97,129},{12... | collective-permute-start | bytes 786440 | tf_op jit(solution)/shard_map/ppermute | solution.py:48
  50.7 17.3 %collective-permute-start.5 = (bf16[4,2,16,1024]{3,2,1,0:T(8,128)(2,1)}, bf16[4,2,16,1024]{3,2,1,0:T(8,128)(2,1)S(1)}, u32[]{:S(2)}, u32[]{:S(2)}) collective-permute-start(bf16[4,2,16,1024]{3,2,1,0:T(8,128)(2,1)} %get-tuple-element.31), channel_id=1, source_target_pairs={{0,32},{1,481},{32,64},{33,1},{64,96},{65,33},{96,128},{97,65},{12... | collective-permute-start | bytes 786440 | tf_op jit(solution)/shard_map/ppermute | solution.py:48
  56.5 17.9 %collective-permute-start.6 = (bf16[4,32,1024]{2,1,0:T(8,128)(2,1)S(1)}, bf16[4,32,1024]{2,1,0:T(8,128)(2,1)S(1)}, u32[]{:S(2)}, u32[]{:S(2)}) collective-permute-start(bf16[4,32,1024]{2,1,0:T(8,128)(2,1)S(1)} %all-to-all-done.2.w0), channel_id=1, source_target_pairs={{0,32},{1,481},{32,64},{33,1},{64,96},{65,33},{96,128},{97,65},{12... | collective-permute-start | bytes 786440 | tf_op jit(solution)/shard_map/ppermute | solution.py:48
  59.9 14.6 %collective-permute-start.7 = (bf16[4,32,1024]{2,1,0:T(8,128)(2,1)S(1)}, bf16[4,32,1024]{2,1,0:T(8,128)(2,1)S(1)}, u32[]{:S(2)}, u32[]{:S(2)}) collective-permute-start(bf16[4,32,1024]{2,1,0:T(8,128)(2,1)S(1)} %all-to-all-done.2.w0), channel_id=1, source_target_pairs={{0,448},{1,65},{32,480},{33,97},{64,0},{65,129},{96,32},{97,161},{... | collective-permute-start | bytes 786440 | tf_op jit(solution)/shard_map/ppermute | solution.py:48
  65.3 11.7 %collective-permute-start.8 = (bf16[4,32,1024]{2,1,0:T(8,128)(2,1)S(1)}, bf16[4,32,1024]{2,1,0:T(8,128)(2,1)}, u32[]{:S(2)}, u32[]{:S(2)}) collective-permute-start(bf16[4,32,1024]{2,1,0:T(8,128)(2,1)S(1)} %all-to-all-done.2.w0), channel_id=1, source_target_pairs={{0,480},{1,33},{32,0},{33,65},{64,32},{65,97},{96,64},{97,129},{12... | collective-permute-start | bytes 786440 | tf_op jit(solution)/shard_map/ppermute | solution.py:48
  68.9 30.9 %all-to-all-start.1 = ((bf16[8,32,1024]{2,1,0:T(8,128)(2,1)}), bf16[8,32,1024]{2,1,0:T(8,128)(2,1)S(1)}, u32[]{:S(2)}, u32[]{:S(2)}) async-start(bf16[8,32,1024]{2,1,0:T(8,128)(2,1)} %shard_map.121), calls=%async_computation.1 | async-start | bytes 1048576 | tf_op jit(solution)/shard_map/all_to_all | solution.py:196
  79.2 10.3 %collective-permute-start.10 = (bf16[192,1024]{1,0:T(8,128)(2,1)S(1)}, bf16[192,1024]{1,0:T(8,128)(2,1)S(1)}, u32[]{:S(2)}, u32[]{:S(2)}) collective-permute-start(bf16[192,1024]{1,0:T(8,128)(2,1)S(1)} %get-tuple-element.35), channel_id=1, source_target_pairs={{0,16},{8,24},{16,0},{24,8},{1,17},{9,25},{17,1},{25,9},{2,18},{10... | collective-permute-start | bytes 1179656 | tf_op jit(solution)/shard_map/ppermute | solution.py:38
  82.4 14.0 %collective-permute-start.11 = (bf16[192,1024]{1,0:T(8,128)(2,1)S(1)}, bf16[192,1024]{1,0:T(8,128)(2,1)S(1)}, u32[]{:S(2)}, u32[]{:S(2)}) collective-permute-start(bf16[192,1024]{1,0:T(8,128)(2,1)S(1)} %get-tuple-element.36), channel_id=1, source_target_pairs={{0,24},{1,9},{8,0},{9,17},{16,8},{17,25},{24,16},{25,1},{2,26},{3,... | collective-permute-start | bytes 1179656 | tf_op jit(solution)/shard_map/ppermute | solution.py:48
  84.3 15.5 %collective-permute-start.9 = (bf16[192,1024]{1,0:T(8,128)(2,1)S(1)}, bf16[192,1024]{1,0:T(8,128)(2,1)S(1)}, u32[]{:S(2)}, u32[]{:S(2)}) collective-permute-start(bf16[192,1024]{1,0:T(8,128)(2,1)S(1)} %get-tuple-element.34), channel_id=1, source_target_pairs={{0,8},{1,25},{8,16},{9,1},{16,24},{17,9},{24,0},{25,17},{2,10},{3,... | collective-permute-start | bytes 1179656 | tf_op jit(solution)/shard_map/ppermute | solution.py:48

commit v8 on v7

--- a/solution.py
+++ b/solution.py
@@ -15,7 +15,7 @@
 HBM = pl.BlockSpec(memory_space=pltpu.HBM)
 
 
-def kernel_call(body, out_shape, in_specs, out_specs=None, scratch=(), flops=0, mib=16):
+def kernel_call(body, out_shape, in_specs, out_specs=None, scratch=(), flops=0, mib=8):
     if out_specs is None:
         out_specs = jax.tree.map(lambda _: VMEM, out_shape)
     return pl.pallas_call(
@@ -86,19 +86,20 @@
                 weight_ref[copy, part * 16 : (part + 1) * 16, at] = scaled
 
 
-def weight_body(place, own, twin, x0, x1, x2, x3, keep_ref, key_ref, value_ref, total):
+def weight_body(place, own, twin, x0, x1, x2, x3, keep_ref, key_ref, value_ref):
     x, zp, core = place[0], place[2], place[3]
     members = [lax.rem(x + k, 4) for k in (0, 3 - 2 * core, 2, 1 + 2 * core)]
     inputs = jnp.concatenate([ref[...] for ref in (x0, x1, x2, x3)], axis=0)
     for i, part in enumerate((own, twin)):
         lhs = jnp.concatenate([part[member] for member in members], axis=1)
         value = jnp.dot(lhs, inputs, preferred_element_type=F32)
-        total[i] = value.reshape(4, 2, 32, 1024)
+        value = value.reshape(4, 2, 32, 1024)
         zm = lax.rem(core + i, 2)
         for zh in range(4):
-            keep_ref[zh, zm] = total[i, zh, zp]
-            key_ref[zh, zm] = total[i, zh, 1 - zp, :16].astype(BF16)
-            value_ref[zh, zm] = total[i, zh, 1 - zp, 16:].astype(BF16)
+            keep_ref[zh, zm] = jnp.where(zp == 0, value[zh, 0], value[zh, 1])
+            away = jnp.where(zp == 0, value[zh, 1], value[zh, 0]).astype(BF16)
+            key_ref[zh, zm] = away[:16]
+            value_ref[zh, zm] = away[16:]
 
 
 def input_body(place, own, twin, w0, w1, w2, w3, keep_ref, out1, out2, out3, weight):
@@ -187,7 +188,6 @@
         weight_body,
         (shape((4, 2, 32, 1024), F32),) + (shape((4, 2, 16, 1024), BF16),) * 2,
         [SMEM] + [VMEM] * 6,
-        scratch=[pltpu.VMEM((2, 4, 2, 32, 1024), F32)],
         flops=10**11,
     )(place, own, twin, inputs, *others)
     key, value = shift_by_core(key, RING, -1), shift_by_core(value, RING, 1)

time: 137 us -> 137 us (level)
  no operation moved by 1% of the time
where the time goes in v8:
time: 137 us; the launch traced here: 136 us
  starting transfers between devices  72.3 us (53%)
  blocking collectives  34.9 us (25%)
  waiting for transfers between devices  13.6 us (10%)
  Pallas kernels  9.03 us (7%)
  local copies, waits for them, and re-layouts  5.24 us (4%)
    ppermute x9, starting transfers between devices, shift_by_core(): return lax.ppermute(value, (*axes, 'c'), pairs)  33.4 us
    all_to_all x1, blocking collectives, spread(): return lax.all_to_all(copies, axes, 0, 0, tiled=True)  17.9 us
    all_to_all x1, blocking collectives, per_device(): peaks = lax.all_to_all(peaks, ('x', *TENSOR), 0, 0, tiled=True)  17 us
    ppermute x9, waiting for transfers between devices, shift_by_core(): return lax.ppermute(value, (*axes, 'c'), pairs)  13.1 us
    all_to_all x1, starting transfers between devices, per_device(): weight = lax.all_to_all(weight, 'zh', 0, 0, tiled=True)  13 us
    all_to_all x1, starting transfers between devices, per_device(): own = lax.all_to_all(own.reshape(16, 64, 192), ('x', 'y'), 0, 0, tiled=True)  7.73 us
    ppermute x1, starting transfers between devices, per_device(): twin = lax.ppermute(own, 'c', [(0, 1), (1, 0)])  7.03 us
    ppermute x2, starting transfers between devices, shift(): lax.ppermute(value, axes, [(i, (i + by) % count) for i in range(count)])  5.74 us
  transfers between devices with their start and end apart: 15, of which 4 were waited for; matrix products, arithmetic and copies ran while one was open for 0% of the time, Pallas kernels for 4%

profile of v8, /device:TPU:1, one launch (start us, length us, event | category | flops | bytes accessed | tf_op | source)
XLA Modules:
  0.0 136.1 jit_solution(15421780289122193612)
XLA Ops:
  0.6 2.4 %shard_map.119 = (bf16[4,4,64,192]{3,2,1,0:T(8,128)(2,1)}, bf16[192,1024]{1,0:T(8,128)(2,1)}, bf16[4,32,1024]{2,1,0:T(8,128)(2,1)}) custom-call(bf16[192,128]{1,0:T(8,128)(2,1)} %refs_0_.1, bf16[192,128]{1,0:T(8,128)(2,1)} %refs_1_.1, bf16[192,1024]{1,0:T(8,128)(2,1)} %refs_2_.1, f32[8,192]{1,0:T(8,128)} %bitcast.23, bf16[16,1024]{1,0:T(8,128)(2,1)} %bitcast.21, ...), custom_call_target="tpu_custom_call" | custom-call | tf_op jit(solution)/shard_map/pallas_call | solution.py:164
  3.0 0.0 copy-start
  3.1 7.7 %all-to-all-start = ((bf16[16,64,192]{2,1,0:T(8,128)(2,1)}), bf16[16,64,192]{2,1,0:T(8,128)(2,1)S(1)}, u32[]{:S(2)}, u32[]{:S(2)}) async-start(bf16[16,64,192]{2,1,0:T(8,128)(2,1)} %bitcast.20), calls=%async_computation | async-start | bytes 1048576 | tf_op jit(solution)/shard_map/all_to_all | solution.py:173
  10.8 0.0 copy-done
  10.8 4.5 %collective-permute-start.1 = (bf16[192,1024]{1,0:T(8,128)(2,1)S(1)}, bf16[192,1024]{1,0:T(8,128)(2,1)S(1)}, u32[]{:S(2)}, u32[]{:S(2)}) collective-permute-start(bf16[192,1024]{1,0:T(8,128)(2,1)S(1)} %copy-done), channel_id=1, source_target_pairs={{0,8},{1,25},{8,16},{9,1},{16,24},{17,9},{24,0},{25,17},{2,10},{3,... | collective-permute-start | bytes 1179656 | tf_op jit(solution)/shard_map/ppermute | solution.py:48
  15.3 2.5 %collective-permute-start.2 = (bf16[192,1024]{1,0:T(8,128)(2,1)S(1)}, bf16[192,1024]{1,0:T(8,128)(2,1)S(1)}, u32[]{:S(2)}, u32[]{:S(2)}) collective-permute-start(bf16[192,1024]{1,0:T(8,128)(2,1)S(1)} %copy-done), channel_id=1, source_target_pairs={{0,16},{8,24},{16,0},{24,8},{1,17},{9,25},{17,1},{25,9},{2,18},{10... | collective-permute-start | bytes 1179656 | tf_op jit(solution)/shard_map/ppermute | solution.py:38
  17.8 2.5 %collective-permute-start.3 = (bf16[192,1024]{1,0:T(8,128)(2,1)S(1)}, bf16[192,1024]{1,0:T(8,128)(2,1)S(1)}, u32[]{:S(2)}, u32[]{:S(2)}) collective-permute-start(bf16[192,1024]{1,0:T(8,128)(2,1)S(1)} %copy-done), channel_id=1, source_target_pairs={{0,24},{1,9},{8,0},{9,17},{16,8},{17,25},{24,16},{25,1},{2,26},{3,... | collective-permute-start | bytes 1179656 | tf_op jit(solution)/shard_map/ppermute | solution.py:48
  20.3 0.0 all-to-all-done
  20.3 7.0 %collective-permute-start = (bf16[4,256,192]{2,1,0:T(8,128)(2,1)S(1)}, bf16[4,256,192]{2,1,0:T(8,128)(2,1)S(1)}, u32[]{:S(2)}, u32[]{:S(2)}) collective-permute-start(bf16[4,256,192]{2,1,0:T(8,128)(2,1)S(1)} %bitcast.15), channel_id=1, source_target_pairs={{0,1},{1,0},{2,3},{3,2},{4,5},{5,4},{6,7},{7,6},{8,9},{9,8},{10,11... | collective-permute-start | bytes 1179656 | tf_op jit(solution)/shard_map/ppermute | solution.py:175
  27.3 0.1 pad_add_fusion.place
  27.4 13.0 %all-to-all-start.2 = ((bf16[4,32,1024]{2,1,0:T(8,128)(2,1)}), bf16[4,32,1024]{2,1,0:T(8,128)(2,1)S(1)}, u32[]{:S(2)}, u32[]{:S(2)}) async-start(bf16[4,32,1024]{2,1,0:T(8,128)(2,1)} %get-tuple-element.32), calls=%async_computation.2 | async-start | bytes 524288 | tf_op jit(solution)/shard_map/all_to_all | solution.py:185
  40.4 0.0 collective-permute-done.1.x1
  40.4 0.7 copy-done.1
  41.1 0.0 collective-permute-done.2.x2
  41.1 0.7 copy-done.3
  41.9 0.0 collective-permute-done.3.x3
  41.9 0.7 copy-done.5
  42.6 0.0 collective-permute-done.twin
  42.6 1.0 copy-done.2
  43.6 1.0 copy-done.4
  44.6 1.0 copy-done.6
  45.6 2.4 %shard_map.120 = (f32[4,2,32,1024]{3,2,1,0:T(8,128)S(1)}, bf16[4,2,16,1024]{3,2,1,0:T(8,128)(2,1)}, bf16[4,2,16,1024]{3,2,1,0:T(8,128)(2,1)}) custom-call(s32[4]{0:T(128)S(1)} %pad_add_fusion.place, bf16[4,256,192]{2,1,0:T(8,128)(2,1)S(1)} %bitcast.16, bf16[4,256,192]{2,1,0:T(8,128)(2,1)S(1)} %collective-permute-done.twin, bf16[192,1024]{1,0:T(8,128)(2,1)S(1)} %copy-done, ...), custom_call_target="tpu_custom_call" | custom-call | flops 99999997952 | tf_op jit(solution)/shard_map/pallas_call | solution.py:187
  48.0 2.6 %collective-permute-start.4 = (bf16[4,2,16,1024]{3,2,1,0:T(8,128)(2,1)}, bf16[4,2,16,1024]{3,2,1,0:T(8,128)(2,1)S(1)}, u32[]{:S(2)}, u32[]{:S(2)}) collective-permute-start(bf16[4,2,16,1024]{3,2,1,0:T(8,128)(2,1)} %get-tuple-element.30), channel_id=1, source_target_pairs={{0,480},{1,33},{32,0},{33,65},{64,32},{65,97},{96,64},{97,129},{12... | collective-permute-start | bytes 786440 | tf_op jit(solution)/shard_map/ppermute | solution.py:48
  50.6 5.8 %collective-permute-start.5 = (bf16[4,2,16,1024]{3,2,1,0:T(8,128)(2,1)}, bf16[4,2,16,1024]{3,2,1,0:T(8,128)(2,1)S(1)}, u32[]{:S(2)}, u32[]{:S(2)}) collective-permute-start(bf16[4,2,16,1024]{3,2,1,0:T(8,128)(2,1)} %get-tuple-element.31), channel_id=1, source_target_pairs={{0,32},{1,481},{32,64},{33,1},{64,96},{65,33},{96,128},{97,65},{12... | collective-permute-start | bytes 786440 | tf_op jit(solution)/shard_map/ppermute | solution.py:48
  56.4 0.0 all-to-all-done.2.w0
  56.4 3.4 %collective-permute-start.6 = (bf16[4,32,1024]{2,1,0:T(8,128)(2,1)S(1)}, bf16[4,32,1024]{2,1,0:T(8,128)(2,1)S(1)}, u32[]{:S(2)}, u32[]{:S(2)}) collective-permute-start(bf16[4,32,1024]{2,1,0:T(8,128)(2,1)S(1)} %all-to-all-done.2.w0), channel_id=1, source_target_pairs={{0,32},{1,481},{32,64},{33,1},{64,96},{65,33},{96,128},{97,65},{12... | collective-permute-start | bytes 786440 | tf_op jit(solution)/shard_map/ppermute | solution.py:48
  59.8 5.5 %collective-permute-start.7 = (bf16[4,32,1024]{2,1,0:T(8,128)(2,1)S(1)}, bf16[4,32,1024]{2,1,0:T(8,128)(2,1)S(1)}, u32[]{:S(2)}, u32[]{:S(2)}) collective-permute-start(bf16[4,32,1024]{2,1,0:T(8,128)(2,1)S(1)} %all-to-all-done.2.w0), channel_id=1, source_target_pairs={{0,448},{1,65},{32,480},{33,97},{64,0},{65,129},{96,32},{97,161},{... | collective-permute-start | bytes 786440 | tf_op jit(solution)/shard_map/ppermute | solution.py:48
  65.3 2.6 %collective-permute-start.8 = (bf16[4,32,1024]{2,1,0:T(8,128)(2,1)S(1)}, bf16[4,32,1024]{2,1,0:T(8,128)(2,1)}, u32[]{:S(2)}, u32[]{:S(2)}) collective-permute-start(bf16[4,32,1024]{2,1,0:T(8,128)(2,1)S(1)} %all-to-all-done.2.w0), channel_id=1, source_target_pairs={{0,480},{1,33},{32,0},{33,65},{64,32},{65,97},{96,64},{97,129},{12... | collective-permute-start | bytes 786440 | tf_op jit(solution)/shard_map/ppermute | solution.py:48
  68.0 0.0 collective-permute-done.4.key_ref
  68.0 0.0 collective-permute-done.5.value_ref
  68.0 0.9 shard_map.121
  68.9 5.5 %all-to-all-start.1 = ((bf16[8,32,1024]{2,1,0:T(8,128)(2,1)}), bf16[8,32,1024]{2,1,0:T(8,128)(2,1)S(1)}, u32[]{:S(2)}, u32[]{:S(2)}) async-start(bf16[8,32,1024]{2,1,0:T(8,128)(2,1)} %shard_map.121), calls=%async_computation.1 | async-start | bytes 1048576 | tf_op jit(solution)/shard_map/all_to_all | solution.py:196
  74.4 0.0 collective-permute-done.6.w1
  74.4 0.0 collective-permute-done.7.w2
  74.4 2.7 %collective-permute-done.8.w3 = bf16[4,32,1024]{2,1,0:T(8,128)(2,1)} collective-permute-done((bf16[4,32,1024]{2,1,0:T(8,128)(2,1)S(1)}, bf16[4,32,1024]{2,1,0:T(8,128)(2,1)}, u32[]{:S(2)}, u32[]{:S(2)}) %collective-permute-start.8) | collective-permute-done | bytes 262176 | tf_op jit(solution)/shard_map/ppermute | solution.py:48
  77.1 2.1 %shard_map.122 = (f32[192,1024]{1,0:T(8,128)S(1)}, bf16[192,1024]{1,0:T(8,128)(2,1)S(1)}, bf16[192,1024]{1,0:T(8,128)(2,1)S(1)}, bf16[192,1024]{1,0:T(8,128)(2,1)S(1)}) custom-call(s32[4]{0:T(128)S(1)} %pad_add_fusion.place, bf16[4,256,192]{2,1,0:T(8,128)(2,1)S(1)} %bitcast.17, bf16[4,256,192]{2,1,0:T(8,128)(2,1)S(1)} %collective-permute-done.twin, ...), custom_call_target="tpu_custom_call" | custom-call | flops 99999997952 | tf_op jit(solution)/shard_map/pallas_call | solution.py:198
  79.2 3.3 %collective-permute-start.10 = (bf16[192,1024]{1,0:T(8,128)(2,1)S(1)}, bf16[192,1024]{1,0:T(8,128)(2,1)S(1)}, u32[]{:S(2)}, u32[]{:S(2)}) collective-permute-start(bf16[192,1024]{1,0:T(8,128)(2,1)S(1)} %get-tuple-element.35), channel_id=1, source_target_pairs={{0,16},{8,24},{16,0},{24,8},{1,17},{9,25},{17,1},{25,9},{2,18},{10... | collective-permute-start | bytes 1179656 | tf_op jit(solution)/shard_map/ppermute | solution.py:38
  82.4 1.9 %collective-permute-start.11 = (bf16[192,1024]{1,0:T(8,128)(2,1)S(1)}, bf16[192,1024]{1,0:T(8,128)(2,1)S(1)}, u32[]{:S(2)}, u32[]{:S(2)}) collective-permute-start(bf16[192,1024]{1,0:T(8,128)(2,1)S(1)} %get-tuple-element.36), channel_id=1, source_target_pairs={{0,24},{1,9},{8,0},{9,17},{16,8},{17,25},{24,16},{25,1},{2,26},{3,... | collective-permute-start | bytes 1179656 | tf_op jit(solution)/shard_map/ppermute | solution.py:48
  84.3 4.6 %collective-permute-start.9 = (bf16[192,1024]{1,0:T(8,128)(2,1)S(1)}, bf16[192,1024]{1,0:T(8,128)(2,1)S(1)}, u32[]{:S(2)}, u32[]{:S(2)}) collective-permute-start(bf16[192,1024]{1,0:T(8,128)(2,1)S(1)} %get-tuple-element.34), channel_id=1, source_target_pairs={{0,8},{1,25},{8,16},{9,1},{16,24},{17,9},{24,0},{25,17},{2,10},{3,... | collective-permute-start | bytes 1179656 | tf_op jit(solution)/shard_map/ppermute | solution.py:48
  88.9 0.5 collective-permute-done.10.r2
  89.5 6.9 %collective-permute-done.11.r3 = bf16[192,1024]{1,0:T(8,128)(2,1)S(1)} collective-permute-done((bf16[192,1024]{1,0:T(8,128)(2,1)S(1)}, bf16[192,1024]{1,0:T(8,128)(2,1)S(1)}, u32[]{:S(2)}, u32[]{:S(2)}) %collective-permute-start.11) | collective-permute-done | bytes 393248 | tf_op jit(solution)/shard_map/ppermute | solution.py:48
  96.4 3.5 %collective-permute-done.9.r1 = bf16[192,1024]{1,0:T(8,128)(2,1)S(1)} collective-permute-done((bf16[192,1024]{1,0:T(8,128)(2,1)S(1)}, bf16[192,1024]{1,0:T(8,128)(2,1)S(1)}, u32[]{:S(2)}, u32[]{:S(2)}) %collective-permute-start.9) | collective-permute-done | bytes 393248 | tf_op jit(solution)/shard_map/ppermute | solution.py:48
  99.8 0.0 all-to-all-done.1.far_ref
  99.8 0.4 shard_map.123
  100.2 17.0 %all_to_all.32 = f32[32,1,128]{2,1,0:T(1,128)S(1)} all-to-all(f32[32,1,128]{2,1,0:T(1,128)S(1)} %bitcast.19), channel_id=1, replica_groups=mesh['zh'=4,'zm'=2,'zp'=2,'x'=4,'y'=4,'c'=2] {'x','y','c'}, dimensions={0} | all-to-all | bytes 32768 | tf_op jit(solution)/shard_map/all_to_all | solution.py:216
  117.2 0.1 reduce_max.9
  117.2 17.9 %all_to_all.33 = f32[16,1,128]{2,1,0:T(1,128)S(1)} all-to-all(f32[16,1,128]{2,1,0:T(1,128)S(1)} %broadcast_in_dim.2), channel_id=1, replica_groups=mesh['zh'=4,'zm'=2,'zp'=2,'x'=4,'y'=4,'c'=2] {'zh','zm','zp'}, dimensions={0} | all-to-all | bytes 16384 | tf_op jit(solution)/shard_map/all_to_all | solution.py:54
  135.2 1.0 shard_map.124
  (7 shorter events, 0.0 us)
Async XLA Ops:
  3.0 7.8 %copy-start = (bf16[192,1024]{1,0:T(8,128)(2,1)S(1)}, bf16[192,1024]{1,0:T(8,128)(2,1)}, u32[]{:S(2)}) copy-start(bf16[192,1024]{1,0:T(8,128)(2,1)} %get-tuple-element.28.x0) | copy-start | bytes 1179652
  3.1 17.2 %all-to-all-start = ((bf16[16,64,192]{2,1,0:T(8,128)(2,1)}), bf16[16,64,192]{2,1,0:T(8,128)(2,1)S(1)}, u32[]{:S(2)}, u32[]{:S(2)}) async-start(bf16[16,64,192]{2,1,0:T(8,128)(2,1)} %bitcast.20), calls=%async_computation | async-start | bytes 1048576 | tf_op jit(solution)/shard_map/all_to_all | solution.py:173
  10.8 29.6 %collective-permute-start.1 = (bf16[192,1024]{1,0:T(8,128)(2,1)S(1)}, bf16[192,1024]{1,0:T(8,128)(2,1)S(1)}, u32[]{:S(2)}, u32[]{:S(2)}) collective-permute-start(bf16[192,1024]{1,0:T(8,128)(2,1)S(1)} %copy-done), channel_id=1, source_target_pairs={{0,8},{1,25},{8,16},{9,1},{16,24},{17,9},{24,0},{25,17},{2,10},{3,... | collective-permute-start | bytes 1179656 | tf_op jit(solution)/shard_map/ppermute | solution.py:48
  15.3 25.8 %collective-permute-start.2 = (bf16[192,1024]{1,0:T(8,128)(2,1)S(1)}, bf16[192,1024]{1,0:T(8,128)(2,1)S(1)}, u32[]{:S(2)}, u32[]{:S(2)}) collective-permute-start(bf16[192,1024]{1,0:T(8,128)(2,1)S(1)} %copy-done), channel_id=1, source_target_pairs={{0,16},{8,24},{16,0},{24,8},{1,17},{9,25},{17,1},{25,9},{2,18},{10... | collective-permute-start | bytes 1179656 | tf_op jit(solution)/shard_map/ppermute | solution.py:38
  17.8 24.1 %collective-permute-start.3 = (bf16[192,1024]{1,0:T(8,128)(2,1)S(1)}, bf16[192,1024]{1,0:T(8,128)(2,1)S(1)}, u32[]{:S(2)}, u32[]{:S(2)}) collective-permute-start(bf16[192,1024]{1,0:T(8,128)(2,1)S(1)} %copy-done), channel_id=1, source_target_pairs={{0,24},{1,9},{8,0},{9,17},{16,8},{17,25},{24,16},{25,1},{2,26},{3,... | collective-permute-start | bytes 1179656 | tf_op jit(solution)/shard_map/ppermute | solution.py:48
  20.3 22.3 %collective-permute-start = (bf16[4,256,192]{2,1,0:T(8,128)(2,1)S(1)}, bf16[4,256,192]{2,1,0:T(8,128)(2,1)S(1)}, u32[]{:S(2)}, u32[]{:S(2)}) collective-permute-start(bf16[4,256,192]{2,1,0:T(8,128)(2,1)S(1)} %bitcast.15), channel_id=1, source_target_pairs={{0,1},{1,0},{2,3},{3,2},{4,5},{5,4},{6,7},{7,6},{8,9},{9,8},{10,11... | collective-permute-start | bytes 1179656 | tf_op jit(solution)/shard_map/ppermute | solution.py:175
  27.4 29.0 %all-to-all-start.2 = ((bf16[4,32,1024]{2,1,0:T(8,128)(2,1)}), bf16[4,32,1024]{2,1,0:T(8,128)(2,1)S(1)}, u32[]{:S(2)}, u32[]{:S(2)}) async-start(bf16[4,32,1024]{2,1,0:T(8,128)(2,1)} %get-tuple-element.32), calls=%async_computation.2 | async-start | bytes 524288 | tf_op jit(solution)/shard_map/all_to_all | solution.py:185
  40.4 0.7 copy-start.1
  41.1 0.7 copy-start.3
  41.9 0.7 copy-start.5
  42.6 1.0 copy-start.2
  43.6 1.0 copy-start.4
  44.6 1.0 copy-start.6
  48.0 20.0 %collective-permute-start.4 = (bf16[4,2,16,1024]{3,2,1,0:T(8,128)(2,1)}, bf16[4,2,16,1024]{3,2,1,0:T(8,128)(2,1)S(1)}, u32[]{:S(2)}, u32[]{:S(2)}) collective-permute-start(bf16[4,2,16,1024]{3,2,1,0:T(8,128)(2,1)} %get-tuple-element.30), channel_id=1, source_target_pairs={{0,480},{1,33},{32,0},{33,65},{64,32},{65,97},{96,64},{97,129},{12... | collective-permute-start | bytes 786440 | tf_op jit(solution)/shard_map/ppermute | solution.py:48
  50.6 17.4 %collective-permute-start.5 = (bf16[4,2,16,1024]{3,2,1,0:T(8,128)(2,1)}, bf16[4,2,16,1024]{3,2,1,0:T(8,128)(2,1)S(1)}, u32[]{:S(2)}, u32[]{:S(2)}) collective-permute-start(bf16[4,2,16,1024]{3,2,1,0:T(8,128)(2,1)} %get-tuple-element.31), channel_id=1, source_target_pairs={{0,32},{1,481},{32,64},{33,1},{64,96},{65,33},{96,128},{97,65},{12... | collective-permute-start | bytes 786440 | tf_op jit(solution)/shard_map/ppermute | solution.py:48
  56.4 17.9 %collective-permute-start.6 = (bf16[4,32,1024]{2,1,0:T(8,128)(2,1)S(1)}, bf16[4,32,1024]{2,1,0:T(8,128)(2,1)S(1)}, u32[]{:S(2)}, u32[]{:S(2)}) collective-permute-start(bf16[4,32,1024]{2,1,0:T(8,128)(2,1)S(1)} %all-to-all-done.2.w0), channel_id=1, source_target_pairs={{0,32},{1,481},{32,64},{33,1},{64,96},{65,33},{96,128},{97,65},{12... | collective-permute-start | bytes 786440 | tf_op jit(solution)/shard_map/ppermute | solution.py:48
  59.8 14.6 %collective-permute-start.7 = (bf16[4,32,1024]{2,1,0:T(8,128)(2,1)S(1)}, bf16[4,32,1024]{2,1,0:T(8,128)(2,1)S(1)}, u32[]{:S(2)}, u32[]{:S(2)}) collective-permute-start(bf16[4,32,1024]{2,1,0:T(8,128)(2,1)S(1)} %all-to-all-done.2.w0), channel_id=1, source_target_pairs={{0,448},{1,65},{32,480},{33,97},{64,0},{65,129},{96,32},{97,161},{... | collective-permute-start | bytes 786440 | tf_op jit(solution)/shard_map/ppermute | solution.py:48
  65.3 11.7 %collective-permute-start.8 = (bf16[4,32,1024]{2,1,0:T(8,128)(2,1)S(1)}, bf16[4,32,1024]{2,1,0:T(8,128)(2,1)}, u32[]{:S(2)}, u32[]{:S(2)}) collective-permute-start(bf16[4,32,1024]{2,1,0:T(8,128)(2,1)S(1)} %all-to-all-done.2.w0), channel_id=1, source_target_pairs={{0,480},{1,33},{32,0},{33,65},{64,32},{65,97},{96,64},{97,129},{12... | collective-permute-start | bytes 786440 | tf_op jit(solution)/shard_map/ppermute | solution.py:48
  68.9 30.9 %all-to-all-start.1 = ((bf16[8,32,1024]{2,1,0:T(8,128)(2,1)}), bf16[8,32,1024]{2,1,0:T(8,128)(2,1)S(1)}, u32[]{:S(2)}, u32[]{:S(2)}) async-start(bf16[8,32,1024]{2,1,0:T(8,128)(2,1)} %shard_map.121), calls=%async_computation.1 | async-start | bytes 1048576 | tf_op jit(solution)/shard_map/all_to_all | solution.py:196
  79.2 10.3 %collective-permute-start.10 = (bf16[192,1024]{1,0:T(8,128)(2,1)S(1)}, bf16[192,1024]{1,0:T(8,128)(2,1)S(1)}, u32[]{:S(2)}, u32[]{:S(2)}) collective-permute-start(bf16[192,1024]{1,0:T(8,128)(2,1)S(1)} %get-tuple-element.35), channel_id=1, source_target_pairs={{0,16},{8,24},{16,0},{24,8},{1,17},{9,25},{17,1},{25,9},{2,18},{10... | collective-permute-start | bytes 1179656 | tf_op jit(solution)/shard_map/ppermute | solution.py:38
  82.4 14.0 %collective-permute-start.11 = (bf16[192,1024]{1,0:T(8,128)(2,1)S(1)}, bf16[192,1024]{1,0:T(8,128)(2,1)S(1)}, u32[]{:S(2)}, u32[]{:S(2)}) collective-permute-start(bf16[192,1024]{1,0:T(8,128)(2,1)S(1)} %get-tuple-element.36), channel_id=1, source_target_pairs={{0,24},{1,9},{8,0},{9,17},{16,8},{17,25},{24,16},{25,1},{2,26},{3,... | collective-permute-start | bytes 1179656 | tf_op jit(solution)/shard_map/ppermute | solution.py:48
  84.3 15.5 %collective-permute-start.9 = (bf16[192,1024]{1,0:T(8,128)(2,1)S(1)}, bf16[192,1024]{1,0:T(8,128)(2,1)S(1)}, u32[]{:S(2)}, u32[]{:S(2)}) collective-permute-start(bf16[192,1024]{1,0:T(8,128)(2,1)S(1)} %get-tuple-element.34), channel_id=1, source_target_pairs={{0,8},{1,25},{8,16},{9,1},{16,24},{17,9},{24,0},{25,17},{2,10},{3,... | collective-permute-start | bytes 1179656 | tf_op jit(solution)/shard_map/ppermute | solution.py:48

commit v9 on v7

--- a/solution.py
+++ b/solution.py
@@ -103,7 +103,7 @@
 
 def input_body(place, own, twin, w0, w1, w2, w3, keep_ref, out1, out2, out3, weight):
     x, zl, core = place[0], place[1] * 2 + place[2], place[3]
-    for k, ref in ((0, w0), (3 - 2 * core, w1), (2, w2), (1 + 2 * core, w3)):
+    for k, ref in ((0, w0), (1 + 2 * core, w1), (2, w2), (3 - 2 * core, w3)):
         group = lax.rem(zl + k, 4)
         half, zp = lax.rem(group // 2 + core, 2), lax.rem(group, 2)
         for zh in range(4):
@@ -191,7 +191,7 @@
         flops=10**11,
     )(place, own, twin, inputs, *others)
     key, value = shift_by_core(key, RING, -1), shift_by_core(value, RING, 1)
-    weights = [weight] + [shift_by_core(weight, RING, by) for by in (1, -2, -1)]
+    weights = [weight] + [shift_by_core(weight, RING, by) for by in (-1, 2, 1)]
     part = kernel_call(near_body, shape((8, 32, 1024), BF16), [VMEM] * 3)(keep, key, value)
     far = lax.all_to_all(part, ("zh", "zm"), 0, 0, tiled=True)
 

time: 137 us -> 139 us (1.015)
    all_to_all x1, blocking collectives: 18.6 us -> 22.1 us  [spread(): return lax.all_to_all(copies, axes, 0, 0, tiled=True)]
    all_to_all x1, blocking collectives: 16.4 us -> 13 us  [per_device(): peaks = lax.all_to_all(peaks, ('x', *TENSOR), 0, 0, tiled=True)]
    ppermute x9, waiting for transfers between devices: 13 us -> 11.1 us  [shift_by_core(): return lax.ppermute(value, (*axes, 'c'), pairs)]
    all_to_all x1, waiting for transfers between devices: 0.01 us -> 1.81 us  [per_device(): far = lax.all_to_all(part, ('zh', 'zm'), 0, 0, tiled=True)]
  transfers between devices with their start and end apart: 15 -> 15, of which waited for: 4 -> 6; matrix products, arithmetic and copies ran while one was open for 0% -> 0% of each run, Pallas kernels for 4% -> 4%
where the time goes in v9:
time: 139 us; the launch traced here: 138 us
  starting transfers between devices  73.6 us (53%)
  blocking collectives  35.1 us (25%)
  waiting for transfers between devices  14.2 us (10%)
  Pallas kernels  9.1 us (7%)
  local copies, waits for them, and re-layouts  5.24 us (4%)
    ppermute x9, starting transfers between devices, shift_by_core(): return lax.ppermute(value, (*axes, 'c'), pairs)  34.2 us
    all_to_all x1, blocking collectives, spread(): return lax.all_to_all(copies, axes, 0, 0, tiled=True)  22.1 us
    all_to_all x1, blocking collectives, per_device(): peaks = lax.all_to_all(peaks, ('x', *TENSOR), 0, 0, tiled=True)  13 us
    all_to_all x1, starting transfers between devices, per_device(): weight = lax.all_to_all(weight, 'zh', 0, 0, tiled=True)  13 us
    ppermute x9, waiting for transfers between devices, shift_by_core(): return lax.ppermute(value, (*axes, 'c'), pairs)  11.1 us
    all_to_all x1, starting transfers between devices, per_device(): own = lax.all_to_all(own.reshape(16, 64, 192), ('x', 'y'), 0, 0, tiled=True)  7.73 us
    ppermute x1, starting transfers between devices, per_device(): twin = lax.ppermute(own, 'c', [(0, 1), (1, 0)])  7.03 us
    all_to_all x1, starting transfers between devices, per_device(): far = lax.all_to_all(part, ('zh', 'zm'), 0, 0, tiled=True)  5.88 us
  transfers between devices with their start and end apart: 15, of which 6 were waited for; matrix products, arithmetic and copies ran while one was open for 0% of the time, Pallas kernels for 4%

profile of v9, /device:TPU:1, one launch (start us, length us, event | category | flops | bytes accessed | tf_op | source)
XLA Modules:
  0.0 138.2 jit_solution(8275337027724181129)
XLA Ops:
  0.6 2.4 %shard_map.119 = (bf16[4,4,64,192]{3,2,1,0:T(8,128)(2,1)}, bf16[192,1024]{1,0:T(8,128)(2,1)}, bf16[4,32,1024]{2,1,0:T(8,128)(2,1)}) custom-call(bf16[192,128]{1,0:T(8,128)(2,1)} %refs_0_.1, bf16[192,128]{1,0:T(8,128)(2,1)} %refs_1_.1, bf16[192,1024]{1,0:T(8,128)(2,1)} %refs_2_.1, f32[8,192]{1,0:T(8,128)} %bitcast.23, bf16[16,1024]{1,0:T(8,128)(2,1)} %bitcast.21, ...), custom_call_target="tpu_custom_call" | custom-call | tf_op jit(solution)/shard_map/pallas_call | solution.py:163
  3.0 0.0 copy-start
  3.1 7.7 %all-to-all-start = ((bf16[16,64,192]{2,1,0:T(8,128)(2,1)}), bf16[16,64,192]{2,1,0:T(8,128)(2,1)S(1)}, u32[]{:S(2)}, u32[]{:S(2)}) async-start(bf16[16,64,192]{2,1,0:T(8,128)(2,1)} %bitcast.20), calls=%async_computation | async-start | bytes 1048576 | tf_op jit(solution)/shard_map/all_to_all | solution.py:172
  10.8 0.0 copy-done
  10.8 4.5 %collective-permute-start.1 = (bf16[192,1024]{1,0:T(8,128)(2,1)S(1)}, bf16[192,1024]{1,0:T(8,128)(2,1)S(1)}, u32[]{:S(2)}, u32[]{:S(2)}) collective-permute-start(bf16[192,1024]{1,0:T(8,128)(2,1)S(1)} %copy-done), channel_id=1, source_target_pairs={{0,8},{1,25},{8,16},{9,1},{16,24},{17,9},{24,0},{25,17},{2,10},{3,... | collective-permute-start | bytes 1179656 | tf_op jit(solution)/shard_map/ppermute | solution.py:48
  15.3 2.5 %collective-permute-start.2 = (bf16[192,1024]{1,0:T(8,128)(2,1)S(1)}, bf16[192,1024]{1,0:T(8,128)(2,1)S(1)}, u32[]{:S(2)}, u32[]{:S(2)}) collective-permute-start(bf16[192,1024]{1,0:T(8,128)(2,1)S(1)} %copy-done), channel_id=1, source_target_pairs={{0,16},{8,24},{16,0},{24,8},{1,17},{9,25},{17,1},{25,9},{2,18},{10... | collective-permute-start | bytes 1179656 | tf_op jit(solution)/shard_map/ppermute | solution.py:38
  17.8 2.5 %collective-permute-start.3 = (bf16[192,1024]{1,0:T(8,128)(2,1)S(1)}, bf16[192,1024]{1,0:T(8,128)(2,1)S(1)}, u32[]{:S(2)}, u32[]{:S(2)}) collective-permute-start(bf16[192,1024]{1,0:T(8,128)(2,1)S(1)} %copy-done), channel_id=1, source_target_pairs={{0,24},{1,9},{8,0},{9,17},{16,8},{17,25},{24,16},{25,1},{2,26},{3,... | collective-permute-start | bytes 1179656 | tf_op jit(solution)/shard_map/ppermute | solution.py:48
  20.3 0.0 all-to-all-done
  20.3 7.0 %collective-permute-start = (bf16[4,256,192]{2,1,0:T(8,128)(2,1)S(1)}, bf16[4,256,192]{2,1,0:T(8,128)(2,1)S(1)}, u32[]{:S(2)}, u32[]{:S(2)}) collective-permute-start(bf16[4,256,192]{2,1,0:T(8,128)(2,1)S(1)} %bitcast.15), channel_id=1, source_target_pairs={{0,1},{1,0},{2,3},{3,2},{4,5},{5,4},{6,7},{7,6},{8,9},{9,8},{10,11... | collective-permute-start | bytes 1179656 | tf_op jit(solution)/shard_map/ppermute | solution.py:174
  27.3 0.1 pad_add_fusion.place
  27.4 13.0 %all-to-all-start.2 = ((bf16[4,32,1024]{2,1,0:T(8,128)(2,1)}), bf16[4,32,1024]{2,1,0:T(8,128)(2,1)S(1)}, u32[]{:S(2)}, u32[]{:S(2)}) async-start(bf16[4,32,1024]{2,1,0:T(8,128)(2,1)} %get-tuple-element.32), calls=%async_computation.2 | async-start | bytes 524288 | tf_op jit(solution)/shard_map/all_to_all | solution.py:184
  40.4 0.0 collective-permute-done.1.x1
  40.4 0.7 copy-done.1
  41.1 0.0 collective-permute-done.2.x2
  41.1 0.7 copy-done.3
  41.9 0.0 collective-permute-done.3.x3
  41.9 0.7 copy-done.5
  42.6 0.0 collective-permute-done.twin
  42.6 1.0 copy-done.2
  43.6 1.0 copy-done.4
  44.6 1.0 copy-done.6
  45.6 2.4 %shard_map.120 = (f32[4,2,32,1024]{3,2,1,0:T(8,128)S(1)}, bf16[4,2,16,1024]{3,2,1,0:T(8,128)(2,1)}, bf16[4,2,16,1024]{3,2,1,0:T(8,128)(2,1)}) custom-call(s32[4]{0:T(128)S(1)} %pad_add_fusion.place, bf16[4,256,192]{2,1,0:T(8,128)(2,1)S(1)} %bitcast.16, bf16[4,256,192]{2,1,0:T(8,128)(2,1)S(1)} %collective-permute-done.twin, bf16[192,1024]{1,0:T(8,128)(2,1)S(1)} %copy-done, ...), custom_call_target="tpu_custom_call" | custom-call | flops 99999997952 | tf_op jit(solution)/shard_map/pallas_call | solution.py:186
  48.1 2.6 %collective-permute-start.4 = (bf16[4,2,16,1024]{3,2,1,0:T(8,128)(2,1)}, bf16[4,2,16,1024]{3,2,1,0:T(8,128)(2,1)S(1)}, u32[]{:S(2)}, u32[]{:S(2)}) collective-permute-start(bf16[4,2,16,1024]{3,2,1,0:T(8,128)(2,1)} %get-tuple-element.30), channel_id=1, source_target_pairs={{0,480},{1,33},{32,0},{33,65},{64,32},{65,97},{96,64},{97,129},{12... | collective-permute-start | bytes 786440 | tf_op jit(solution)/shard_map/ppermute | solution.py:48
  50.7 5.8 %collective-permute-start.5 = (bf16[4,2,16,1024]{3,2,1,0:T(8,128)(2,1)}, bf16[4,2,16,1024]{3,2,1,0:T(8,128)(2,1)S(1)}, u32[]{:S(2)}, u32[]{:S(2)}) collective-permute-start(bf16[4,2,16,1024]{3,2,1,0:T(8,128)(2,1)} %get-tuple-element.31), channel_id=1, source_target_pairs={{0,32},{1,481},{32,64},{33,1},{64,96},{65,33},{96,128},{97,65},{12... | collective-permute-start | bytes 786440 | tf_op jit(solution)/shard_map/ppermute | solution.py:48
  56.5 0.0 all-to-all-done.2.w0
  56.5 5.7 %collective-permute-start.6 = (bf16[4,32,1024]{2,1,0:T(8,128)(2,1)S(1)}, bf16[4,32,1024]{2,1,0:T(8,128)(2,1)S(1)}, u32[]{:S(2)}, u32[]{:S(2)}) collective-permute-start(bf16[4,32,1024]{2,1,0:T(8,128)(2,1)S(1)} %all-to-all-done.2.w0), channel_id=1, source_target_pairs={{0,480},{1,33},{32,0},{33,65},{64,32},{65,97},{96,64},{97,129},{12... | collective-permute-start | bytes 786440 | tf_op jit(solution)/shard_map/ppermute | solution.py:48
  62.3 3.2 %collective-permute-start.7 = (bf16[4,32,1024]{2,1,0:T(8,128)(2,1)S(1)}, bf16[4,32,1024]{2,1,0:T(8,128)(2,1)S(1)}, u32[]{:S(2)}, u32[]{:S(2)}) collective-permute-start(bf16[4,32,1024]{2,1,0:T(8,128)(2,1)S(1)} %all-to-all-done.2.w0), channel_id=1, source_target_pairs={{0,64},{1,449},{32,96},{33,481},{64,128},{65,1},{96,160},{97,33},{... | collective-permute-start | bytes 786440 | tf_op jit(solution)/shard_map/ppermute | solution.py:48
  65.5 3.4 %collective-permute-start.8 = (bf16[4,32,1024]{2,1,0:T(8,128)(2,1)S(1)}, bf16[4,32,1024]{2,1,0:T(8,128)(2,1)}, u32[]{:S(2)}, u32[]{:S(2)}) collective-permute-start(bf16[4,32,1024]{2,1,0:T(8,128)(2,1)S(1)} %all-to-all-done.2.w0), channel_id=1, source_target_pairs={{0,32},{1,481},{32,64},{33,1},{64,96},{65,33},{96,128},{97,65},{12... | collective-permute-start | bytes 786440 | tf_op jit(solution)/shard_map/ppermute | solution.py:48
  68.8 0.0 collective-permute-done.4.key_ref
  68.9 0.0 collective-permute-done.5.value_ref
  68.9 0.9 shard_map.121
  69.8 5.9 %all-to-all-start.1 = ((bf16[8,32,1024]{2,1,0:T(8,128)(2,1)}), bf16[8,32,1024]{2,1,0:T(8,128)(2,1)S(1)}, u32[]{:S(2)}, u32[]{:S(2)}) async-start(bf16[8,32,1024]{2,1,0:T(8,128)(2,1)} %shard_map.121), calls=%async_computation.1 | async-start | bytes 1048576 | tf_op jit(solution)/shard_map/all_to_all | solution.py:196
  75.7 0.0 collective-permute-done.6.w1
  75.7 0.3 collective-permute-done.7.w2
  76.0 1.5 %collective-permute-done.8.w3 = bf16[4,32,1024]{2,1,0:T(8,128)(2,1)} collective-permute-done((bf16[4,32,1024]{2,1,0:T(8,128)(2,1)S(1)}, bf16[4,32,1024]{2,1,0:T(8,128)(2,1)}, u32[]{:S(2)}, u32[]{:S(2)}) %collective-permute-start.8) | collective-permute-done | bytes 262176 | tf_op jit(solution)/shard_map/ppermute | solution.py:48
  77.4 2.1 %shard_map.122 = (f32[192,1024]{1,0:T(8,128)S(1)}, bf16[192,1024]{1,0:T(8,128)(2,1)S(1)}, bf16[192,1024]{1,0:T(8,128)(2,1)S(1)}, bf16[192,1024]{1,0:T(8,128)(2,1)S(1)}) custom-call(s32[4]{0:T(128)S(1)} %pad_add_fusion.place, bf16[4,256,192]{2,1,0:T(8,128)(2,1)S(1)} %bitcast.17, bf16[4,256,192]{2,1,0:T(8,128)(2,1)S(1)} %collective-permute-done.twin, ...), custom_call_target="tpu_custom_call" | custom-call | flops 99999997952 | tf_op jit(solution)/shard_map/pallas_call | solution.py:198
  79.5 3.3 %collective-permute-start.10 = (bf16[192,1024]{1,0:T(8,128)(2,1)S(1)}, bf16[192,1024]{1,0:T(8,128)(2,1)S(1)}, u32[]{:S(2)}, u32[]{:S(2)}) collective-permute-start(bf16[192,1024]{1,0:T(8,128)(2,1)S(1)} %get-tuple-element.35), channel_id=1, source_target_pairs={{0,16},{8,24},{16,0},{24,8},{1,17},{9,25},{17,1},{25,9},{2,18},{10... | collective-permute-start | bytes 1179656 | tf_op jit(solution)/shard_map/ppermute | solution.py:38
  82.8 1.9 %collective-permute-start.11 = (bf16[192,1024]{1,0:T(8,128)(2,1)S(1)}, bf16[192,1024]{1,0:T(8,128)(2,1)S(1)}, u32[]{:S(2)}, u32[]{:S(2)}) collective-permute-start(bf16[192,1024]{1,0:T(8,128)(2,1)S(1)} %get-tuple-element.36), channel_id=1, source_target_pairs={{0,24},{1,9},{8,0},{9,17},{16,8},{17,25},{24,16},{25,1},{2,26},{3,... | collective-permute-start | bytes 1179656 | tf_op jit(solution)/shard_map/ppermute | solution.py:48
  84.7 4.6 %collective-permute-start.9 = (bf16[192,1024]{1,0:T(8,128)(2,1)S(1)}, bf16[192,1024]{1,0:T(8,128)(2,1)S(1)}, u32[]{:S(2)}, u32[]{:S(2)}) collective-permute-start(bf16[192,1024]{1,0:T(8,128)(2,1)S(1)} %get-tuple-element.34), channel_id=1, source_target_pairs={{0,8},{1,25},{8,16},{9,1},{16,24},{17,9},{24,0},{25,17},{2,10},{3,... | collective-permute-start | bytes 1179656 | tf_op jit(solution)/shard_map/ppermute | solution.py:48
  89.3 1.3 collective-permute-done.10.r2
  90.6 9.1 %collective-permute-done.11.r3 = bf16[192,1024]{1,0:T(8,128)(2,1)S(1)} collective-permute-done((bf16[192,1024]{1,0:T(8,128)(2,1)S(1)}, bf16[192,1024]{1,0:T(8,128)(2,1)S(1)}, u32[]{:S(2)}, u32[]{:S(2)}) %collective-permute-start.11) | collective-permute-done | bytes 393248 | tf_op jit(solution)/shard_map/ppermute | solution.py:48
  99.7 0.1 collective-permute-done.9.r1
  99.8 1.8 %all-to-all-done.1.far_ref = bf16[8,32,1024]{2,1,0:T(8,128)(2,1)S(1)} async-done(((bf16[8,32,1024]{2,1,0:T(8,128)(2,1)}), bf16[8,32,1024]{2,1,0:T(8,128)(2,1)S(1)}, u32[]{:S(2)}, u32[]{:S(2)}) %all-to-all-start.1) | async-done | bytes 524320 | tf_op jit(solution)/shard_map/all_to_all | solution.py:196
  101.7 0.4 shard_map.123
  102.0 13.0 %all_to_all.32 = f32[32,1,128]{2,1,0:T(1,128)S(1)} all-to-all(f32[32,1,128]{2,1,0:T(1,128)S(1)} %bitcast.19), channel_id=1, replica_groups=mesh['zh'=4,'zm'=2,'zp'=2,'x'=4,'y'=4,'c'=2] {'x','y','c'}, dimensions={0} | all-to-all | bytes 32768 | tf_op jit(solution)/shard_map/all_to_all | solution.py:216
  115.1 0.1 reduce_max.9
  115.1 22.1 %all_to_all.33 = f32[16,1,128]{2,1,0:T(1,128)S(1)} all-to-all(f32[16,1,128]{2,1,0:T(1,128)S(1)} %broadcast_in_dim.2), channel_id=1, replica_groups=mesh['zh'=4,'zm'=2,'zp'=2,'x'=4,'y'=4,'c'=2] {'zh','zm','zp'}, dimensions={0} | all-to-all | bytes 16384 | tf_op jit(solution)/shard_map/all_to_all | solution.py:54
  137.2 1.0 shard_map.124
  (7 shorter events, 0.0 us)
Async XLA Ops:
  3.0 7.8 %copy-start = (bf16[192,1024]{1,0:T(8,128)(2,1)S(1)}, bf16[192,1024]{1,0:T(8,128)(2,1)}, u32[]{:S(2)}) copy-start(bf16[192,1024]{1,0:T(8,128)(2,1)} %get-tuple-element.28.x0) | copy-start | bytes 1179652
  3.1 17.2 %all-to-all-start = ((bf16[16,64,192]{2,1,0:T(8,128)(2,1)}), bf16[16,64,192]{2,1,0:T(8,128)(2,1)S(1)}, u32[]{:S(2)}, u32[]{:S(2)}) async-start(bf16[16,64,192]{2,1,0:T(8,128)(2,1)} %bitcast.20), calls=%async_computation | async-start | bytes 1048576 | tf_op jit(solution)/shard_map/all_to_all | solution.py:172
  10.8 29.6 %collective-permute-start.1 = (bf16[192,1024]{1,0:T(8,128)(2,1)S(1)}, bf16[192,1024]{1,0:T(8,128)(2,1)S(1)}, u32[]{:S(2)}, u32[]{:S(2)}) collective-permute-start(bf16[192,1024]{1,0:T(8,128)(2,1)S(1)} %copy-done), channel_id=1, source_target_pairs={{0,8},{1,25},{8,16},{9,1},{16,24},{17,9},{24,0},{25,17},{2,10},{3,... | collective-permute-start | bytes 1179656 | tf_op jit(solution)/shard_map/ppermute | solution.py:48
  15.3 25.8 %collective-permute-start.2 = (bf16[192,1024]{1,0:T(8,128)(2,1)S(1)}, bf16[192,1024]{1,0:T(8,128)(2,1)S(1)}, u32[]{:S(2)}, u32[]{:S(2)}) collective-permute-start(bf16[192,1024]{1,0:T(8,128)(2,1)S(1)} %copy-done), channel_id=1, source_target_pairs={{0,16},{8,24},{16,0},{24,8},{1,17},{9,25},{17,1},{25,9},{2,18},{10... | collective-permute-start | bytes 1179656 | tf_op jit(solution)/shard_map/ppermute | solution.py:38
  17.8 24.1 %collective-permute-start.3 = (bf16[192,1024]{1,0:T(8,128)(2,1)S(1)}, bf16[192,1024]{1,0:T(8,128)(2,1)S(1)}, u32[]{:S(2)}, u32[]{:S(2)}) collective-permute-start(bf16[192,1024]{1,0:T(8,128)(2,1)S(1)} %copy-done), channel_id=1, source_target_pairs={{0,24},{1,9},{8,0},{9,17},{16,8},{17,25},{24,16},{25,1},{2,26},{3,... | collective-permute-start | bytes 1179656 | tf_op jit(solution)/shard_map/ppermute | solution.py:48
  20.3 22.3 %collective-permute-start = (bf16[4,256,192]{2,1,0:T(8,128)(2,1)S(1)}, bf16[4,256,192]{2,1,0:T(8,128)(2,1)S(1)}, u32[]{:S(2)}, u32[]{:S(2)}) collective-permute-start(bf16[4,256,192]{2,1,0:T(8,128)(2,1)S(1)} %bitcast.15), channel_id=1, source_target_pairs={{0,1},{1,0},{2,3},{3,2},{4,5},{5,4},{6,7},{7,6},{8,9},{9,8},{10,11... | collective-permute-start | bytes 1179656 | tf_op jit(solution)/shard_map/ppermute | solution.py:174
  27.4 29.1 %all-to-all-start.2 = ((bf16[4,32,1024]{2,1,0:T(8,128)(2,1)}), bf16[4,32,1024]{2,1,0:T(8,128)(2,1)S(1)}, u32[]{:S(2)}, u32[]{:S(2)}) async-start(bf16[4,32,1024]{2,1,0:T(8,128)(2,1)} %get-tuple-element.32), calls=%async_computation.2 | async-start | bytes 524288 | tf_op jit(solution)/shard_map/all_to_all | solution.py:184
  40.4 0.7 copy-start.1
  41.1 0.7 copy-start.3
  41.9 0.7 copy-start.5
  42.6 1.0 copy-start.2
  43.6 1.0 copy-start.4
  44.6 1.0 copy-start.6
  48.1 20.8 %collective-permute-start.4 = (bf16[4,2,16,1024]{3,2,1,0:T(8,128)(2,1)}, bf16[4,2,16,1024]{3,2,1,0:T(8,128)(2,1)S(1)}, u32[]{:S(2)}, u32[]{:S(2)}) collective-permute-start(bf16[4,2,16,1024]{3,2,1,0:T(8,128)(2,1)} %get-tuple-element.30), channel_id=1, source_target_pairs={{0,480},{1,33},{32,0},{33,65},{64,32},{65,97},{96,64},{97,129},{12... | collective-permute-start | bytes 786440 | tf_op jit(solution)/shard_map/ppermute | solution.py:48
  50.7 18.2 %collective-permute-start.5 = (bf16[4,2,16,1024]{3,2,1,0:T(8,128)(2,1)}, bf16[4,2,16,1024]{3,2,1,0:T(8,128)(2,1)S(1)}, u32[]{:S(2)}, u32[]{:S(2)}) collective-permute-start(bf16[4,2,16,1024]{3,2,1,0:T(8,128)(2,1)} %get-tuple-element.31), channel_id=1, source_target_pairs={{0,32},{1,481},{32,64},{33,1},{64,96},{65,33},{96,128},{97,65},{12... | collective-permute-start | bytes 786440 | tf_op jit(solution)/shard_map/ppermute | solution.py:48
  56.5 19.1 %collective-permute-start.6 = (bf16[4,32,1024]{2,1,0:T(8,128)(2,1)S(1)}, bf16[4,32,1024]{2,1,0:T(8,128)(2,1)S(1)}, u32[]{:S(2)}, u32[]{:S(2)}) collective-permute-start(bf16[4,32,1024]{2,1,0:T(8,128)(2,1)S(1)} %all-to-all-done.2.w0), channel_id=1, source_target_pairs={{0,480},{1,33},{32,0},{33,65},{64,32},{65,97},{96,64},{97,129},{12... | collective-permute-start | bytes 786440 | tf_op jit(solution)/shard_map/ppermute | solution.py:48
  62.3 13.7 %collective-permute-start.7 = (bf16[4,32,1024]{2,1,0:T(8,128)(2,1)S(1)}, bf16[4,32,1024]{2,1,0:T(8,128)(2,1)S(1)}, u32[]{:S(2)}, u32[]{:S(2)}) collective-permute-start(bf16[4,32,1024]{2,1,0:T(8,128)(2,1)S(1)} %all-to-all-done.2.w0), channel_id=1, source_target_pairs={{0,64},{1,449},{32,96},{33,481},{64,128},{65,1},{96,160},{97,33},{... | collective-permute-start | bytes 786440 | tf_op jit(solution)/shard_map/ppermute | solution.py:48
  65.5 12.0 %collective-permute-start.8 = (bf16[4,32,1024]{2,1,0:T(8,128)(2,1)S(1)}, bf16[4,32,1024]{2,1,0:T(8,128)(2,1)}, u32[]{:S(2)}, u32[]{:S(2)}) collective-permute-start(bf16[4,32,1024]{2,1,0:T(8,128)(2,1)S(1)} %all-to-all-done.2.w0), channel_id=1, source_target_pairs={{0,32},{1,481},{32,64},{33,1},{64,96},{65,33},{96,128},{97,65},{12... | collective-permute-start | bytes 786440 | tf_op jit(solution)/shard_map/ppermute | solution.py:48
  69.8 31.9 %all-to-all-start.1 = ((bf16[8,32,1024]{2,1,0:T(8,128)(2,1)}), bf16[8,32,1024]{2,1,0:T(8,128)(2,1)S(1)}, u32[]{:S(2)}, u32[]{:S(2)}) async-start(bf16[8,32,1024]{2,1,0:T(8,128)(2,1)} %shard_map.121), calls=%async_computation.1 | async-start | bytes 1048576 | tf_op jit(solution)/shard_map/all_to_all | solution.py:196
  79.5 11.0 %collective-permute-start.10 = (bf16[192,1024]{1,0:T(8,128)(2,1)S(1)}, bf16[192,1024]{1,0:T(8,128)(2,1)S(1)}, u32[]{:S(2)}, u32[]{:S(2)}) collective-permute-start(bf16[192,1024]{1,0:T(8,128)(2,1)S(1)} %get-tuple-element.35), channel_id=1, source_target_pairs={{0,16},{8,24},{16,0},{24,8},{1,17},{9,25},{17,1},{25,9},{2,18},{10... | collective-permute-start | bytes 1179656 | tf_op jit(solution)/shard_map/ppermute | solution.py:38
  82.8 16.9 %collective-permute-start.11 = (bf16[192,1024]{1,0:T(8,128)(2,1)S(1)}, bf16[192,1024]{1,0:T(8,128)(2,1)S(1)}, u32[]{:S(2)}, u32[]{:S(2)}) collective-permute-start(bf16[192,1024]{1,0:T(8,128)(2,1)S(1)} %get-tuple-element.36), channel_id=1, source_target_pairs={{0,24},{1,9},{8,0},{9,17},{16,8},{17,25},{24,16},{25,1},{2,26},{3,... | collective-permute-start | bytes 1179656 | tf_op jit(solution)/shard_map/ppermute | solution.py:48
  84.7 15.1 %collective-permute-start.9 = (bf16[192,1024]{1,0:T(8,128)(2,1)S(1)}, bf16[192,1024]{1,0:T(8,128)(2,1)S(1)}, u32[]{:S(2)}, u32[]{:S(2)}) collective-permute-start(bf16[192,1024]{1,0:T(8,128)(2,1)S(1)} %get-tuple-element.34), channel_id=1, source_target_pairs={{0,8},{1,25},{8,16},{9,1},{16,24},{17,9},{24,0},{25,17},{2,10},{3,... | collective-permute-start | bytes 1179656 | tf_op jit(solution)/shard_map/ppermute | solution.py:48
